TPU v7x, 32 devices: a whole 2x2x4 slice. The times are simulated.
32 devices in a mesh: row: 2 (over x), col: 4 (over z), layer: 4 (over y, core).
Axes of the slice: x: 2, y: 2, z: 4, core: 2. Of those that a mesh axis runs over, the one named last changes fastest.
Arguments:
- amplitudes: float32 [1024, 2048], P('row', ('col', 'layer')), may hold values from -6 to 6
- integrals: float32 [2048, 16384], P(('row', 'layer'), 'col'), may hold values from -0.125 to 0.125
Outputs:
- ladder: float32 [1024, 16384], P('row', ('col', 'layer'))
All inputs are finite; a program needn't handle non-finite values.
Results may differ from a plain program's by a relative error of at most 0.000082.
Values sent between devices are 32-bit elements; how exact they have to be, the bound alone decides.
No kernel may reach another device: no remote copies, remote signals or barrier semaphores. Data moves between devices by JAX's collectives and lax.ppermute only.
A program may use at most 64 MiB of HBM per device.

v0:
```python
import jax
import jax.numpy as jnp
from jax import lax
from jax.sharding import PartitionSpec as P


def shards(amplitudes, integrals):
    amp_panel = lax.all_gather(amplitudes, "layer", axis=1, tiled=True)
    amp_whole = lax.all_gather(amp_panel, "col", axis=1, tiled=True)
    int_mine = lax.all_to_all(integrals, "layer", split_axis=1, concat_axis=0, tiled=True)
    product = jnp.dot(
        amp_whole,
        lax.all_gather(int_mine, "row", axis=0, tiled=True),
        precision=lax.Precision.HIGHEST,
        preferred_element_type=jnp.float32,
    )
    return 0.5 * product


def solution(mesh):
    in_specs = (P("row", ("col", "layer")), P(("row", "layer"), "col"))
    out_specs = P("row", ("col", "layer"))
    return jax.shard_map(shards, mesh=mesh, in_specs=in_specs, out_specs=out_specs, check_vma=False)
```

profile of v0, /device:TPU:0, one launch (start us, length us, event | category | flops | bytes accessed | tf_op | source)
XLA Modules:
  0.0 239.3 jit_solution(7371168743059997588)
XLA Ops:
  6.5 0.0 all-gather.4.cloned.1.call-start
  6.5 0.7 all-gather.4.cloned.1.call-update
  7.3 0.0 all-gather.6.cloned.1.call-start
  7.3 21.2 %all-gather.4.cloned.1.call-done = f32[512,512]{1,0:T(8,128)} async-done(((f32[512,128]{1,0:T(8,128)}), f32[512,512]{1,0:T(8,128)}) %all-gather.4.cloned.1.call-update) | async-done | bytes 1048592 | tf_op jit(solution)/shard_map/all_gather | solution.py:8
  28.5 0.0 all-gather.6.cloned.1.call-update
  28.5 0.0 all-gather.8.cloned.1.call-start
  28.6 5.6 %copy.3 = f32[256,4096]{0,1:T(8,128)} copy(f32[256,4096]{1,0:T(8,128)} %param.3) | data formatting | bytes 8388608 | tf_op args[1]
  34.2 53.9 %all_to_all.19 = f32[256,4,1024]{0,2,1:T(8,128)} all-to-all(f32[256,4,1024]{0,2,1:T(8,128)} %bitcast.7), channel_id=1, replica_groups=mesh['row'=2,'col'=4,'layer'=4] {'layer'}, dimensions={1} | all-to-all | bytes 8388608 | tf_op jit(solution)/shard_map/all_to_all | solution.py:10
  88.1 5.4 %copy.4 = f32[4,256,1024]{2,1,0:T(8,128)} copy(f32[4,256,1024]{1,2,0:T(8,128)} %bitcast.6) | data formatting | bytes 8388608 | tf_op jit(solution)/shard_map/all_to_all | solution.py:10
  93.5 0.0 all-gather.8.cloned.1.call-update
  93.5 17.4 %all-gather.6.cloned.1.call-done = f32[512,2048]{1,0:T(8,128)} async-done(((f32[512,512]{1,0:T(8,128)}), f32[512,2048]{1,0:T(8,128)}) %all-gather.6.cloned.1.call-update) | async-done | bytes 4194320 | tf_op jit(solution)/shard_map/all_gather | solution.py:9
  110.9 104.1 %all-gather.8.cloned.1.call-done = f32[2048,1024]{1,0:T(8,128)} async-done(((f32[1024,1024]{1,0:T(8,128)}), f32[2048,1024]{1,0:T(8,128)}) %all-gather.8.cloned.1.call-update) | async-done | bytes 8388624 | tf_op jit(solution)/shard_map/all_gather | solution.py:13
  215.0 17.8 %convolution_multiply_fusion = f32[512,1024]{1,0:T(8,128)} fusion(f32[512,2048]{1,0:T(8,128)} %all-gather.6.cloned.1.call-done, f32[2048,1024]{1,0:T(8,128)} %all-gather.8.cloned.1.call-done), kind=kOutput, calls=%fused_computation | convolution fusion | flops 12885426176 | bytes 14680064 | tf_op jit(solution)/shard_map/dot_general | solution.py:11
Async XLA Ops:
  6.5 22.0 %all-gather.4.cloned.1.call-start = ((), (), s32[]{:S(2)}) async-start(), calls=%async_computation.1 | async-start | bytes 1310720 | tf_op jit(solution)/shard_map/all_gather | solution.py:8
  7.3 103.6 %all-gather.6.cloned.1.call-start = ((), (), s32[]{:S(2)}) async-start(), calls=%async_computation.2 | async-start | bytes 5242880 | tf_op jit(solution)/shard_map/all_gather | solution.py:9
  28.5 186.5 %all-gather.8.cloned.1.call-start = ((), (), s32[]{:S(2)}) async-start(), calls=%async_computation.3 | async-start | bytes 12582912 | tf_op jit(solution)/shard_map/all_gather | solution.py:13
Sparse Core Ops, SparseCore 0:
  8.9 19.5 all-gather.3
  30.1 80.7 all-gather.5
  112.4 102.5 all-gather.7
where the time goes:
time: 240 us; the launch traced here: 239 us
  waiting for transfers between devices  143 us (60%)
  blocking collectives  53.9 us (22%)
  matrix products  17.8 us (7%)
  between operations  13.1 us (5%)
  local copies, waits for them, and re-layouts  11 us (5%)
    all_gather x1, waiting for transfers between devices, shards(): lax.all_gather(int_mine, 'row', axis=0, tiled=True)  104 us
    all_to_all x1, blocking collectives, shards(): lax.all_to_all(integrals, 'layer', split_axis=1, concat_axis=0, tiled=True)  53.9 us
    all_gather x1, waiting for transfers between devices, shards(): amp_panel = lax.all_gather(amplitudes, 'layer', axis=1, tiled=True)  21.2 us
    dot_general x1, matrix products, shards(): jnp.dot(amp_whole, lax.all_gather(int_mine, 'row', axis=0, tiled=True), p...  17.8 us
    all_gather x1, waiting for transfers between devices, shards(): amp_whole = lax.all_gather(amp_panel, 'col', axis=1, tiled=True)  17.4 us
    unnamed x1, local copies, waits for them, and re-layouts  5.64 us
    all_to_all x1, local copies, waits for them, and re-layouts, shards(): lax.all_to_all(integrals, 'layer', split_axis=1, concat_axis=0, tiled=True)  5.38 us
  transfers between devices with their start and end apart: 3, of which 3 were waited for; matrix products, arithmetic and copies ran while one was open for 5% of the time, Pallas kernels for 0%

commit v1 on v0

v1 whole, which is shorter than its diff:
```python
import jax
import jax.numpy as jnp
from jax import lax
from jax.experimental import pallas as pl
from jax.experimental.pallas import tpu as pltpu
from jax.sharding import PartitionSpec as P

AXES = ("row", "col", "layer")
F32, BF16 = jnp.float32, jnp.bfloat16


def gather_plan(amplitudes, integrals):
    amp_panel = lax.all_gather(amplitudes, "layer", axis=1, tiled=True)
    amp_whole = lax.all_gather(amp_panel, "col", axis=1, tiled=True)
    int_mine = lax.all_to_all(integrals, "layer", split_axis=1, concat_axis=0, tiled=True)
    product = jnp.dot(
        amp_whole,
        lax.all_gather(int_mine, "row", axis=0, tiled=True),
        precision=lax.Precision.HIGHEST,
        preferred_element_type=F32,
    )
    return 0.5 * product


def split(value):
    high = value.astype(BF16)
    return high, (value - high.astype(F32)).astype(BF16)


def prep_kernel(place, b0, b1, b2, b3, twin, high, low):
    p, y, core = place[0], place[1], place[2]
    kb = b0.shape[1]
    for rel, mine in enumerate((b0, b1, b2, b3)):
        slot = (p ^ (rel >> 1)) * 2 + (y ^ (rel & 1))
        for value, at in ((mine[...], core), (twin[rel], 1 - core)):
            h, l = split(value)
            high[slot, :, pl.ds(pl.multiple_of(at * kb, kb), kb)] = h
            low[slot, :, pl.ds(pl.multiple_of(at * kb, kb), kb)] = l


def prep(place, blocks, twin):
    rows, kb = blocks[0].shape
    shape = jax.ShapeDtypeStruct((4, rows, 2 * kb), BF16)
    return pl.pallas_call(
        prep_kernel,
        out_shape=(shape, shape),
        in_specs=[pl.BlockSpec(memory_space=pltpu.SMEM)] + [pl.BlockSpec(memory_space=pltpu.VMEM)] * 5,
        out_specs=(pl.BlockSpec(memory_space=pltpu.VMEM),) * 2,
        cost_estimate=pl.CostEstimate(flops=0, bytes_accessed=64 * rows * kb, transcendentals=0),
        name="prep",
    )(place, *blocks, twin)


def mul_kernel(place, high, low, c0, c1, c2, c3, out):
    layer = place[3]
    total = jnp.zeros(out.shape, F32)
    for rel, piece in enumerate((c0, c1, c2, c3)):
        slot = layer ^ rel
        bh, bl = split(piece[...])
        ah, al = high[slot], low[slot]
        total += jnp.dot(ah, bh, preferred_element_type=F32)
        total += jnp.dot(ah, bl, preferred_element_type=F32)
        total += jnp.dot(al, bh, preferred_element_type=F32)
    out[...] = total


def mul(place, amp, pieces):
    high, low = amp
    rows, n = high.shape[1], pieces[0].shape[1]
    k = high.shape[0] * high.shape[2]
    return pl.pallas_call(
        mul_kernel,
        out_shape=jax.ShapeDtypeStruct((rows, n), F32),
        in_specs=[pl.BlockSpec(memory_space=pltpu.SMEM)] + [pl.BlockSpec(memory_space=pltpu.VMEM)] * 6,
        out_specs=pl.BlockSpec(memory_space=pltpu.VMEM),
        cost_estimate=pl.CostEstimate(flops=6 * rows * n * k, bytes_accessed=4 * (rows * k + n * k + rows * n), transcendentals=0),
        name="mul",
    )(place, high, low, *pieces)


def add_kernel(mine, other, *refs):
    refs[-1][...] = 0.5 * (mine[...] + other[...])


def put(whole, mine, other, at, width):
    rows, n = mine.shape
    tile = 128
    spec = pl.BlockSpec((rows, tile), lambda g: (0, g))
    last = [] if whole is None else [whole]
    return pl.pallas_call(
        add_kernel,
        grid=(n // tile,),
        out_shape=jax.ShapeDtypeStruct((rows, width), F32),
        in_specs=[spec, spec] + [pl.BlockSpec(memory_space=pl.ANY)] * len(last),
        out_specs=pl.BlockSpec((rows, tile), lambda g: (0, at // tile + g)),
        input_output_aliases={2: 0} if last else {},
        cost_estimate=pl.CostEstimate(flops=2 * rows * n, bytes_accessed=12 * rows * n, transcendentals=0),
        name="put",
    )(mine, other, *last)


def swap_plan(C, L, cuts):
    half = C // 2
    every = [(r, c, l) for r in range(2) for c in range(C) for l in range(L)]

    def flat(r, c, l):
        return (r * C + c) * L + l

    def send(value, where, who=lambda r, c, l: True):
        return lax.ppermute(value, AXES, [(flat(*d), flat(*where(*d))) for d in every if who(*d)])

    def home(r, c, l):
        return c // half == r

    def shards(amplitudes, integrals):
        r, c, l = (lax.axis_index(a) for a in AXES)
        here = c // half == r
        place = jnp.stack([c % half, l // 2, l % 2, l]).astype(jnp.int32)
        width = integrals.shape[1] // L

        def piece(rel, at, n):
            return lax.dynamic_slice_in_dim(integrals, (l ^ rel) * width + at, n, 1)

        first = send(amplitudes, lambda r, c, l: (r, (c + half) % C, l) if home(r, c, l) else (1 - r, c, l))
        second = send(amplitudes, lambda r, c, l: (1 - r, (c + half) % C, l), lambda r, c, l: not home(r, c, l))
        turned = send(amplitudes, lambda r, c, l: (r, c, l ^ 2), home)
        other = jnp.where(here, first, second)
        blocks = [other] + [
            send(other, lambda r, c, l, p=p, y=y: (r, c ^ p, l ^ (2 * y))) for p, y in ((0, 1), (1, 0), (1, 1))
        ]
        far = prep(place, blocks, send(jnp.stack(blocks), lambda r, c, l: (r, c, l ^ 1)))

        turned = jnp.where(here, turned, send(turned, lambda r, c, l: (r, (c + half) % C, l), home))
        own = jnp.stack([jnp.where(here, amplitudes, first), turned])
        pair = send(own, lambda r, c, l: (r, c ^ 1, l))
        blocks = [own[0], own[1], pair[0], pair[1]]
        near = prep(place, blocks, send(jnp.stack(blocks), lambda r, c, l: (r, c, l ^ 1)))

        whole = None
        at = 0
        for n in cuts:
            pieces = [piece(0, at, n)]
            for rel in (1, 2, 3):
                pieces.append(send(piece(rel, at, n), lambda r, c, l: (r, c, l ^ rel)))
            got = send(mul(place, far, pieces), lambda r, c, l: (1 - r, c, l))
            whole = put(whole, mul(place, near, pieces), got, at, width)
            at += n
        return whole

    return shards


def solution(mesh):
    in_specs = (P("row", ("col", "layer")), P(("row", "layer"), "col"))
    out_specs = P("row", ("col", "layer"))
    R, C, L = (mesh.shape[a] for a in AXES)
    plan = swap_plan(C, L, (256,) * 4) if (R, C, L) == (2, 4, 4) else gather_plan
    return jax.shard_map(plan, mesh=mesh, in_specs=in_specs, out_specs=out_specs, check_vma=False)
```

time: 240 us -> 144 us (0.60)
  waiting for transfers between devices: 143 us -> 48.3 us
  blocking collectives: 53.9 us -> 0 us
  Pallas kernels: 0 us -> 43.2 us
  starting transfers between devices: 0.08 us -> 39.2 us
  matrix products: 17.8 us -> 0 us
  between operations: 13.1 us -> 0.2 us
  other arithmetic: 0 us -> 3.92 us
  local copies, waits for them, and re-layouts: 11 us -> 8.33 us
    all_gather x3 -> x0, waiting for transfers between devices: 143 us -> none  [the longest x1 104 us: shards(): lax.all_gather(int_mine, 'row', axis=0, tiled=True)]
    all_to_all x1 -> x0, blocking collectives: 53.9 us -> none  [shards(): lax.all_to_all(integrals, 'layer', split_axis=1, concat_axis=0, tiled=True)]
    ppermute x0 -> x26, waiting for transfers between devices: none -> 48.3 us  [send(): lax.ppermute(value, AXES, [(flat(*d), flat(*where(*d))) for d in every if...]
    pallas_call x0 -> x14, Pallas kernels: none -> 43.2 us  [the longest x8 28.9 us: mul(): pl.pallas_call(mul_kernel, out_shape=jax.ShapeDtypeStruct((rows, n), F32)...]
    ppermute x0 -> x26, starting transfers between devices: none -> 39.2 us  [send(): lax.ppermute(value, AXES, [(flat(*d), flat(*where(*d))) for d in every if...]
    dot_general x1 -> x0, matrix products: 17.8 us -> none  [shards(): jnp.dot(amp_whole, lax.all_gather(int_mine, 'row', axis=0, tiled=True), p...]
    all_to_all x1 -> x0, local copies, waits for them, and re-layouts: 5.38 us -> none  [shards(): lax.all_to_all(integrals, 'layer', split_axis=1, concat_axis=0, tiled=True)]
    dynamic_slice x0 -> x1, local copies, waits for them, and re-layouts: none -> 3.76 us  [piece(): return lax.dynamic_slice_in_dim(integrals, (l ^ rel) * width + at, n, 1)]
  transfers between devices with their start and end apart: 3 -> 26, of which waited for: 3 -> 11; matrix products, arithmetic and copies ran while one was open for 5% -> 6% of each run, Pallas kernels for 0% -> 29%
where the time goes in v1:
time: 144 us; the launch traced here: 143 us
  waiting for transfers between devices  48.3 us (34%)
  Pallas kernels  43.2 us (30%)
  starting transfers between devices  39.2 us (27%)
  local copies, waits for them, and re-layouts  8.33 us (6%)
  other arithmetic  3.92 us (3%)
    ppermute x26, waiting for transfers between devices, send(): lax.ppermute(value, AXES, [(flat(*d), flat(*where(*d))) for d in every if...  48.3 us
    ppermute x26, starting transfers between devices, send(): lax.ppermute(value, AXES, [(flat(*d), flat(*where(*d))) for d in every if...  39.2 us
    pallas_call x8, Pallas kernels, mul(): pl.pallas_call(mul_kernel, out_shape=jax.ShapeDtypeStruct((rows, n), F32)...  28.9 us
    pallas_call x4, Pallas kernels, put(): pl.pallas_call(add_kernel, grid=(n // tile,), out_shape=jax.ShapeDtypeStr...  7.69 us
    pallas_call x2, Pallas kernels, prep(): pl.pallas_call(prep_kernel, out_shape=(shape, shape), in_specs=[pl.BlockS...  6.61 us
    dynamic_slice x1, local copies, waits for them, and re-layouts, piece(): return lax.dynamic_slice_in_dim(integrals, (l ^ rel) * width + at, n, 1)  3.76 us
    unnamed x32, local copies, waits for them, and re-layouts  3.74 us
  transfers between devices with their start and end apart: 26, of which 11 were waited for; matrix products, arithmetic and copies ran while one was open for 6% of the time, Pallas kernels for 29%

profile of v1, /device:TPU:0, one launch (start us, length us, event | category | flops | bytes accessed | tf_op | source)
XLA Modules:
  0.0 143.2 jit_solution(10687268119262582900)
XLA Ops:
  0.0 4.9 %collective-permute-start.1 = (f32[512,128]{1,0:T(8,128)}, f32[512,128]{1,0:T(8,128)S(1)}, u32[]{:S(2)}, u32[]{:S(2)}) collective-permute-start(f32[512,128]{1,0:T(8,128)} %param.2), channel_id=1, source_target_pairs={{0,2},{1,3},{2,0},{3,1},{4,6},{5,7},{6,4},{7,5},{24,26},{25,27},{2... | collective-permute-start | bytes 786440 | tf_op jit(solution)/shard_map/ppermute | solution.py:110
  5.6 5.7 %collective-permute-done.1 = f32[512,128]{1,0:T(8,128)S(1)} collective-permute-done((f32[512,128]{1,0:T(8,128)}, f32[512,128]{1,0:T(8,128)S(1)}, u32[]{:S(2)}, u32[]{:S(2)}) %collective-permute-start.1) | collective-permute-done | bytes 262176 | tf_op jit(solution)/shard_map/ppermute | solution.py:110
  11.4 1.8 %collective-permute-start.2 = (f32[512,128]{1,0:T(8,128)S(1)}, f32[512,128]{1,0:T(8,128)S(1)}, u32[]{:S(2)}, u32[]{:S(2)}) collective-permute-start(f32[512,128]{1,0:T(8,128)S(1)} %collective-permute-done.1), channel_id=1, source_target_pairs={{0,8},{1,9},{2,10},{3,11},{4,12},{5,13},{6,14},{7,15},{24,16},{25,... | collective-permute-start | bytes 786440 | tf_op jit(solution)/shard_map/ppermute | solution.py:110
  13.2 1.0 broadcast_select_fusion
  14.2 11.3 %collective-permute-start.11 = (f32[512,128]{1,0:T(8,128)S(1)}, f32[512,128]{1,0:T(8,128)S(1)}, u32[]{:S(2)}, u32[]{:S(2)}) collective-permute-start(f32[512,128]{1,0:T(8,128)S(1)} %get-tuple-element.31.b0), channel_id=1, source_target_pairs={{0,6},{1,7},{2,4},{3,5},{4,2},{5,3},{6,0},{7,1},{8,14},{9,15},{10,... | collective-permute-start | bytes 786440 | tf_op jit(solution)/shard_map/ppermute | solution.py:110
  26.2 3.0 %collective-permute-start.3 = (f32[2,512,128]{2,1,0:T(8,128)S(1)}, f32[2,512,128]{2,1,0:T(8,128)S(1)}, u32[]{:S(2)}, u32[]{:S(2)}) collective-permute-start(f32[2,512,128]{2,1,0:T(8,128)S(1)} %pad_maximum_fusion.2), channel_id=1, source_target_pairs={{0,4},{1,5},{2,6},{3,7},{4,0},{5,1},{6,2},{7,3},{8,12},{9,13},{10,... | collective-permute-start | bytes 1572872 | tf_op jit(solution)/shard_map/ppermute | solution.py:110
  29.2 3.4 %collective-permute-done.11.b3 = f32[512,128]{1,0:T(8,128)S(1)} collective-permute-done((f32[512,128]{1,0:T(8,128)S(1)}, f32[512,128]{1,0:T(8,128)S(1)}, u32[]{:S(2)}, u32[]{:S(2)}) %collective-permute-start.11) | collective-permute-done | bytes 262176 | tf_op jit(solution)/shard_map/ppermute | solution.py:110
  32.6 5.2 %collective-permute-done.10.b2 = f32[512,128]{1,0:T(8,128)S(1)} collective-permute-done((f32[512,128]{1,0:T(8,128)S(1)}, f32[512,128]{1,0:T(8,128)S(1)}, u32[]{:S(2)}, u32[]{:S(2)}) %collective-permute-start.10) | collective-permute-done | bytes 262176 | tf_op jit(solution)/shard_map/ppermute | solution.py:110
  37.9 1.1 pad_maximum_fusion.1
  39.1 3.8 %constant_dynamic-slice_fusion = (f32[256,256]{1,0:T(8,128)S(1)}, f32[256,256]{1,0:T(8,128)S(1)}, f32[256,256]{1,0:T(8,128)}, f32[256,256]{1,0:T(8,128)S(1)}, f3...) fusion(f32[256,4096]{1,0:T(8,128)} %param.3, ...), kind=kLoop, calls=%fused_computation.8 | loop fusion | bytes 8388672 | tf_op jit(solution)/shard_map/dynamic_slice | solution.py:122
  42.8 1.1 collective-permute-start.24
  44.0 1.1 collective-permute-start.20
  45.1 5.9 %collective-permute-done.24.c3 = f32[256,256]{1,0:T(8,128)S(1)} collective-permute-done((f32[256,256]{1,0:T(8,128)S(1)}, f32[256,256]{1,0:T(8,128)S(1)}, u32[]{:S(2)}, u32[]{:S(2)}) %collective-permute-start.24) | collective-permute-done | bytes 262176 | tf_op jit(solution)/shard_map/ppermute | solution.py:110
  51.0 1.0 collective-permute-start.19
  52.0 0.9 collective-permute-start.18
  52.9 1.0 pad_maximum_fusion
  54.0 2.6 %collective-permute-done.20.c3 = f32[256,256]{1,0:T(8,128)S(1)} collective-permute-done((f32[256,256]{1,0:T(8,128)S(1)}, f32[256,256]{1,0:T(8,128)S(1)}, u32[]{:S(2)}, u32[]{:S(2)}) %collective-permute-start.20) | collective-permute-done | bytes 262176 | tf_op jit(solution)/shard_map/ppermute | solution.py:110
  56.6 1.5 %collective-permute-start.16 = (f32[256,256]{1,0:T(8,128)S(1)}, f32[256,256]{1,0:T(8,128)S(1)}, u32[]{:S(2)}, u32[]{:S(2)}) collective-permute-start(f32[256,256]{1,0:T(8,128)S(1)} %get-tuple-element.20), channel_id=1, source_target_pairs={{0,3},{1,2},{2,1},{3,0},{4,7},{5,6},{6,5},{7,4},{8,11},{9,10},{10,... | collective-permute-start | bytes 786440 | tf_op jit(solution)/shard_map/ppermute | solution.py:110
  58.1 5.3 %collective-permute-done.19.c2 = f32[256,256]{1,0:T(8,128)} collective-permute-done((f32[256,256]{1,0:T(8,128)S(1)}, f32[256,256]{1,0:T(8,128)}, u32[]{:S(2)}, u32[]{:S(2)}) %collective-permute-start.19) | collective-permute-done | bytes 262176 | tf_op jit(solution)/shard_map/ppermute | solution.py:110
  63.4 1.0 collective-permute-start.15
  64.4 1.0 collective-permute-start.23
  65.4 2.4 %collective-permute-done.16.c3 = f32[256,256]{1,0:T(8,128)S(1)} collective-permute-done((f32[256,256]{1,0:T(8,128)S(1)}, f32[256,256]{1,0:T(8,128)S(1)}, u32[]{:S(2)}, u32[]{:S(2)}) %collective-permute-start.16) | collective-permute-done | bytes 262176 | tf_op jit(solution)/shard_map/ppermute | solution.py:110
  67.8 0.9 collective-permute-start.14
  68.7 5.8 %collective-permute-done.15.c2 = f32[256,256]{1,0:T(8,128)S(1)} collective-permute-done((f32[256,256]{1,0:T(8,128)}, f32[256,256]{1,0:T(8,128)S(1)}, u32[]{:S(2)}, u32[]{:S(2)}) %collective-permute-start.15) | collective-permute-done | bytes 262176 | tf_op jit(solution)/shard_map/ppermute | solution.py:110
  74.5 5.7 %collective-permute-done.23.c2 = f32[256,256]{1,0:T(8,128)} collective-permute-done((f32[256,256]{1,0:T(8,128)}, f32[256,256]{1,0:T(8,128)}, u32[]{:S(2)}, u32[]{:S(2)}) %collective-permute-start.23) | collective-permute-done | bytes 262176 | tf_op jit(solution)/shard_map/ppermute | solution.py:110
  80.3 1.0 collective-permute-start.6
  82.2 3.3 %prep.3 = (bf16[4,512,256]{2,1,0:T(8,128)(2,1)}, bf16[4,512,256]{2,1,0:T(8,128)(2,1)}) custom-call(s32[4]{0:T(128)} %pad_add_fusion.place, f32[512,128]{1,0:T(8,128)} %copy-done.2, f32[512,128]{1,0:T(8,128)} %copy-done.7, f32[512,128]{1,0:T(8,128)} %copy-done.6, f32[512,128]{1,0:T(8,128)} %copy-done.5, f32[4,512,128]{2,1,0:T(8,128)} %copy-done.3), custom_call_target="tpu_custom_call" | custom-call | bytes 4194304 | tf_op jit(solution)/shard_map/prep/pallas_call | solution.py:44
  85.5 3.6 %mul.43 = f32[512,256]{1,0:T(8,128)} custom-call(s32[4]{0:T(128)} %pad_add_fusion.place, bf16[4,512,256]{2,1,0:T(8,128)(2,1)} %get-tuple-element.11.high, bf16[4,512,256]{2,1,0:T(8,128)(2,1)} %get-tuple-element.12.low, f32[256,256]{1,0:T(8,128)} %get-tuple-element.15.c0, f32[256,256]{1,0:T(8,128)} %copy-done.10, f32[256,256]{1,0:T(8,128)} %collective-permute-done.23.c2, ...), custom_call_target="tpu_custom_call" | custom-call | flops 805306368 | bytes 3670016 | tf_op jit(solution)/shard_map/mul/pallas_call | solution.py:71
  89.1 5.2 %collective-permute-start.25 = (f32[512,256]{1,0:T(8,128)}, f32[512,256]{1,0:T(8,128)}, u32[]{:S(2)}, u32[]{:S(2)}) collective-permute-start(f32[512,256]{1,0:T(8,128)} %mul.43), channel_id=1, source_target_pairs={{0,16},{1,17},{2,18},{3,19},{4,20},{5,21},{6,22},{7,23},{8,24},{9,... | collective-permute-start | bytes 1572872 | tf_op jit(solution)/shard_map/ppermute | solution.py:110
  94.4 3.6 %mul.41 = f32[512,256]{1,0:T(8,128)} custom-call(s32[4]{0:T(128)} %pad_add_fusion.place, bf16[4,512,256]{2,1,0:T(8,128)(2,1)} %get-tuple-element.11.high, bf16[4,512,256]{2,1,0:T(8,128)(2,1)} %get-tuple-element.12.low, f32[256,256]{1,0:T(8,128)} %get-tuple-element.19.c0, f32[256,256]{1,0:T(8,128)} %collective-permute-done.18.c1, ...), custom_call_target="tpu_custom_call" | custom-call | flops 805306368 | bytes 3670016 | tf_op jit(solution)/shard_map/mul/pallas_call | solution.py:71
  98.0 3.6 %mul.39 = f32[512,256]{1,0:T(8,128)} custom-call(s32[4]{0:T(128)} %pad_add_fusion.place, bf16[4,512,256]{2,1,0:T(8,128)(2,1)} %get-tuple-element.11.high, bf16[4,512,256]{2,1,0:T(8,128)(2,1)} %get-tuple-element.12.low, f32[256,256]{1,0:T(8,128)} %get-tuple-element.23.c0, f32[256,256]{1,0:T(8,128)} %collective-permute-done.14.c1, f32[256,256]{1,0:T(8,128)} %copy-done.12, ...), custom_call_target="tpu_custom_call" | custom-call | flops 805306368 | bytes 3670016 | tf_op jit(solution)/shard_map/mul/pallas_call | solution.py:71
  101.6 2.0 %collective-permute-start.17 = (f32[512,256]{1,0:T(8,128)}, f32[512,256]{1,0:T(8,128)S(1)}, u32[]{:S(2)}, u32[]{:S(2)}) collective-permute-start(f32[512,256]{1,0:T(8,128)} %mul.39), channel_id=1, source_target_pairs={{0,16},{1,17},{2,18},{3,19},{4,20},{5,21},{6,22},{7,23},{8,24},{9,... | collective-permute-start | bytes 1572872 | tf_op jit(solution)/shard_map/ppermute | solution.py:110
  103.6 3.6 %mul.37 = f32[512,256]{1,0:T(8,128)} custom-call(s32[4]{0:T(128)} %pad_add_fusion.place, bf16[4,512,256]{2,1,0:T(8,128)(2,1)} %get-tuple-element.11.high, bf16[4,512,256]{2,1,0:T(8,128)(2,1)} %get-tuple-element.12.low, f32[256,256]{1,0:T(8,128)} %get-tuple-element.27.c0, f32[256,256]{1,0:T(8,128)} %collective-permute-done.5.c1, ...), custom_call_target="tpu_custom_call" | custom-call | flops 805306368 | bytes 3670016 | tf_op jit(solution)/shard_map/mul/pallas_call | solution.py:71
  107.3 0.8 slice_bitcast_fusion
  108.1 1.0 copy-done.4
  109.1 3.3 %prep.2 = (bf16[4,512,256]{2,1,0:T(8,128)(2,1)}, bf16[4,512,256]{2,1,0:T(8,128)(2,1)}) custom-call(s32[4]{0:T(128)} %pad_add_fusion.place, f32[512,128]{1,0:T(8,128)} %copy-done, f32[512,128]{1,0:T(8,128)} %copy-done.1, f32[512,128]{1,0:T(8,128)} %get-tuple-element.30.b2, f32[512,128]{1,0:T(8,128)} %get-tuple-element.29.b3, f32[4,512,128]{2,1,0:T(8,128)} %copy-done.4), custom_call_target="tpu_custom_call" | custom-call | bytes 4194304 | tf_op jit(solution)/shard_map/prep/pallas_call | solution.py:44
  112.4 3.6 %mul.42.mine = f32[512,256]{1,0:T(8,128)} custom-call(s32[4]{0:T(128)} %pad_add_fusion.place, bf16[4,512,256]{2,1,0:T(8,128)(2,1)} %get-tuple-element.9.high, bf16[4,512,256]{2,1,0:T(8,128)(2,1)} %get-tuple-element.10.low, f32[256,256]{1,0:T(8,128)} %get-tuple-element.15.c0, f32[256,256]{1,0:T(8,128)} %copy-done.10, f32[256,256]{1,0:T(8,128)} %collective-permute-done.23.c2, ...), custom_call_target="tpu_custom_call" | custom-call | flops 805306368 | bytes 3670016 | tf_op jit(solution)/shard_map/mul/pallas_call | solution.py:71
  116.0 1.9 %put.4.refs_0_ = f32[512,1024]{1,0:T(8,128)} custom-call(f32[512,256]{1,0:T(8,128)} %mul.42.mine, f32[512,256]{1,0:T(8,128)} %collective-permute-done.25.other), custom_call_target="tpu_custom_call" | custom-call | flops 262144 | bytes 1572864 | tf_op jit(solution)/shard_map/put/pallas_call | solution.py:90
  118.0 3.6 %mul.40.mine = f32[512,256]{1,0:T(8,128)} custom-call(s32[4]{0:T(128)} %pad_add_fusion.place, bf16[4,512,256]{2,1,0:T(8,128)(2,1)} %get-tuple-element.9.high, bf16[4,512,256]{2,1,0:T(8,128)(2,1)} %get-tuple-element.10.low, f32[256,256]{1,0:T(8,128)} %get-tuple-element.19.c0, f32[256,256]{1,0:T(8,128)} %collective-permute-done.18.c1, ...), custom_call_target="tpu_custom_call" | custom-call | flops 805306368 | bytes 3670016 | tf_op jit(solution)/shard_map/mul/pallas_call | solution.py:71
  122.4 1.9 %put.5.refs_0_ = f32[512,1024]{1,0:T(8,128)} custom-call(f32[512,256]{1,0:T(8,128)} %mul.40.mine, f32[512,256]{1,0:T(8,128)} %copy-done.15, f32[512,1024]{1,0:T(8,128)} %put.4.refs_0_), custom_call_target="tpu_custom_call", output_to_operand_aliasing={{}: (2, {})} | custom-call | flops 262144 | bytes 1572864 | tf_op jit(solution)/shard_map/put/pallas_call | solution.py:90
  124.3 3.6 %mul.38.mine = f32[512,256]{1,0:T(8,128)} custom-call(s32[4]{0:T(128)} %pad_add_fusion.place, bf16[4,512,256]{2,1,0:T(8,128)(2,1)} %get-tuple-element.9.high, bf16[4,512,256]{2,1,0:T(8,128)(2,1)} %get-tuple-element.10.low, f32[256,256]{1,0:T(8,128)} %get-tuple-element.23.c0, f32[256,256]{1,0:T(8,128)} %collective-permute-done.14.c1, f32[256,256]{1,0:T(8,128)} %copy-done.12, ...), custom_call_target="tpu_custom_call" | custom-call | flops 805306368 | bytes 3670016 | tf_op jit(solution)/shard_map/mul/pallas_call | solution.py:71
  127.9 1.9 %collective-permute-done.17.other = f32[512,256]{1,0:T(8,128)S(1)} collective-permute-done((f32[512,256]{1,0:T(8,128)}, f32[512,256]{1,0:T(8,128)S(1)}, u32[]{:S(2)}, u32[]{:S(2)}) %collective-permute-start.17) | collective-permute-done | bytes 524320 | tf_op jit(solution)/shard_map/ppermute | solution.py:110
  129.8 0.8 copy-done.14
  130.6 1.9 %put.6.refs_0_ = f32[512,1024]{1,0:T(8,128)} custom-call(f32[512,256]{1,0:T(8,128)} %mul.38.mine, f32[512,256]{1,0:T(8,128)} %copy-done.14, f32[512,1024]{1,0:T(8,128)} %put.5.refs_0_), custom_call_target="tpu_custom_call", output_to_operand_aliasing={{}: (2, {})} | custom-call | flops 262144 | bytes 1572864 | tf_op jit(solution)/shard_map/put/pallas_call | solution.py:90
  132.5 3.6 %mul.36.mine = f32[512,256]{1,0:T(8,128)} custom-call(s32[4]{0:T(128)} %pad_add_fusion.place, bf16[4,512,256]{2,1,0:T(8,128)(2,1)} %get-tuple-element.9.high, bf16[4,512,256]{2,1,0:T(8,128)(2,1)} %get-tuple-element.10.low, f32[256,256]{1,0:T(8,128)} %get-tuple-element.27.c0, f32[256,256]{1,0:T(8,128)} %collective-permute-done.5.c1, ...), custom_call_target="tpu_custom_call" | custom-call | flops 805306368 | bytes 3670016 | tf_op jit(solution)/shard_map/mul/pallas_call | solution.py:71
  136.1 4.4 %collective-permute-done.13.other = f32[512,256]{1,0:T(8,128)S(1)} collective-permute-done((f32[512,256]{1,0:T(8,128)}, f32[512,256]{1,0:T(8,128)S(1)}, u32[]{:S(2)}, u32[]{:S(2)}) %collective-permute-start.13) | collective-permute-done | bytes 524320 | tf_op jit(solution)/shard_map/ppermute | solution.py:110
  140.5 0.8 copy-done.13
  141.3 1.9 %put.7 = f32[512,1024]{1,0:T(8,128)} custom-call(f32[512,256]{1,0:T(8,128)} %mul.36.mine, f32[512,256]{1,0:T(8,128)} %copy-done.13, f32[512,1024]{1,0:T(8,128)} %put.6.refs_0_), custom_call_target="tpu_custom_call", output_to_operand_aliasing={{}: (2, {})} | custom-call | flops 262144 | bytes 1572864 | tf_op jit(solution)/shard_map/put/pallas_call | solution.py:90
  (58 shorter events, 3.5 us)
Async XLA Ops:
  0.0 11.4 %collective-permute-start.1 = (f32[512,128]{1,0:T(8,128)}, f32[512,128]{1,0:T(8,128)S(1)}, u32[]{:S(2)}, u32[]{:S(2)}) collective-permute-start(f32[512,128]{1,0:T(8,128)} %param.2), channel_id=1, source_target_pairs={{0,2},{1,3},{2,0},{3,1},{4,6},{5,7},{6,4},{7,5},{24,26},{25,27},{2... | collective-permute-start | bytes 786440 | tf_op jit(solution)/shard_map/ppermute | solution.py:110
  4.9 8.3 %collective-permute-start = (f32[512,128]{1,0:T(8,128)}, f32[512,128]{1,0:T(8,128)S(1)}, u32[]{:S(2)}, u32[]{:S(2)}) collective-permute-start(f32[512,128]{1,0:T(8,128)} %param.2), channel_id=1, source_target_pairs={{0,8},{1,9},{2,10},{3,11},{4,12},{5,13},{6,14},{7,15},{8,24},{9,25... | collective-permute-start | bytes 786440 | tf_op jit(solution)/shard_map/ppermute | solution.py:110
  4.9 8.2 %collective-permute-start.8 = (f32[512,128]{1,0:T(8,128)}, f32[512,128]{1,0:T(8,128)S(1)}, u32[]{:S(2)}, u32[]{:S(2)}) collective-permute-start(f32[512,128]{1,0:T(8,128)} %param.2), channel_id=1, source_target_pairs={{8,16},{9,17},{10,18},{11,19},{12,20},{13,21},{14,22},{15,23},{16,... | collective-permute-start | bytes 786440 | tf_op jit(solution)/shard_map/ppermute | solution.py:110
  11.4 14.8 %collective-permute-start.2 = (f32[512,128]{1,0:T(8,128)S(1)}, f32[512,128]{1,0:T(8,128)S(1)}, u32[]{:S(2)}, u32[]{:S(2)}) collective-permute-start(f32[512,128]{1,0:T(8,128)S(1)} %collective-permute-done.1), channel_id=1, source_target_pairs={{0,8},{1,9},{2,10},{3,11},{4,12},{5,13},{6,14},{7,15},{24,16},{25,... | collective-permute-start | bytes 786440 | tf_op jit(solution)/shard_map/ppermute | solution.py:110
  14.2 28.6 %copy-start.2 = (f32[512,128]{1,0:T(8,128)}, f32[512,128]{1,0:T(8,128)S(1)}, u32[]{:S(2)}) copy-start(f32[512,128]{1,0:T(8,128)S(1)} %get-tuple-element.31.b0) | copy-start | bytes 786436
  14.2 38.7 %copy-start = (f32[512,128]{1,0:T(8,128)}, f32[512,128]{1,0:T(8,128)S(1)}, u32[]{:S(2)}) copy-start(f32[512,128]{1,0:T(8,128)S(1)} %get-tuple-element.32.b0) | copy-start | bytes 786436
  14.2 18.4 %collective-permute-start.11 = (f32[512,128]{1,0:T(8,128)S(1)}, f32[512,128]{1,0:T(8,128)S(1)}, u32[]{:S(2)}, u32[]{:S(2)}) collective-permute-start(f32[512,128]{1,0:T(8,128)S(1)} %get-tuple-element.31.b0), channel_id=1, source_target_pairs={{0,6},{1,7},{2,4},{3,5},{4,2},{5,3},{6,0},{7,1},{8,14},{9,15},{10,... | collective-permute-start | bytes 786440 | tf_op jit(solution)/shard_map/ppermute | solution.py:110
  25.5 12.4 %collective-permute-start.10 = (f32[512,128]{1,0:T(8,128)S(1)}, f32[512,128]{1,0:T(8,128)S(1)}, u32[]{:S(2)}, u32[]{:S(2)}) collective-permute-start(f32[512,128]{1,0:T(8,128)S(1)} %get-tuple-element.31.b0), channel_id=1, source_target_pairs={{0,4},{1,5},{2,6},{3,7},{4,0},{5,1},{6,2},{7,3},{8,12},{9,13},{10,... | collective-permute-start | bytes 786440 | tf_op jit(solution)/shard_map/ppermute | solution.py:110
  25.5 12.4 %collective-permute-start.9 = (f32[512,128]{1,0:T(8,128)S(1)}, f32[512,128]{1,0:T(8,128)S(1)}, u32[]{:S(2)}, u32[]{:S(2)}) collective-permute-start(f32[512,128]{1,0:T(8,128)S(1)} %get-tuple-element.31.b0), channel_id=1, source_target_pairs={{0,2},{1,3},{2,0},{3,1},{4,6},{5,7},{6,4},{7,5},{8,10},{9,11},{10,... | collective-permute-start | bytes 786440 | tf_op jit(solution)/shard_map/ppermute | solution.py:110
  26.2 26.7 %copy-start.1 = (f32[512,128]{1,0:T(8,128)}, f32[512,128]{1,0:T(8,128)S(1)}, u32[]{:S(2)}) copy-start(f32[512,128]{1,0:T(8,128)S(1)} %broadcast_select_fusion.1.b1) | copy-start | bytes 786436
  26.2 25.7 %collective-permute-start.3 = (f32[2,512,128]{2,1,0:T(8,128)S(1)}, f32[2,512,128]{2,1,0:T(8,128)S(1)}, u32[]{:S(2)}, u32[]{:S(2)}) collective-permute-start(f32[2,512,128]{2,1,0:T(8,128)S(1)} %pad_maximum_fusion.2), channel_id=1, source_target_pairs={{0,4},{1,5},{2,6},{3,7},{4,0},{5,1},{6,2},{7,3},{8,12},{9,13},{10,... | collective-permute-start | bytes 1572872 | tf_op jit(solution)/shard_map/ppermute | solution.py:110
  32.6 5.2 %copy-start.5 = (f32[512,128]{1,0:T(8,128)}, f32[512,128]{1,0:T(8,128)S(1)}, u32[]{:S(2)}) copy-start(f32[512,128]{1,0:T(8,128)S(1)} %collective-permute-done.11.b3) | copy-start | bytes 786436
  37.8 1.2 copy-start.6
  37.8 1.2 copy-start.7
  39.0 42.2 %collective-permute-start.12 = (f32[4,512,128]{2,1,0:T(8,128)}, f32[4,512,128]{2,1,0:T(8,128)S(1)}, u32[]{:S(2)}, u32[]{:S(2)}) collective-permute-start(f32[4,512,128]{2,1,0:T(8,128)} %pad_maximum_fusion.1), channel_id=1, source_target_pairs={{0,1},{1,0},{2,3},{3,2},{4,5},{5,4},{6,7},{7,6},{8,9},{9,8},{10,11... | collective-permute-start | bytes 3145736 | tf_op jit(solution)/shard_map/ppermute | solution.py:110
  42.8 8.1 %collective-permute-start.24 = (f32[256,256]{1,0:T(8,128)S(1)}, f32[256,256]{1,0:T(8,128)S(1)}, u32[]{:S(2)}, u32[]{:S(2)}) collective-permute-start(f32[256,256]{1,0:T(8,128)S(1)} %get-tuple-element.13), channel_id=1, source_target_pairs={{0,3},{1,2},{2,1},{3,0},{4,7},{5,6},{6,5},{7,4},{8,11},{9,10},{10,... | collective-permute-start | bytes 786440 | tf_op jit(solution)/shard_map/ppermute | solution.py:110
  43.9 10.0 %collective-permute-start.22 = (f32[256,256]{1,0:T(8,128)S(1)}, f32[256,256]{1,0:T(8,128)S(1)}, u32[]{:S(2)}, u32[]{:S(2)}) collective-permute-start(f32[256,256]{1,0:T(8,128)S(1)} %get-tuple-element.14), channel_id=1, source_target_pairs={{0,1},{1,0},{2,3},{3,2},{4,5},{5,4},{6,7},{7,6},{8,9},{9,8},{10,11... | collective-permute-start | bytes 786440 | tf_op jit(solution)/shard_map/ppermute | solution.py:110
  44.0 12.6 %collective-permute-start.20 = (f32[256,256]{1,0:T(8,128)S(1)}, f32[256,256]{1,0:T(8,128)S(1)}, u32[]{:S(2)}, u32[]{:S(2)}) collective-permute-start(f32[256,256]{1,0:T(8,128)S(1)} %get-tuple-element.16), channel_id=1, source_target_pairs={{0,3},{1,2},{2,1},{3,0},{4,7},{5,6},{6,5},{7,4},{8,11},{9,10},{10,... | collective-permute-start | bytes 786440 | tf_op jit(solution)/shard_map/ppermute | solution.py:110
  51.0 1.0 copy-start.9
  51.0 12.4 %collective-permute-start.19 = (f32[256,256]{1,0:T(8,128)S(1)}, f32[256,256]{1,0:T(8,128)}, u32[]{:S(2)}, u32[]{:S(2)}) collective-permute-start(f32[256,256]{1,0:T(8,128)S(1)} %get-tuple-element.17), channel_id=1, source_target_pairs={{0,2},{1,3},{2,0},{3,1},{4,6},{5,7},{6,4},{7,5},{8,10},{9,11},{10,... | collective-permute-start | bytes 786440 | tf_op jit(solution)/shard_map/ppermute | solution.py:110
  52.0 12.4 %collective-permute-start.18 = (f32[256,256]{1,0:T(8,128)S(1)}, f32[256,256]{1,0:T(8,128)}, u32[]{:S(2)}, u32[]{:S(2)}) collective-permute-start(f32[256,256]{1,0:T(8,128)S(1)} %get-tuple-element.18), channel_id=1, source_target_pairs={{0,1},{1,0},{2,3},{3,2},{4,5},{5,4},{6,7},{7,6},{8,9},{9,8},{10,11... | collective-permute-start | bytes 786440 | tf_op jit(solution)/shard_map/ppermute | solution.py:110
  53.9 2.6 %copy-start.10 = (f32[256,256]{1,0:T(8,128)}, f32[256,256]{1,0:T(8,128)S(1)}, u32[]{:S(2)}) copy-start(f32[256,256]{1,0:T(8,128)S(1)} %collective-permute-done.22.c1) | copy-start | bytes 786436
  53.9 54.2 %collective-permute-start.4 = (f32[4,512,128]{2,1,0:T(8,128)}, f32[4,512,128]{2,1,0:T(8,128)S(1)}, u32[]{:S(2)}, u32[]{:S(2)}) collective-permute-start(f32[4,512,128]{2,1,0:T(8,128)} %pad_maximum_fusion), channel_id=1, source_target_pairs={{0,1},{1,0},{2,3},{3,2},{4,5},{5,4},{6,7},{7,6},{8,9},{9,8},{10,11... | collective-permute-start | bytes 3145736 | tf_op jit(solution)/shard_map/ppermute | solution.py:110
  56.6 37.8 %copy-start.8 = (f32[256,256]{1,0:T(8,128)}, f32[256,256]{1,0:T(8,128)S(1)}, u32[]{:S(2)}) copy-start(f32[256,256]{1,0:T(8,128)S(1)} %collective-permute-done.20.c3) | copy-start | bytes 786436
  56.6 11.2 %collective-permute-start.16 = (f32[256,256]{1,0:T(8,128)S(1)}, f32[256,256]{1,0:T(8,128)S(1)}, u32[]{:S(2)}, u32[]{:S(2)}) collective-permute-start(f32[256,256]{1,0:T(8,128)S(1)} %get-tuple-element.20), channel_id=1, source_target_pairs={{0,3},{1,2},{2,1},{3,0},{4,7},{5,6},{6,5},{7,4},{8,11},{9,10},{10,... | collective-permute-start | bytes 786440 | tf_op jit(solution)/shard_map/ppermute | solution.py:110
  63.4 11.1 %collective-permute-start.15 = (f32[256,256]{1,0:T(8,128)}, f32[256,256]{1,0:T(8,128)S(1)}, u32[]{:S(2)}, u32[]{:S(2)}) collective-permute-start(f32[256,256]{1,0:T(8,128)} %get-tuple-element.21), channel_id=1, source_target_pairs={{0,2},{1,3},{2,0},{3,1},{4,6},{5,7},{6,4},{7,5},{8,10},{9,11},{10,... | collective-permute-start | bytes 786440 | tf_op jit(solution)/shard_map/ppermute | solution.py:110
  64.4 15.9 %collective-permute-start.23 = (f32[256,256]{1,0:T(8,128)}, f32[256,256]{1,0:T(8,128)}, u32[]{:S(2)}, u32[]{:S(2)}) collective-permute-start(f32[256,256]{1,0:T(8,128)} %get-tuple-element.28), channel_id=1, source_target_pairs={{0,2},{1,3},{2,0},{3,1},{4,6},{5,7},{6,4},{7,5},{8,10},{9,11},{10,... | collective-permute-start | bytes 786440 | tf_op jit(solution)/shard_map/ppermute | solution.py:110
  67.8 30.2 %copy-start.11 = (f32[256,256]{1,0:T(8,128)}, f32[256,256]{1,0:T(8,128)S(1)}, u32[]{:S(2)}) copy-start(f32[256,256]{1,0:T(8,128)S(1)} %collective-permute-done.16.c3) | copy-start | bytes 786436
  67.8 21.3 %collective-permute-start.14 = (f32[256,256]{1,0:T(8,128)}, f32[256,256]{1,0:T(8,128)}, u32[]{:S(2)}, u32[]{:S(2)}) collective-permute-start(f32[256,256]{1,0:T(8,128)} %get-tuple-element.22), channel_id=1, source_target_pairs={{0,1},{1,0},{2,3},{3,2},{4,5},{5,4},{6,7},{7,6},{8,9},{9,8},{10,11... | collective-permute-start | bytes 786440 | tf_op jit(solution)/shard_map/ppermute | solution.py:110
  74.5 23.5 %copy-start.12 = (f32[256,256]{1,0:T(8,128)}, f32[256,256]{1,0:T(8,128)S(1)}, u32[]{:S(2)}) copy-start(f32[256,256]{1,0:T(8,128)S(1)} %collective-permute-done.15.c2) | copy-start | bytes 786436
  74.5 23.4 %collective-permute-start.7 = (f32[256,256]{1,0:T(8,128)}, f32[256,256]{1,0:T(8,128)}, u32[]{:S(2)}, u32[]{:S(2)}) collective-permute-start(f32[256,256]{1,0:T(8,128)} %get-tuple-element.24), channel_id=1, source_target_pairs={{0,3},{1,2},{2,1},{3,0},{4,7},{5,6},{6,5},{7,4},{8,11},{9,10},{10,... | collective-permute-start | bytes 786440 | tf_op jit(solution)/shard_map/ppermute | solution.py:110
  80.3 21.4 %collective-permute-start.6 = (f32[256,256]{1,0:T(8,128)}, f32[256,256]{1,0:T(8,128)}, u32[]{:S(2)}, u32[]{:S(2)}) collective-permute-start(f32[256,256]{1,0:T(8,128)} %get-tuple-element.25), channel_id=1, source_target_pairs={{0,2},{1,3},{2,0},{3,1},{4,6},{5,7},{6,4},{7,5},{8,10},{9,11},{10,... | collective-permute-start | bytes 786440 | tf_op jit(solution)/shard_map/ppermute | solution.py:110
  81.2 1.0 copy-start.3
  81.3 22.4 %collective-permute-start.5 = (f32[256,256]{1,0:T(8,128)}, f32[256,256]{1,0:T(8,128)}, u32[]{:S(2)}, u32[]{:S(2)}) collective-permute-start(f32[256,256]{1,0:T(8,128)} %get-tuple-element.26), channel_id=1, source_target_pairs={{0,1},{1,0},{2,3},{3,2},{4,5},{5,4},{6,7},{7,6},{8,9},{9,8},{10,11... | collective-permute-start | bytes 786440 | tf_op jit(solution)/shard_map/ppermute | solution.py:110
  89.1 26.9 %collective-permute-start.25 = (f32[512,256]{1,0:T(8,128)}, f32[512,256]{1,0:T(8,128)}, u32[]{:S(2)}, u32[]{:S(2)}) collective-permute-start(f32[512,256]{1,0:T(8,128)} %mul.43), channel_id=1, source_target_pairs={{0,16},{1,17},{2,18},{3,19},{4,20},{5,21},{6,22},{7,23},{8,24},{9,... | collective-permute-start | bytes 1572872 | tf_op jit(solution)/shard_map/ppermute | solution.py:110
  98.0 23.6 %collective-permute-start.21 = (f32[512,256]{1,0:T(8,128)}, f32[512,256]{1,0:T(8,128)S(1)}, u32[]{:S(2)}, u32[]{:S(2)}) collective-permute-start(f32[512,256]{1,0:T(8,128)} %mul.41), channel_id=1, source_target_pairs={{0,16},{1,17},{2,18},{3,19},{4,20},{5,21},{6,22},{7,23},{8,24},{9,... | collective-permute-start | bytes 1572872 | tf_op jit(solution)/shard_map/ppermute | solution.py:110
  101.6 28.1 %collective-permute-start.17 = (f32[512,256]{1,0:T(8,128)}, f32[512,256]{1,0:T(8,128)S(1)}, u32[]{:S(2)}, u32[]{:S(2)}) collective-permute-start(f32[512,256]{1,0:T(8,128)} %mul.39), channel_id=1, source_target_pairs={{0,16},{1,17},{2,18},{3,19},{4,20},{5,21},{6,22},{7,23},{8,24},{9,... | collective-permute-start | bytes 1572872 | tf_op jit(solution)/shard_map/ppermute | solution.py:110
  107.3 33.2 %collective-permute-start.13 = (f32[512,256]{1,0:T(8,128)}, f32[512,256]{1,0:T(8,128)S(1)}, u32[]{:S(2)}, u32[]{:S(2)}) collective-permute-start(f32[512,256]{1,0:T(8,128)} %mul.37), channel_id=1, source_target_pairs={{0,16},{1,17},{2,18},{3,19},{4,20},{5,21},{6,22},{7,23},{8,24},{9,... | collective-permute-start | bytes 1572872 | tf_op jit(solution)/shard_map/ppermute | solution.py:110
  108.1 1.0 copy-start.4
  121.6 0.8 copy-start.15
  129.8 0.8 copy-start.14
  140.5 0.8 copy-start.13

commit v2 on v0

v2 whole, which is shorter than its diff:
```python
import jax
import jax.numpy as jnp
from jax import lax
from jax.experimental import pallas as pl
from jax.experimental.pallas import tpu as pltpu
from jax.sharding import PartitionSpec as P

AXES = ("row", "col", "layer")
F32, BF16 = jnp.float32, jnp.bfloat16
SMEM = pl.BlockSpec(memory_space=pltpu.SMEM)
ANY = pl.BlockSpec(memory_space=pltpu.HBM)
FREE = pl.CostEstimate(flops=0, bytes_accessed=0, transcendentals=0)
OWN = 0
DEPTH = 3
LAG = 2
MOVED = 3
PAIR = 7
CUTLIM = 62
JOINLIM = 32


def gather_plan(amplitudes, integrals):
    amp_panel = lax.all_gather(amplitudes, "layer", axis=1, tiled=True)
    amp_whole = lax.all_gather(amp_panel, "col", axis=1, tiled=True)
    int_mine = lax.all_to_all(integrals, "layer", split_axis=1, concat_axis=0, tiled=True)
    product = jnp.dot(
        amp_whole,
        lax.all_gather(int_mine, "row", axis=0, tiled=True),
        precision=lax.Precision.HIGHEST,
        preferred_element_type=F32,
    )
    return 0.5 * product


def after(value, *done):
    return lax.optimization_barrier((value, *done))[0]


def split(value):
    high = value.astype(BF16)
    return high, (value - high.astype(F32)).astype(BF16)


def copies(pairs, sems):
    made = [pltpu.make_async_copy(src, dst, sems.at[i]) for i, (src, dst) in enumerate(pairs)]
    for copy in made:
        copy.start()
    return made


def cut(integrals, wanted, limit):
    rows, width = integrals.shape[0], integrals.shape[1] // 4
    wide = [sum(n for _, _, n in parts) for parts in wanted]

    def kernel(source, *refs):
        layer = lax.axis_index("layer")
        pairs = []
        for parts, out in zip(wanted, refs):
            to = 0
            for rel, at, n in parts:
                pairs.append((source.at[:, pl.ds(pl.multiple_of((layer ^ rel) * width + at, 128), n)], out.at[:, pl.ds(to, n)]))
                to += n
        for copy in copies(pairs, refs[-1]):
            copy.wait()

    return pl.pallas_call(
        kernel,
        out_shape=[jax.ShapeDtypeStruct((rows, n), F32) for n in wide],
        in_specs=[ANY],
        out_specs=[pl.BlockSpec(memory_space=pltpu.VMEM)] * len(wanted),
        scratch_shapes=[pltpu.SemaphoreType.DMA((sum(len(parts) for parts in wanted),))],
        compiler_params=pltpu.CompilerParams(vmem_limit_bytes=limit << 20),
        cost_estimate=FREE,
        name="cut",
    )(integrals)


def join(integrals, twin, cuts):
    rows, width = integrals.shape[0], integrals.shape[1] // 4

    def kernel(source, theirs, *refs):
        layer = lax.axis_index("layer")
        pairs = []
        for (at, n), out in zip(cuts, refs):
            pairs.append((source.at[:, pl.ds(pl.multiple_of((layer ^ 2) * width + at, 128), n)], out.at[:rows]))
            pairs.append((theirs.at[:, pl.ds(width + at - cuts[0][0], n)], out.at[rows:]))
        for copy in copies(pairs, refs[-1]):
            copy.wait()

    return pl.pallas_call(
        kernel,
        out_shape=[jax.ShapeDtypeStruct((2 * rows, n), F32) for _, n in cuts],
        in_specs=[ANY] * 2,
        out_specs=[pl.BlockSpec(memory_space=pltpu.VMEM)] * len(cuts),
        scratch_shapes=[pltpu.SemaphoreType.DMA((2 * len(cuts),))],
        compiler_params=pltpu.CompilerParams(vmem_limit_bytes=JOINLIM << 20),
        cost_estimate=FREE,
        name="join",
    )(integrals, twin)


def mul(token, blocks, twin, integrals, near, pieces, at, scale):
    _, rows, kb = blocks.shape
    depth, width = integrals.shape[0], integrals.shape[1] // 4
    k = 8 * kb
    n = sum(piece[0].shape[1] for piece in pieces)
    flat = [part for piece in pieces for part in piece]
    count = 8 + 2 * (len(pieces) + 1)

    def kernel(turn, mine, other, source, c1, *refs):
        out, turned, a, b, sems = refs[len(flat) :]
        turned[0] = turn[0]
        layer, p = lax.axis_index("layer"), lax.axis_index("col") % 2
        y, core = layer // 2, layer % 2

        def rows_of(rel):
            return pl.ds(pl.multiple_of((layer ^ rel) * depth, depth), depth)

        pairs = [(source.at[:, pl.ds(pl.multiple_of(layer * width + at, 128), n)], b.at[rows_of(0), :])]
        pairs.append((c1.at[:, pl.ds(at, n)], b.at[rows_of(1), :]))
        to, rest = 0, list(refs)
        for piece in pieces:
            got = [rest.pop(0) for _ in piece]
            wide = piece[0].shape[1]
            c2, c3 = got if len(got) == 2 else (got[0].at[:depth], got[0].at[depth:])
            pairs += [(c2, b.at[rows_of(2), pl.ds(to, wide)]), (c3, b.at[rows_of(3), pl.ds(to, wide)])]
            to += wide
        for rel in range(4):
            slot = (p ^ (rel >> 1)) * 2 + (y ^ (rel & 1))
            for ref, where in ((mine, core), (other, 1 - core)):
                lanes = pl.ds(pl.multiple_of((slot * 2 + where) * kb, kb), kb)
                pairs.append((ref.at[rel], a.at[:, lanes]))
        for copy in copies(pairs, sems):
            copy.wait()
        ah, al = split(a[...])
        for first in range(0, n, 256):
            lanes = pl.ds(first, min(256, n - first))
            bh, bl = split(b[:, lanes])
            out[:, lanes] = scale * (
                jnp.dot(ah, bh, preferred_element_type=F32)
                + jnp.dot(ah, bl, preferred_element_type=F32)
                + jnp.dot(al, bh, preferred_element_type=F32)
            )

    return pl.pallas_call(
        kernel,
        out_shape=(jax.ShapeDtypeStruct((rows, n), F32), jax.ShapeDtypeStruct((1,), jnp.int32)),
        in_specs=[SMEM] + [ANY] * (4 + len(flat)),
        out_specs=(pl.BlockSpec(memory_space=pltpu.VMEM), SMEM),
        scratch_shapes=[pltpu.VMEM((rows, k), F32), pltpu.VMEM((k, n), F32), pltpu.SemaphoreType.DMA((count,))],
        compiler_params=pltpu.CompilerParams(vmem_limit_bytes=24 << 20),
        cost_estimate=FREE,
        name="mul",
    )(token, blocks, twin, integrals, near, *flat)


def add(token, mine, others):
    rows, width = mine.shape
    starts = [sum(o.shape[1] for o in others[:i]) for i in range(len(others))]

    def kernel(turn, a, *refs):
        sources, out, total, sems = refs[: len(others)], refs[-3], refs[-2], refs[-1]
        made = []
        for i, (source, at) in enumerate(zip(sources, starts)):
            lanes = pl.ds(at, others[i].shape[1])
            total[:, lanes] = a[:, lanes] + 0.5 * source[...]
            made.append(pltpu.make_async_copy(total.at[:, lanes], out.at[:, lanes], sems.at[i]))
            made[-1].start()
        for copy in made:
            copy.wait()

    return pl.pallas_call(
        kernel,
        out_shape=jax.ShapeDtypeStruct((rows, width), F32),
        in_specs=[SMEM] + [pl.BlockSpec(memory_space=pltpu.VMEM)] * (1 + len(others)),
        out_specs=ANY,
        scratch_shapes=[pltpu.VMEM((rows, width), F32), pltpu.SemaphoreType.DMA((len(others),))],
        compiler_params=pltpu.CompilerParams(vmem_limit_bytes=24 << 20),
        cost_estimate=FREE,
        name="add",
    )(token, mine, *others)


def swap_plan(C, L, cuts):
    half = C // 2
    every = [(r, c, l) for r in range(2) for c in range(C) for l in range(L)]

    def flat(r, c, l):
        return (r * C + c) * L + l

    def send(value, where, who=lambda r, c, l: True):
        return lax.ppermute(value, AXES, [(flat(*d), flat(*where(*d))) for d in every if who(*d)])

    def home(r, c, l):
        return c // half == r

    def away(r, c, l):
        return c // half != r

    def shards(amplitudes, integrals):
        r, c, l = (lax.axis_index(a) for a in AXES)
        here = c // half == r
        width = integrals.shape[1] // L
        starts = [sum(cuts[:i]) for i in range(len(cuts))]
        last = len(cuts) - 1
        v = {"turn": r.reshape(1).astype(jnp.int32)}

        def tick(*names):
            names = ("turn", *names)
            v.update(zip(names, lax.optimization_barrier([v[name] for name in names])))

        def now(*names):
            tick(*names)
            return v[names[0]] if len(names) == 1 else [v[name] for name in names]

        def twin_of(value):
            return send(value, lambda r, c, l: (r, c, l ^ 1))

        def far_sum(i):
            part, v["turn"] = mul(v["turn"], *v["far"], integrals, v["near_twin"], [v["b", i]], starts[i], 1.0)
            v["sum", i] = send(part, lambda r, c, l: (1 - r, c, l))

        def go(i):
            v["b", i] = [send(now(("slab", i)), lambda r, c, l: (r, c, l ^ 2))]

        v["straight"] = send(amplitudes, lambda r, c, l: (1 - r, c, l), away)
        v["slant"] = send(amplitudes, lambda r, c, l: (1 - r, (c + half) % C, l), away)
        *first, rest = cut(integrals, [[(rel, 0, cuts[0])] for rel in (2, 3)] + [[(1, 0, width), (3, cuts[0], width - cuts[0])]], CUTLIM)
        v["b", 0] = [send(part, lambda r, c, l, rel=rel: (r, c, l ^ rel)) for rel, part in zip((2, 3), first)]
        v["rest"], v["amp"] = lax.optimization_barrier((rest, amplitudes))
        v["turned"] = send(v["amp"], lambda r, c, l: (r, c, l ^ 2), home)
        tick("straight", "slant", ("b", 0), "turned", "rest", "amp")
        other = jnp.where(here, v["straight"], v["slant"])
        v["blocks"] = [other] + [
            send(other, lambda r, c, l, p=p, y=y: (r, c ^ p, l ^ (2 * y))) for p, y in ((0, 1), (1, 0), (1, 1))
        ]
        v["near_twin"] = twin_of(v["rest"])
        slabs = join(integrals, v["near_twin"], [(starts[i], cuts[i]) for i in range(1, last + 1)])
        v.update({("slab", i + 1): slab for i, slab in enumerate(slabs)})
        tick("blocks", "near_twin", "turned", "amp", *[("slab", i) for i in range(1, last + 1)])
        far = jnp.stack(v["blocks"])
        v["far"] = [far, twin_of(far)]
        for i in range(1, DEPTH):
            go(i)
        tick("far")
        for i in range(last + 1):
            if i:
                tick(("b", i))
            if i + DEPTH <= last:
                go(i + DEPTH)
            far_sum(i)
            if i == OWN:
                v["own"] = jnp.stack(now("amp", "turned"))
                v["moved"] = send(v["own"], lambda r, c, l: (r, (c + half) % C, l), home)
            if i >= LAG:
                tick(("sum", i - LAG))
            if i == MOVED:
                tick("moved")
                v["own"] = jnp.where(here, *now("own", "moved"))
                v["pair"] = send(v["own"], lambda r, c, l: (r, c ^ 1, l))
            if i == PAIR:
                tick("pair")
                near = jnp.concatenate(now("own", "pair"))
                v["near"] = [near, twin_of(near)]
        tick("near")
        part, v["turn"] = mul(v["turn"], *v["near"], integrals, v["near_twin"], [v["b", i] for i in range(last + 1)], 0, 0.5)
        return add(v["turn"], part, [v["sum", i] for i in range(last + 1)])

    return shards


def solution(mesh):
    in_specs = (P("row", ("col", "layer")), P(("row", "layer"), "col"))
    out_specs = P("row", ("col", "layer"))
    R, C, L = (mesh.shape[a] for a in AXES)
    plan = swap_plan(C, L, (128, 128, 128, 128, 128, 128, 128, 128)) if (R, C, L) == (2, 4, 4) else gather_plan
    return jax.shard_map(plan, mesh=mesh, in_specs=in_specs, out_specs=out_specs, check_vma=False)
```

time: 240 us -> 104 us (0.43)
  waiting for transfers between devices: 143 us -> 34.8 us
  blocking collectives: 53.9 us -> 0 us
  starting transfers between devices: 0.08 us -> 36.6 us
  Pallas kernels: 0 us -> 29.7 us
  matrix products: 17.8 us -> 0 us
  between operations: 13.1 us -> 0.42 us
  local copies, waits for them, and re-layouts: 11 us -> 2.27 us
    all_gather x3 -> x0, waiting for transfers between devices: 143 us -> none  [the longest x1 104 us: shards(): lax.all_gather(int_mine, 'row', axis=0, tiled=True)]
    all_to_all x1 -> x0, blocking collectives: 53.9 us -> none  [shards(): lax.all_to_all(integrals, 'layer', split_axis=1, concat_axis=0, tiled=True)]
    ppermute x0 -> x28, starting transfers between devices: none -> 36.6 us  [send(): lax.ppermute(value, AXES, [(flat(*d), flat(*where(*d))) for d in every if...]
    ppermute x0 -> x28, waiting for transfers between devices: none -> 34.8 us  [send(): lax.ppermute(value, AXES, [(flat(*d), flat(*where(*d))) for d in every if...]
    pallas_call x0 -> x12, Pallas kernels: none -> 29.7 us  [the longest x9 24.3 us: mul(): pl.pallas_call(kernel, out_shape=(jax.ShapeDtypeStruct((rows, n), F32), j...]
    dot_general x1 -> x0, matrix products: 17.8 us -> none  [shards(): jnp.dot(amp_whole, lax.all_gather(int_mine, 'row', axis=0, tiled=True), p...]
    all_to_all x1 -> x0, local copies, waits for them, and re-layouts: 5.38 us -> none  [shards(): lax.all_to_all(integrals, 'layer', split_axis=1, concat_axis=0, tiled=True)]
    unnamed x1 -> x7, local copies, waits for them, and re-layouts: 5.64 us -> 2.23 us
  transfers between devices with their start and end apart: 3 -> 28, of which waited for: 3 -> 15; matrix products, arithmetic and copies ran while one was open for 5% -> 0% of each run, Pallas kernels for 0% -> 27%
where the time goes in v2:
time: 104 us
  starting transfers between devices  36.6 us (35%)
  waiting for transfers between devices  34.8 us (33%)
  Pallas kernels  29.7 us (29%)
  local copies, waits for them, and re-layouts  2.27 us (2%)
    ppermute x28, starting transfers between devices, send(): lax.ppermute(value, AXES, [(flat(*d), flat(*where(*d))) for d in every if...  36.6 us
    ppermute x28, waiting for transfers between devices, send(): lax.ppermute(value, AXES, [(flat(*d), flat(*where(*d))) for d in every if...  34.8 us
    pallas_call x9, Pallas kernels, mul(): pl.pallas_call(kernel, out_shape=(jax.ShapeDtypeStruct((rows, n), F32), j...  24.3 us
    pallas_call x1, Pallas kernels, cut(): pl.pallas_call(kernel, out_shape=[jax.ShapeDtypeStruct((rows, n), F32) fo...  3.04 us
    unnamed x7, local copies, waits for them, and re-layouts  2.23 us
  transfers between devices with their start and end apart: 28, of which 15 were waited for; matrix products, arithmetic and copies ran while one was open for 0% of the time, Pallas kernels for 27%

profile of v2, /device:TPU:0, one launch (start us, length us, event | category | flops | bytes accessed | tf_op | source)
XLA Modules:
  0.0 104.0 jit_solution(7693620267679513759)
XLA Ops:
  0.0 1.4 %collective-permute-start = (f32[512,128]{1,0:T(8,128)}, f32[512,128]{1,0:T(8,128)S(1)}, u32[]{:S(2)}, u32[]{:S(2)}) collective-permute-start(f32[512,128]{1,0:T(8,128)} %param.2), channel_id=1, source_target_pairs={{8,24},{9,25},{10,26},{11,27},{12,28},{13,29},{14,30},{15,31},{16,... | collective-permute-start | bytes 786440 | tf_op jit(solution)/shard_map/ppermute | solution.py:192
  1.4 0.7 collective-permute-start.1
  2.1 3.0 %cut.1 = (f32[256,128]{1,0:T(8,128)}, f32[256,128]{1,0:T(8,128)}, f32[256,1920]{1,0:T(8,128)}) custom-call(f32[256,4096]{1,0:T(8,128)} %source.21), custom_call_target="tpu_custom_call" | custom-call | tf_op jit(solution)/shard_map/cut/pallas_call | solution.py:66
  5.2 4.9 %collective-permute-start.4 = (f32[512,128]{1,0:T(8,128)S(1)}, f32[512,128]{1,0:T(8,128)S(1)}, u32[]{:S(2)}, u32[]{:S(2)}) collective-permute-start(f32[512,128]{1,0:T(8,128)S(1)} %copy-done.2), channel_id=1, source_target_pairs={{0,2},{1,3},{2,0},{3,1},{4,6},{5,7},{6,4},{7,5},{24,26},{25,27},{2... | collective-permute-start | bytes 786440 | tf_op jit(solution)/shard_map/ppermute | solution.py:192
  10.1 0.9 collective-permute-start.3
  11.0 9.0 %collective-permute-done.2.refs_0_ = f32[256,128]{1,0:T(8,128)S(1)} collective-permute-done((f32[256,128]{1,0:T(8,128)}, f32[256,128]{1,0:T(8,128)S(1)}, u32[]{:S(2)}, u32[]{:S(2)}) %collective-permute-start.2) | collective-permute-done | bytes 131104 | tf_op jit(solution)/shard_map/ppermute | solution.py:192
  20.0 1.3 %collective-permute-done.3.refs_1_ = f32[256,128]{1,0:T(8,128)S(1)} collective-permute-done((f32[256,128]{1,0:T(8,128)}, f32[256,128]{1,0:T(8,128)S(1)}, u32[]{:S(2)}, u32[]{:S(2)}) %collective-permute-start.3) | collective-permute-done | bytes 131104 | tf_op jit(solution)/shard_map/ppermute | solution.py:192
  21.3 0.5 collective-permute-start.8
  21.9 2.8 %collective-permute-start.7 = (f32[512,128]{1,0:T(8,128)S(1)}, f32[512,128]{1,0:T(8,128)S(1)}, u32[]{:S(2)}, u32[]{:S(2)}) collective-permute-start(f32[512,128]{1,0:T(8,128)S(1)} %broadcast_select_fusion.1), channel_id=1, source_target_pairs={{0,6},{1,7},{2,4},{3,5},{4,2},{5,3},{6,0},{7,1},{8,14},{9,15},{10,... | collective-permute-start | bytes 786440 | tf_op jit(solution)/shard_map/ppermute | solution.py:192
  24.7 0.4 collective-permute-start.6
  25.2 0.3 collective-permute-start.5
  25.7 2.2 %copy-done = f32[256,4096]{1,0:T(8,128)S(1)} copy-done((f32[256,4096]{1,0:T(8,128)S(1)}, f32[256,4096]{1,0:T(8,128)}, u32[]{:S(2)}) %copy-start) | copy-done | bytes 4194328
  27.9 0.3 join.1
  28.2 3.8 %collective-permute-done.7 = f32[512,128]{1,0:T(8,128)S(1)} collective-permute-done((f32[512,128]{1,0:T(8,128)S(1)}, f32[512,128]{1,0:T(8,128)S(1)}, u32[]{:S(2)}, u32[]{:S(2)}) %collective-permute-start.7) | collective-permute-done | bytes 262176 | tf_op jit(solution)/shard_map/ppermute | solution.py:192
  32.1 5.0 %collective-permute-done.6 = f32[512,128]{1,0:T(8,128)S(1)} collective-permute-done((f32[512,128]{1,0:T(8,128)S(1)}, f32[512,128]{1,0:T(8,128)S(1)}, u32[]{:S(2)}, u32[]{:S(2)}) %collective-permute-start.6) | collective-permute-done | bytes 262176 | tf_op jit(solution)/shard_map/ppermute | solution.py:192
  37.2 1.5 %collective-permute-start.10 = (f32[512,128]{1,0:T(8,128)S(1)}, f32[512,128]{1,0:T(8,128)S(1)}, u32[]{:S(2)}, u32[]{:S(2)}) collective-permute-start(f32[512,128]{1,0:T(8,128)S(1)} %get-tuple-element.156), channel_id=1, source_target_pairs={{0,2},{1,3},{2,0},{3,1},{4,6},{5,7},{6,4},{7,5},{8,10},{9,11},{10,... | collective-permute-start | bytes 786440 | tf_op jit(solution)/shard_map/ppermute | solution.py:192
  38.7 1.2 %collective-permute-done.9.other = f32[4,512,128]{2,1,0:T(8,128)S(1)} collective-permute-done((f32[4,512,128]{2,1,0:T(8,128)S(1)}, f32[4,512,128]{2,1,0:T(8,128)S(1)}, u32[]{:S(2)}, u32[]{:S(2)}) %collective-permute-start.9) | collective-permute-done | bytes 1048608 | tf_op jit(solution)/shard_map/ppermute | solution.py:192
  39.8 1.8 %mul.9 = (f32[512,128]{1,0:T(8,128)S(1)}, s32[1]{0:T(128)}) custom-call(s32[1]{0:T(128)} %bitcast.turn, f32[4,512,128]{2,1,0:T(8,128)S(1)} %pad_maximum_fusion.mine, f32[4,512,128]{2,1,0:T(8,128)S(1)} %collective-permute-done.9.other, f32[256,4096]{1,0:T(8,128)S(1)} %copy-done.1, f32[256,1920]{1,0:T(8,128)S(1)} %collective-permute-done.8.theirs.c1, ...), custom_call_target="tpu_custom_call" | custom-call | tf_op jit(solution)/shard_map/mul/pallas_call | solution.py:145
  41.7 5.1 %collective-permute-start.15 = (f32[2,512,128]{2,1,0:T(8,128)S(1)}, f32[2,512,128]{2,1,0:T(8,128)S(1)}, u32[]{:S(2)}, u32[]{:S(2)}) collective-permute-start(f32[2,512,128]{2,1,0:T(8,128)S(1)} %pad_maximum_fusion.1), channel_id=1, source_target_pairs={{0,8},{1,9},{2,10},{3,11},{4,12},{5,13},{6,14},{7,15},{24,16},{25,... | collective-permute-start | bytes 1572872 | tf_op jit(solution)/shard_map/ppermute | solution.py:192
  46.7 0.7 collective-permute-start.11
  47.4 1.4 %collective-permute-start.13 = (f32[512,128]{1,0:T(8,128)S(1)}, f32[512,128]{1,0:T(8,128)S(1)}, u32[]{:S(2)}, u32[]{:S(2)}) collective-permute-start(f32[512,128]{1,0:T(8,128)S(1)} %get-tuple-element.170), channel_id=1, source_target_pairs={{0,2},{1,3},{2,0},{3,1},{4,6},{5,7},{6,4},{7,5},{8,10},{9,11},{10,... | collective-permute-start | bytes 786440 | tf_op jit(solution)/shard_map/ppermute | solution.py:192
  48.8 2.5 %mul.10 = (f32[512,128]{1,0:T(8,128)S(1)}, s32[1]{0:T(128)}) custom-call(s32[1]{0:T(128)} %get-tuple-element.159.turn, f32[4,512,128]{2,1,0:T(8,128)S(1)} %pad_maximum_fusion.mine, f32[4,512,128]{2,1,0:T(8,128)S(1)} %collective-permute-done.9.other, f32[256,4096]{1,0:T(8,128)S(1)} %copy-done.1, f32[256,1920]{1,0:T(8,128)S(1)} %collective-permute-done.8.theirs.c1, ...), custom_call_target="tpu_custom_call" | custom-call | tf_op jit(solution)/shard_map/mul/pallas_call | solution.py:145
  51.3 2.1 %collective-permute-start.14 = (f32[512,128]{1,0:T(8,128)S(1)}, f32[512,128]{1,0:T(8,128)S(1)}, u32[]{:S(2)}, u32[]{:S(2)}) collective-permute-start(f32[512,128]{1,0:T(8,128)S(1)} %get-tuple-element.176), channel_id=1, source_target_pairs={{0,16},{1,17},{2,18},{3,19},{4,20},{5,21},{6,22},{7,23},{8,24},{9,... | collective-permute-start | bytes 786440 | tf_op jit(solution)/shard_map/ppermute | solution.py:192
  53.4 2.6 %collective-permute-done.11.refs_0_.refs_3_ = f32[512,128]{1,0:T(8,128)S(1)} collective-permute-done((f32[512,128]{1,0:T(8,128)S(1)}, f32[512,128]{1,0:T(8,128)S(1)}, u32[]{:S(2)}, u32[]{:S(2)}) %collective-permute-start.11) | collective-permute-done | bytes 262176 | tf_op jit(solution)/shard_map/ppermute | solution.py:192
  56.0 2.4 %mul.11 = (f32[512,128]{1,0:T(8,128)S(1)}, s32[1]{0:T(128)}) custom-call(s32[1]{0:T(128)} %get-tuple-element.165.turn, f32[4,512,128]{2,1,0:T(8,128)S(1)} %pad_maximum_fusion.mine, f32[4,512,128]{2,1,0:T(8,128)S(1)} %collective-permute-done.9.other, f32[256,4096]{1,0:T(8,128)S(1)} %copy-done.1, f32[256,1920]{1,0:T(8,128)S(1)} %collective-permute-done.8.theirs.c1, ...), custom_call_target="tpu_custom_call" | custom-call | tf_op jit(solution)/shard_map/mul/pallas_call | solution.py:145
  58.5 0.7 collective-permute-start.18
  59.2 2.4 %collective-permute-done.13.refs_0_.refs_4_ = f32[512,128]{1,0:T(8,128)S(1)} collective-permute-done((f32[512,128]{1,0:T(8,128)S(1)}, f32[512,128]{1,0:T(8,128)S(1)}, u32[]{:S(2)}, u32[]{:S(2)}) %collective-permute-start.13) | collective-permute-done | bytes 262176 | tf_op jit(solution)/shard_map/ppermute | solution.py:192
  61.6 0.6 collective-permute-start.16
  62.2 2.5 %mul.12 = (f32[512,128]{1,0:T(8,128)S(1)}, s32[1]{0:T(128)}) custom-call(s32[1]{0:T(128)} %get-tuple-element.173.turn, f32[4,512,128]{2,1,0:T(8,128)S(1)} %pad_maximum_fusion.mine, f32[4,512,128]{2,1,0:T(8,128)S(1)} %collective-permute-done.9.other, f32[256,4096]{1,0:T(8,128)S(1)} %copy-done.1, f32[256,1920]{1,0:T(8,128)S(1)} %collective-permute-done.8.theirs.c1, ...), custom_call_target="tpu_custom_call" | custom-call | tf_op jit(solution)/shard_map/mul/pallas_call | solution.py:145
  64.7 0.4 collective-permute-start.19
  65.2 5.6 %collective-permute-start.24 = (f32[2,512,128]{2,1,0:T(8,128)S(1)}, f32[2,512,128]{2,1,0:T(8,128)S(1)}, u32[]{:S(2)}, u32[]{:S(2)}) collective-permute-start(f32[2,512,128]{2,1,0:T(8,128)S(1)} %broadcast_select_fusion), channel_id=1, source_target_pairs={{0,4},{1,5},{2,6},{3,7},{4,0},{5,1},{6,2},{7,3},{8,12},{9,13},{10,... | collective-permute-start | bytes 1572872 | tf_op jit(solution)/shard_map/ppermute | solution.py:192
  70.8 0.9 collective-permute-done.16.refs_0_.refs_5_
  71.7 0.6 collective-permute-start.20
  72.3 2.4 %mul.13 = (f32[512,128]{1,0:T(8,128)S(1)}, s32[1]{0:T(128)}) custom-call(s32[1]{0:T(128)} %get-tuple-element.186.turn, f32[4,512,128]{2,1,0:T(8,128)S(1)} %pad_maximum_fusion.mine, f32[4,512,128]{2,1,0:T(8,128)S(1)} %collective-permute-done.9.other, f32[256,4096]{1,0:T(8,128)S(1)} %copy-done.1, f32[256,1920]{1,0:T(8,128)S(1)} %collective-permute-done.8.theirs.c1, ...), custom_call_target="tpu_custom_call" | custom-call | tf_op jit(solution)/shard_map/mul/pallas_call | solution.py:145
  75.1 1.4 %collective-permute-start.22 = (f32[512,128]{1,0:T(8,128)S(1)}, f32[512,128]{1,0:T(8,128)S(1)}, u32[]{:S(2)}, u32[]{:S(2)}) collective-permute-start(f32[512,128]{1,0:T(8,128)S(1)} %get-tuple-element.203), channel_id=1, source_target_pairs={{0,2},{1,3},{2,0},{3,1},{4,6},{5,7},{6,4},{7,5},{8,10},{9,11},{10,... | collective-permute-start | bytes 786440 | tf_op jit(solution)/shard_map/ppermute | solution.py:192
  76.5 2.5 %mul.14 = (f32[512,128]{1,0:T(8,128)S(1)}, s32[1]{0:T(128)}) custom-call(s32[1]{0:T(128)} %get-tuple-element.192.turn, f32[4,512,128]{2,1,0:T(8,128)S(1)} %pad_maximum_fusion.mine, f32[4,512,128]{2,1,0:T(8,128)S(1)} %collective-permute-done.9.other, f32[256,4096]{1,0:T(8,128)S(1)} %copy-done.1, f32[256,1920]{1,0:T(8,128)S(1)} %collective-permute-done.8.theirs.c1, ...), custom_call_target="tpu_custom_call" | custom-call | tf_op jit(solution)/shard_map/mul/pallas_call | solution.py:145
  79.0 1.9 %collective-permute-start.23 = (f32[512,128]{1,0:T(8,128)S(1)}, f32[512,128]{1,0:T(8,128)S(1)}, u32[]{:S(2)}, u32[]{:S(2)}) collective-permute-start(f32[512,128]{1,0:T(8,128)S(1)} %get-tuple-element.207), channel_id=1, source_target_pairs={{0,16},{1,17},{2,18},{3,19},{4,20},{5,21},{6,22},{7,23},{8,24},{9,... | collective-permute-start | bytes 786440 | tf_op jit(solution)/shard_map/ppermute | solution.py:192
  81.0 2.4 %mul.15 = (f32[512,128]{1,0:T(8,128)S(1)}, s32[1]{0:T(128)}) custom-call(s32[1]{0:T(128)} %get-tuple-element.198.turn, f32[4,512,128]{2,1,0:T(8,128)S(1)} %pad_maximum_fusion.mine, f32[4,512,128]{2,1,0:T(8,128)S(1)} %collective-permute-done.9.other, f32[256,4096]{1,0:T(8,128)S(1)} %copy-done.1, f32[256,1920]{1,0:T(8,128)S(1)} %collective-permute-done.8.theirs.c1, ...), custom_call_target="tpu_custom_call" | custom-call | tf_op jit(solution)/shard_map/mul/pallas_call | solution.py:145
  83.4 1.0 collective-permute-done.22.refs_0_.refs_8_
  84.4 2.5 %mul.16 = (f32[512,128]{1,0:T(8,128)S(1)}, s32[1]{0:T(128)}) custom-call(s32[1]{0:T(128)} %get-tuple-element.204.turn, f32[4,512,128]{2,1,0:T(8,128)S(1)} %pad_maximum_fusion.mine, f32[4,512,128]{2,1,0:T(8,128)S(1)} %collective-permute-done.9.other, f32[256,4096]{1,0:T(8,128)S(1)} %copy-done.1, f32[256,1920]{1,0:T(8,128)S(1)} %collective-permute-done.8.theirs.c1, ...), custom_call_target="tpu_custom_call" | custom-call | tf_op jit(solution)/shard_map/mul/pallas_call | solution.py:145
  86.9 0.4 collective-permute-done.23.refs_5_
  87.4 0.8 collective-permute-start.26
  88.2 1.3 %collective-permute-start.27 = (f32[512,128]{1,0:T(8,128)S(1)}, f32[512,128]{1,0:T(8,128)S(1)}, u32[]{:S(2)}, u32[]{:S(2)}) collective-permute-start(f32[512,128]{1,0:T(8,128)S(1)} %get-tuple-element.228), channel_id=1, source_target_pairs={{0,16},{1,17},{2,18},{3,19},{4,20},{5,21},{6,22},{7,23},{8,24},{9,... | collective-permute-start | bytes 786440 | tf_op jit(solution)/shard_map/ppermute | solution.py:192
  89.5 0.6 collective-permute-done.25.other
  90.1 5.4 %mul.17 = (f32[512,1024]{1,0:T(8,128)S(1)}, s32[1]{0:T(128)}) custom-call(s32[1]{0:T(128)} %get-tuple-element.216.turn, f32[4,512,128]{2,1,0:T(8,128)S(1)} %constant_dynamic-update-slice_fusion.mine, f32[4,512,128]{2,1,0:T(8,128)S(1)} %collective-permute-done.25.other, f32[256,4096]{1,0:T(8,128)S(1)} %copy-done.1, ...), custom_call_target="tpu_custom_call" | custom-call | tf_op jit(solution)/shard_map/mul/pallas_call | solution.py:145
  95.4 1.2 %collective-permute-done.26.refs_6_ = f32[512,128]{1,0:T(8,128)S(1)} collective-permute-done((f32[512,128]{1,0:T(8,128)S(1)}, f32[512,128]{1,0:T(8,128)S(1)}, u32[]{:S(2)}, u32[]{:S(2)}) %collective-permute-start.26) | collective-permute-done | bytes 262176 | tf_op jit(solution)/shard_map/ppermute | solution.py:192
  96.6 5.2 %collective-permute-done.27.refs_7_ = f32[512,128]{1,0:T(8,128)S(1)} collective-permute-done((f32[512,128]{1,0:T(8,128)S(1)}, f32[512,128]{1,0:T(8,128)S(1)}, u32[]{:S(2)}, u32[]{:S(2)}) %collective-permute-start.27) | collective-permute-done | bytes 262176 | tf_op jit(solution)/shard_map/ppermute | solution.py:192
  101.8 2.0 %add.2 = f32[512,1024]{1,0:T(8,128)} custom-call(s32[1]{0:T(128)} %get-tuple-element.219.turn, f32[512,1024]{1,0:T(8,128)S(1)} %get-tuple-element.220.a, f32[512,128]{1,0:T(8,128)S(1)} %collective-permute-done.12.refs_0_, f32[512,128]{1,0:T(8,128)S(1)} %collective-permute-done.14.refs_1_, f32[512,128]{1,0:T(8,128)S(1)} %collective-permute-done.17.refs_2_, ...), custom_call_target="tpu_custom_call" | custom-call | tf_op jit(solution)/shard_map/add/pallas_call | solution.py:172
  (32 shorter events, 1.3 us)
Async XLA Ops:
  0.0 5.2 %copy-start.2 = (f32[512,128]{1,0:T(8,128)S(1)}, f32[512,128]{1,0:T(8,128)}, u32[]{:S(2)}) copy-start(f32[512,128]{1,0:T(8,128)} %param.2) | copy-start | bytes 786436
  0.0 21.3 %collective-permute-start = (f32[512,128]{1,0:T(8,128)}, f32[512,128]{1,0:T(8,128)S(1)}, u32[]{:S(2)}, u32[]{:S(2)}) collective-permute-start(f32[512,128]{1,0:T(8,128)} %param.2), channel_id=1, source_target_pairs={{8,24},{9,25},{10,26},{11,27},{12,28},{13,29},{14,30},{15,31},{16,... | collective-permute-start | bytes 786440 | tf_op jit(solution)/shard_map/ppermute | solution.py:192
  1.4 19.9 %collective-permute-start.1 = (f32[512,128]{1,0:T(8,128)}, f32[512,128]{1,0:T(8,128)S(1)}, u32[]{:S(2)}, u32[]{:S(2)}) collective-permute-start(f32[512,128]{1,0:T(8,128)} %param.2), channel_id=1, source_target_pairs={{8,16},{9,17},{10,18},{11,19},{12,20},{13,21},{14,22},{15,23},{16,... | collective-permute-start | bytes 786440 | tf_op jit(solution)/shard_map/ppermute | solution.py:192
  5.2 16.2 %collective-permute-start.4 = (f32[512,128]{1,0:T(8,128)S(1)}, f32[512,128]{1,0:T(8,128)S(1)}, u32[]{:S(2)}, u32[]{:S(2)}) collective-permute-start(f32[512,128]{1,0:T(8,128)S(1)} %copy-done.2), channel_id=1, source_target_pairs={{0,2},{1,3},{2,0},{3,1},{4,6},{5,7},{6,4},{7,5},{24,26},{25,27},{2... | collective-permute-start | bytes 786440 | tf_op jit(solution)/shard_map/ppermute | solution.py:192
  10.1 9.9 %collective-permute-start.2 = (f32[256,128]{1,0:T(8,128)}, f32[256,128]{1,0:T(8,128)S(1)}, u32[]{:S(2)}, u32[]{:S(2)}) collective-permute-start(f32[256,128]{1,0:T(8,128)} %get-tuple-element.117), channel_id=1, source_target_pairs={{0,2},{1,3},{2,0},{3,1},{4,6},{5,7},{6,4},{7,5},{8,10},{9,11},{10,... | collective-permute-start | bytes 393224 | tf_op jit(solution)/shard_map/ppermute | solution.py:192
  10.1 11.2 %collective-permute-start.3 = (f32[256,128]{1,0:T(8,128)}, f32[256,128]{1,0:T(8,128)S(1)}, u32[]{:S(2)}, u32[]{:S(2)}) collective-permute-start(f32[256,128]{1,0:T(8,128)} %get-tuple-element.118), channel_id=1, source_target_pairs={{0,3},{1,2},{2,1},{3,0},{4,7},{5,6},{6,5},{7,4},{8,11},{9,10},{10,... | collective-permute-start | bytes 393224 | tf_op jit(solution)/shard_map/ppermute | solution.py:192
  21.3 4.3 %collective-permute-start.8 = (f32[256,1920]{1,0:T(8,128)}, f32[256,1920]{1,0:T(8,128)S(1)}, u32[]{:S(2)}, u32[]{:S(2)}) collective-permute-start(f32[256,1920]{1,0:T(8,128)} %get-tuple-element.125), channel_id=1, source_target_pairs={{0,1},{1,0},{2,3},{3,2},{4,5},{5,4},{6,7},{7,6},{8,9},{9,8},{10,11... | collective-permute-start | bytes 5898248 | tf_op jit(solution)/shard_map/ppermute | solution.py:192
  21.9 10.2 %collective-permute-start.7 = (f32[512,128]{1,0:T(8,128)S(1)}, f32[512,128]{1,0:T(8,128)S(1)}, u32[]{:S(2)}, u32[]{:S(2)}) collective-permute-start(f32[512,128]{1,0:T(8,128)S(1)} %broadcast_select_fusion.1), channel_id=1, source_target_pairs={{0,6},{1,7},{2,4},{3,5},{4,2},{5,3},{6,0},{7,1},{8,14},{9,15},{10,... | collective-permute-start | bytes 786440 | tf_op jit(solution)/shard_map/ppermute | solution.py:192
  24.7 12.3 %collective-permute-start.6 = (f32[512,128]{1,0:T(8,128)S(1)}, f32[512,128]{1,0:T(8,128)S(1)}, u32[]{:S(2)}, u32[]{:S(2)}) collective-permute-start(f32[512,128]{1,0:T(8,128)S(1)} %broadcast_select_fusion.1), channel_id=1, source_target_pairs={{0,4},{1,5},{2,6},{3,7},{4,0},{5,1},{6,2},{7,3},{8,12},{9,13},{10,... | collective-permute-start | bytes 786440 | tf_op jit(solution)/shard_map/ppermute | solution.py:192
  25.2 11.9 %collective-permute-start.5 = (f32[512,128]{1,0:T(8,128)S(1)}, f32[512,128]{1,0:T(8,128)S(1)}, u32[]{:S(2)}, u32[]{:S(2)}) collective-permute-start(f32[512,128]{1,0:T(8,128)S(1)} %broadcast_select_fusion.1), channel_id=1, source_target_pairs={{0,2},{1,3},{2,0},{3,1},{4,6},{5,7},{6,4},{7,5},{8,10},{9,11},{10,... | collective-permute-start | bytes 786440 | tf_op jit(solution)/shard_map/ppermute | solution.py:192
  25.7 2.2 %copy-start = (f32[256,4096]{1,0:T(8,128)S(1)}, f32[256,4096]{1,0:T(8,128)}, u32[]{:S(2)}) copy-start(f32[256,4096]{1,0:T(8,128)} %source.21) | copy-start | bytes 12582916
  27.9 12.0 %copy-start.1 = (f32[256,4096]{1,0:T(8,128)S(1)}, f32[256,4096]{1,0:T(8,128)}, u32[]{:S(2)}) copy-start(f32[256,4096]{1,0:T(8,128)} %source.21) | copy-start | bytes 12582916
  37.1 2.7 %collective-permute-start.9 = (f32[4,512,128]{2,1,0:T(8,128)S(1)}, f32[4,512,128]{2,1,0:T(8,128)S(1)}, u32[]{:S(2)}, u32[]{:S(2)}) collective-permute-start(f32[4,512,128]{2,1,0:T(8,128)S(1)} %pad_maximum_fusion.mine), channel_id=1, source_target_pairs={{0,1},{1,0},{2,3},{3,2},{4,5},{5,4},{6,7},{7,6},{8,9},{9,8},{10,11... | collective-permute-start | bytes 3145736 | tf_op jit(solution)/shard_map/ppermute | solution.py:192
  37.2 11.6 %collective-permute-start.10 = (f32[512,128]{1,0:T(8,128)S(1)}, f32[512,128]{1,0:T(8,128)S(1)}, u32[]{:S(2)}, u32[]{:S(2)}) collective-permute-start(f32[512,128]{1,0:T(8,128)S(1)} %get-tuple-element.156), channel_id=1, source_target_pairs={{0,2},{1,3},{2,0},{3,1},{4,6},{5,7},{6,4},{7,5},{8,10},{9,11},{10,... | collective-permute-start | bytes 786440 | tf_op jit(solution)/shard_map/ppermute | solution.py:192
  41.7 23.4 %collective-permute-start.15 = (f32[2,512,128]{2,1,0:T(8,128)S(1)}, f32[2,512,128]{2,1,0:T(8,128)S(1)}, u32[]{:S(2)}, u32[]{:S(2)}) collective-permute-start(f32[2,512,128]{2,1,0:T(8,128)S(1)} %pad_maximum_fusion.1), channel_id=1, source_target_pairs={{0,8},{1,9},{2,10},{3,11},{4,12},{5,13},{6,14},{7,15},{24,16},{25,... | collective-permute-start | bytes 1572872 | tf_op jit(solution)/shard_map/ppermute | solution.py:192
  46.7 9.3 %collective-permute-start.11 = (f32[512,128]{1,0:T(8,128)S(1)}, f32[512,128]{1,0:T(8,128)S(1)}, u32[]{:S(2)}, u32[]{:S(2)}) collective-permute-start(f32[512,128]{1,0:T(8,128)S(1)} %get-tuple-element.162), channel_id=1, source_target_pairs={{0,2},{1,3},{2,0},{3,1},{4,6},{5,7},{6,4},{7,5},{8,10},{9,11},{10,... | collective-permute-start | bytes 786440 | tf_op jit(solution)/shard_map/ppermute | solution.py:192
  47.4 11.1 %collective-permute-start.12 = (f32[512,128]{1,0:T(8,128)S(1)}, f32[512,128]{1,0:T(8,128)S(1)}, u32[]{:S(2)}, u32[]{:S(2)}) collective-permute-start(f32[512,128]{1,0:T(8,128)S(1)} %get-tuple-element.168), channel_id=1, source_target_pairs={{0,16},{1,17},{2,18},{3,19},{4,20},{5,21},{6,22},{7,23},{8,24},{9,... | collective-permute-start | bytes 786440 | tf_op jit(solution)/shard_map/ppermute | solution.py:192
  47.4 14.2 %collective-permute-start.13 = (f32[512,128]{1,0:T(8,128)S(1)}, f32[512,128]{1,0:T(8,128)S(1)}, u32[]{:S(2)}, u32[]{:S(2)}) collective-permute-start(f32[512,128]{1,0:T(8,128)S(1)} %get-tuple-element.170), channel_id=1, source_target_pairs={{0,2},{1,3},{2,0},{3,1},{4,6},{5,7},{6,4},{7,5},{8,10},{9,11},{10,... | collective-permute-start | bytes 786440 | tf_op jit(solution)/shard_map/ppermute | solution.py:192
  51.3 13.4 %collective-permute-start.14 = (f32[512,128]{1,0:T(8,128)S(1)}, f32[512,128]{1,0:T(8,128)S(1)}, u32[]{:S(2)}, u32[]{:S(2)}) collective-permute-start(f32[512,128]{1,0:T(8,128)S(1)} %get-tuple-element.176), channel_id=1, source_target_pairs={{0,16},{1,17},{2,18},{3,19},{4,20},{5,21},{6,22},{7,23},{8,24},{9,... | collective-permute-start | bytes 786440 | tf_op jit(solution)/shard_map/ppermute | solution.py:192
  58.4 16.3 %collective-permute-start.17 = (f32[512,128]{1,0:T(8,128)S(1)}, f32[512,128]{1,0:T(8,128)S(1)}, u32[]{:S(2)}, u32[]{:S(2)}) collective-permute-start(f32[512,128]{1,0:T(8,128)S(1)} %get-tuple-element.189), channel_id=1, source_target_pairs={{0,16},{1,17},{2,18},{3,19},{4,20},{5,21},{6,22},{7,23},{8,24},{9,... | collective-permute-start | bytes 786440 | tf_op jit(solution)/shard_map/ppermute | solution.py:192
  58.5 16.5 %collective-permute-start.18 = (f32[512,128]{1,0:T(8,128)S(1)}, f32[512,128]{1,0:T(8,128)S(1)}, u32[]{:S(2)}, u32[]{:S(2)}) collective-permute-start(f32[512,128]{1,0:T(8,128)S(1)} %get-tuple-element.191), channel_id=1, source_target_pairs={{0,2},{1,3},{2,0},{3,1},{4,6},{5,7},{6,4},{7,5},{8,10},{9,11},{10,... | collective-permute-start | bytes 786440 | tf_op jit(solution)/shard_map/ppermute | solution.py:192
  61.6 10.1 %collective-permute-start.16 = (f32[512,128]{1,0:T(8,128)S(1)}, f32[512,128]{1,0:T(8,128)S(1)}, u32[]{:S(2)}, u32[]{:S(2)}) collective-permute-start(f32[512,128]{1,0:T(8,128)S(1)} %get-tuple-element.183), channel_id=1, source_target_pairs={{0,2},{1,3},{2,0},{3,1},{4,6},{5,7},{6,4},{7,5},{8,10},{9,11},{10,... | collective-permute-start | bytes 786440 | tf_op jit(solution)/shard_map/ppermute | solution.py:192
  64.7 14.3 %collective-permute-start.19 = (f32[512,128]{1,0:T(8,128)S(1)}, f32[512,128]{1,0:T(8,128)S(1)}, u32[]{:S(2)}, u32[]{:S(2)}) collective-permute-start(f32[512,128]{1,0:T(8,128)S(1)} %get-tuple-element.195), channel_id=1, source_target_pairs={{0,16},{1,17},{2,18},{3,19},{4,20},{5,21},{6,22},{7,23},{8,24},{9,... | collective-permute-start | bytes 786440 | tf_op jit(solution)/shard_map/ppermute | solution.py:192
  65.2 22.1 %collective-permute-start.24 = (f32[2,512,128]{2,1,0:T(8,128)S(1)}, f32[2,512,128]{2,1,0:T(8,128)S(1)}, u32[]{:S(2)}, u32[]{:S(2)}) collective-permute-start(f32[2,512,128]{2,1,0:T(8,128)S(1)} %broadcast_select_fusion), channel_id=1, source_target_pairs={{0,4},{1,5},{2,6},{3,7},{4,0},{5,1},{6,2},{7,3},{8,12},{9,13},{10,... | collective-permute-start | bytes 1572872 | tf_op jit(solution)/shard_map/ppermute | solution.py:192
  71.7 9.2 %collective-permute-start.20 = (f32[512,128]{1,0:T(8,128)S(1)}, f32[512,128]{1,0:T(8,128)S(1)}, u32[]{:S(2)}, u32[]{:S(2)}) collective-permute-start(f32[512,128]{1,0:T(8,128)S(1)} %get-tuple-element.197), channel_id=1, source_target_pairs={{0,2},{1,3},{2,0},{3,1},{4,6},{5,7},{6,4},{7,5},{8,10},{9,11},{10,... | collective-permute-start | bytes 786440 | tf_op jit(solution)/shard_map/ppermute | solution.py:192
  74.8 8.7 %collective-permute-start.21 = (f32[512,128]{1,0:T(8,128)S(1)}, f32[512,128]{1,0:T(8,128)S(1)}, u32[]{:S(2)}, u32[]{:S(2)}) collective-permute-start(f32[512,128]{1,0:T(8,128)S(1)} %get-tuple-element.201), channel_id=1, source_target_pairs={{0,16},{1,17},{2,18},{3,19},{4,20},{5,21},{6,22},{7,23},{8,24},{9,... | collective-permute-start | bytes 786440 | tf_op jit(solution)/shard_map/ppermute | solution.py:192
  75.1 9.3 %collective-permute-start.22 = (f32[512,128]{1,0:T(8,128)S(1)}, f32[512,128]{1,0:T(8,128)S(1)}, u32[]{:S(2)}, u32[]{:S(2)}) collective-permute-start(f32[512,128]{1,0:T(8,128)S(1)} %get-tuple-element.203), channel_id=1, source_target_pairs={{0,2},{1,3},{2,0},{3,1},{4,6},{5,7},{6,4},{7,5},{8,10},{9,11},{10,... | collective-permute-start | bytes 786440 | tf_op jit(solution)/shard_map/ppermute | solution.py:192
  79.0 8.3 %collective-permute-start.23 = (f32[512,128]{1,0:T(8,128)S(1)}, f32[512,128]{1,0:T(8,128)S(1)}, u32[]{:S(2)}, u32[]{:S(2)}) collective-permute-start(f32[512,128]{1,0:T(8,128)S(1)} %get-tuple-element.207), channel_id=1, source_target_pairs={{0,16},{1,17},{2,18},{3,19},{4,20},{5,21},{6,22},{7,23},{8,24},{9,... | collective-permute-start | bytes 786440 | tf_op jit(solution)/shard_map/ppermute | solution.py:192
  87.3 2.7 %collective-permute-start.25 = (f32[4,512,128]{2,1,0:T(8,128)S(1)}, f32[4,512,128]{2,1,0:T(8,128)S(1)}, u32[]{:S(2)}, u32[]{:S(2)}) collective-permute-start(f32[4,512,128]{2,1,0:T(8,128)S(1)} %constant_dynamic-update-slice_fusion.mine), channel_id=1, source_target_pairs={{0,1},{1,0},{2,3},{3,2},{4,5},{5,4},{6,7},{7,6},{8,9},{9,8},{10,11... | collective-permute-start | bytes 3145736 | tf_op jit(solution)/shard_map/ppermute | solution.py:192
  87.4 9.2 %collective-permute-start.26 = (f32[512,128]{1,0:T(8,128)S(1)}, f32[512,128]{1,0:T(8,128)S(1)}, u32[]{:S(2)}, u32[]{:S(2)}) collective-permute-start(f32[512,128]{1,0:T(8,128)S(1)} %get-tuple-element.227), channel_id=1, source_target_pairs={{0,16},{1,17},{2,18},{3,19},{4,20},{5,21},{6,22},{7,23},{8,24},{9,... | collective-permute-start | bytes 786440 | tf_op jit(solution)/shard_map/ppermute | solution.py:192
  88.2 13.5 %collective-permute-start.27 = (f32[512,128]{1,0:T(8,128)S(1)}, f32[512,128]{1,0:T(8,128)S(1)}, u32[]{:S(2)}, u32[]{:S(2)}) collective-permute-start(f32[512,128]{1,0:T(8,128)S(1)} %get-tuple-element.228), channel_id=1, source_target_pairs={{0,16},{1,17},{2,18},{3,19},{4,20},{5,21},{6,22},{7,23},{8,24},{9,... | collective-permute-start | bytes 786440 | tf_op jit(solution)/shard_map/ppermute | solution.py:192

commit v3 on v2

--- a/solution.py
+++ b/solution.py
@@ -12,7 +12,7 @@
 FREE = pl.CostEstimate(flops=0, bytes_accessed=0, transcendentals=0)
 OWN = 0
 DEPTH = 3
-LAG = 2
+LAG = 1
 MOVED = 3
 PAIR = 7
 CUTLIM = 62
@@ -30,10 +30,6 @@
         preferred_element_type=F32,
     )
     return 0.5 * product
-
-
-def after(value, *done):
-    return lax.optimization_barrier((value, *done))[0]
 
 
 def split(value):
@@ -149,7 +145,7 @@
         out_specs=(pl.BlockSpec(memory_space=pltpu.VMEM), SMEM),
         scratch_shapes=[pltpu.VMEM((rows, k), F32), pltpu.VMEM((k, n), F32), pltpu.SemaphoreType.DMA((count,))],
         compiler_params=pltpu.CompilerParams(vmem_limit_bytes=24 << 20),
-        cost_estimate=FREE,
+        cost_estimate=pl.CostEstimate(flops=6 * rows * n * k, bytes_accessed=0, transcendentals=0),
         name="mul",
     )(token, blocks, twin, integrals, near, *flat)
 
@@ -228,7 +224,7 @@
         *first, rest = cut(integrals, [[(rel, 0, cuts[0])] for rel in (2, 3)] + [[(1, 0, width), (3, cuts[0], width - cuts[0])]], CUTLIM)
         v["b", 0] = [send(part, lambda r, c, l, rel=rel: (r, c, l ^ rel)) for rel, part in zip((2, 3), first)]
         v["rest"], v["amp"] = lax.optimization_barrier((rest, amplitudes))
-        v["turned"] = send(v["amp"], lambda r, c, l: (r, c, l ^ 2), home)
+        v["turned"] = send(amplitudes, lambda r, c, l: (r, c, l ^ 2), home)
         tick("straight", "slant", ("b", 0), "turned", "rest", "amp")
         other = jnp.where(here, v["straight"], v["slant"])
         v["blocks"] = [other] + [

time: 104 us -> 99.8 us (0.960)
  waiting for transfers between devices: 34.8 us -> 30.2 us
    ppermute x28, waiting for transfers between devices: 34.8 us -> 30.2 us  [send(): lax.ppermute(value, AXES, [(flat(*d), flat(*where(*d))) for d in every if...]
  transfers between devices with their start and end apart: 28 -> 28, of which waited for: 15 -> 15; matrix products, arithmetic and copies ran while one was open for 0% -> 0% of each run, Pallas kernels for 27% -> 28%
where the time goes in v3:
time: 99.8 us; the launch traced here: 99.2 us
  starting transfers between devices  36.4 us (36%)
  waiting for transfers between devices  30.2 us (30%)
  Pallas kernels  29.7 us (30%)
  local copies, waits for them, and re-layouts  2.27 us (2%)
    ppermute x28, starting transfers between devices, send(): lax.ppermute(value, AXES, [(flat(*d), flat(*where(*d))) for d in every if...  36.4 us
    ppermute x28, waiting for transfers between devices, send(): lax.ppermute(value, AXES, [(flat(*d), flat(*where(*d))) for d in every if...  30.2 us
    pallas_call x9, Pallas kernels, mul(): pl.pallas_call(kernel, out_shape=(jax.ShapeDtypeStruct((rows, n), F32), j...  24.3 us
    pallas_call x1, Pallas kernels, cut(): pl.pallas_call(kernel, out_shape=[jax.ShapeDtypeStruct((rows, n), F32) fo...  3.04 us
    unnamed x7, local copies, waits for them, and re-layouts  2.23 us
    pallas_call x1, Pallas kernels, add(): pl.pallas_call(kernel, out_shape=jax.ShapeDtypeStruct((rows, width), F32)...  2.02 us
  transfers between devices with their start and end apart: 28, of which 15 were waited for; matrix products, arithmetic and copies ran while one was open for 0% of the time, Pallas kernels for 28%

profile of v3, /device:TPU:0, one launch (start us, length us, event | category | flops | bytes accessed | tf_op | source)
XLA Modules:
  0.0 99.2 jit_solution(4065628597270706263)
XLA Ops:
  0.0 0.7 collective-permute-start.1
  0.7 1.3 %collective-permute-start = (f32[512,128]{1,0:T(8,128)}, f32[512,128]{1,0:T(8,128)S(1)}, u32[]{:S(2)}, u32[]{:S(2)}) collective-permute-start(f32[512,128]{1,0:T(8,128)} %param.2), channel_id=1, source_target_pairs={{8,24},{9,25},{10,26},{11,27},{12,28},{13,29},{14,30},{15,31},{16,... | collective-permute-start | bytes 786440 | tf_op jit(solution)/shard_map/ppermute | solution.py:188
  2.0 4.9 %collective-permute-start.4 = (f32[512,128]{1,0:T(8,128)}, f32[512,128]{1,0:T(8,128)S(1)}, u32[]{:S(2)}, u32[]{:S(2)}) collective-permute-start(f32[512,128]{1,0:T(8,128)} %param.2), channel_id=1, source_target_pairs={{0,2},{1,3},{2,0},{3,1},{4,6},{5,7},{6,4},{7,5},{24,26},{25,27},{2... | collective-permute-start | bytes 786440 | tf_op jit(solution)/shard_map/ppermute | solution.py:188
  6.9 3.0 %cut.1 = (f32[256,128]{1,0:T(8,128)}, f32[256,128]{1,0:T(8,128)}, f32[256,1920]{1,0:T(8,128)}) custom-call(f32[256,4096]{1,0:T(8,128)} %source.21), custom_call_target="tpu_custom_call" | custom-call | tf_op jit(solution)/shard_map/cut/pallas_call | solution.py:62
  10.0 0.9 collective-permute-start.3
  10.9 6.1 %collective-permute-done.2.refs_0_ = f32[256,128]{1,0:T(8,128)S(1)} collective-permute-done((f32[256,128]{1,0:T(8,128)}, f32[256,128]{1,0:T(8,128)S(1)}, u32[]{:S(2)}, u32[]{:S(2)}) %collective-permute-start.2) | collective-permute-done | bytes 131104 | tf_op jit(solution)/shard_map/ppermute | solution.py:188
  17.0 1.3 %collective-permute-done.3.refs_1_ = f32[256,128]{1,0:T(8,128)S(1)} collective-permute-done((f32[256,128]{1,0:T(8,128)}, f32[256,128]{1,0:T(8,128)S(1)}, u32[]{:S(2)}, u32[]{:S(2)}) %collective-permute-start.3) | collective-permute-done | bytes 131104 | tf_op jit(solution)/shard_map/ppermute | solution.py:188
  18.3 0.5 collective-permute-start.8
  18.9 2.8 %collective-permute-start.7 = (f32[512,128]{1,0:T(8,128)S(1)}, f32[512,128]{1,0:T(8,128)S(1)}, u32[]{:S(2)}, u32[]{:S(2)}) collective-permute-start(f32[512,128]{1,0:T(8,128)S(1)} %broadcast_select_fusion.1), channel_id=1, source_target_pairs={{0,6},{1,7},{2,4},{3,5},{4,2},{5,3},{6,0},{7,1},{8,14},{9,15},{10,... | collective-permute-start | bytes 786440 | tf_op jit(solution)/shard_map/ppermute | solution.py:188
  21.7 0.4 collective-permute-start.6
  22.7 2.2 %copy-done = f32[256,4096]{1,0:T(8,128)S(1)} copy-done((f32[256,4096]{1,0:T(8,128)S(1)}, f32[256,4096]{1,0:T(8,128)}, u32[]{:S(2)}) %copy-start) | copy-done | bytes 4194328
  25.2 3.8 %collective-permute-done.7 = f32[512,128]{1,0:T(8,128)S(1)} collective-permute-done((f32[512,128]{1,0:T(8,128)S(1)}, f32[512,128]{1,0:T(8,128)S(1)}, u32[]{:S(2)}, u32[]{:S(2)}) %collective-permute-start.7) | collective-permute-done | bytes 262176 | tf_op jit(solution)/shard_map/ppermute | solution.py:188
  29.1 5.0 %collective-permute-done.6 = f32[512,128]{1,0:T(8,128)S(1)} collective-permute-done((f32[512,128]{1,0:T(8,128)S(1)}, f32[512,128]{1,0:T(8,128)S(1)}, u32[]{:S(2)}, u32[]{:S(2)}) %collective-permute-start.6) | collective-permute-done | bytes 262176 | tf_op jit(solution)/shard_map/ppermute | solution.py:188
  34.2 1.5 %collective-permute-start.12 = (f32[512,128]{1,0:T(8,128)S(1)}, f32[512,128]{1,0:T(8,128)S(1)}, u32[]{:S(2)}, u32[]{:S(2)}) collective-permute-start(f32[512,128]{1,0:T(8,128)S(1)} %get-tuple-element.166), channel_id=1, source_target_pairs={{0,2},{1,3},{2,0},{3,1},{4,6},{5,7},{6,4},{7,5},{8,10},{9,11},{10,... | collective-permute-start | bytes 786440 | tf_op jit(solution)/shard_map/ppermute | solution.py:188
  35.7 0.6 collective-permute-start.10
  36.3 0.6 collective-permute-done.9.other
  36.9 1.8 %mul.9 = (f32[512,128]{1,0:T(8,128)S(1)}, s32[1]{0:T(128)}) custom-call(s32[1]{0:T(128)} %bitcast.turn, f32[4,512,128]{2,1,0:T(8,128)S(1)} %pad_maximum_fusion.mine, f32[4,512,128]{2,1,0:T(8,128)S(1)} %collective-permute-done.9.other, f32[256,4096]{1,0:T(8,128)S(1)} %copy-done.1, f32[256,1920]{1,0:T(8,128)S(1)} %collective-permute-done.8.theirs.c1, ...), custom_call_target="tpu_custom_call" | custom-call | flops 402653184 | tf_op jit(solution)/shard_map/mul/pallas_call | solution.py:141
  38.6 2.0 %collective-permute-start.11 = (f32[512,128]{1,0:T(8,128)S(1)}, f32[512,128]{1,0:T(8,128)S(1)}, u32[]{:S(2)}, u32[]{:S(2)}) collective-permute-start(f32[512,128]{1,0:T(8,128)S(1)} %get-tuple-element.164), channel_id=1, source_target_pairs={{0,16},{1,17},{2,18},{3,19},{4,20},{5,21},{6,22},{7,23},{8,24},{9,... | collective-permute-start | bytes 786440 | tf_op jit(solution)/shard_map/ppermute | solution.py:188
  40.6 4.3 %collective-permute-start.16 = (f32[2,512,128]{2,1,0:T(8,128)S(1)}, f32[2,512,128]{2,1,0:T(8,128)S(1)}, u32[]{:S(2)}, u32[]{:S(2)}) collective-permute-start(f32[2,512,128]{2,1,0:T(8,128)S(1)} %pad_maximum_fusion.1), channel_id=1, source_target_pairs={{0,8},{1,9},{2,10},{3,11},{4,12},{5,13},{6,14},{7,15},{24,16},{25,... | collective-permute-start | bytes 1572872 | tf_op jit(solution)/shard_map/ppermute | solution.py:188
  45.0 3.6 %collective-permute-done.10.refs_0_.refs_2_ = f32[512,128]{1,0:T(8,128)S(1)} collective-permute-done((f32[512,128]{1,0:T(8,128)S(1)}, f32[512,128]{1,0:T(8,128)S(1)}, u32[]{:S(2)}, u32[]{:S(2)}) %collective-permute-start.10) | collective-permute-done | bytes 262176 | tf_op jit(solution)/shard_map/ppermute | solution.py:188
  48.6 2.5 %mul.10 = (f32[512,128]{1,0:T(8,128)S(1)}, s32[1]{0:T(128)}) custom-call(s32[1]{0:T(128)} %get-tuple-element.161.turn, f32[4,512,128]{2,1,0:T(8,128)S(1)} %pad_maximum_fusion.mine, f32[4,512,128]{2,1,0:T(8,128)S(1)} %collective-permute-done.9.other, f32[256,4096]{1,0:T(8,128)S(1)} %copy-done.1, f32[256,1920]{1,0:T(8,128)S(1)} %collective-permute-done.8.theirs.c1, ...), custom_call_target="tpu_custom_call" | custom-call | flops 402653184 | tf_op jit(solution)/shard_map/mul/pallas_call | solution.py:141
  51.0 2.0 %collective-permute-start.13 = (f32[512,128]{1,0:T(8,128)S(1)}, f32[512,128]{1,0:T(8,128)S(1)}, u32[]{:S(2)}, u32[]{:S(2)}) collective-permute-start(f32[512,128]{1,0:T(8,128)S(1)} %get-tuple-element.172), channel_id=1, source_target_pairs={{0,16},{1,17},{2,18},{3,19},{4,20},{5,21},{6,22},{7,23},{8,24},{9,... | collective-permute-start | bytes 786440 | tf_op jit(solution)/shard_map/ppermute | solution.py:188
  53.0 1.4 %collective-permute-start.14 = (f32[512,128]{1,0:T(8,128)S(1)}, f32[512,128]{1,0:T(8,128)S(1)}, u32[]{:S(2)}, u32[]{:S(2)}) collective-permute-start(f32[512,128]{1,0:T(8,128)S(1)} %get-tuple-element.174), channel_id=1, source_target_pairs={{0,2},{1,3},{2,0},{3,1},{4,6},{5,7},{6,4},{7,5},{8,10},{9,11},{10,... | collective-permute-start | bytes 786440 | tf_op jit(solution)/shard_map/ppermute | solution.py:188
  54.4 2.4 %mul.11 = (f32[512,128]{1,0:T(8,128)S(1)}, s32[1]{0:T(128)}) custom-call(s32[1]{0:T(128)} %get-tuple-element.169.turn, f32[4,512,128]{2,1,0:T(8,128)S(1)} %pad_maximum_fusion.mine, f32[4,512,128]{2,1,0:T(8,128)S(1)} %collective-permute-done.9.other, f32[256,4096]{1,0:T(8,128)S(1)} %copy-done.1, f32[256,1920]{1,0:T(8,128)S(1)} %collective-permute-done.8.theirs.c1, ...), custom_call_target="tpu_custom_call" | custom-call | flops 402653184 | tf_op jit(solution)/shard_map/mul/pallas_call | solution.py:141
  57.0 0.6 collective-permute-start.17
  57.7 2.1 %collective-permute-done.13.refs_1_ = f32[512,128]{1,0:T(8,128)S(1)} collective-permute-done((f32[512,128]{1,0:T(8,128)S(1)}, f32[512,128]{1,0:T(8,128)S(1)}, u32[]{:S(2)}, u32[]{:S(2)}) %collective-permute-start.13) | collective-permute-done | bytes 262176 | tf_op jit(solution)/shard_map/ppermute | solution.py:188
  59.7 2.0 %collective-permute-start.19 = (f32[512,128]{1,0:T(8,128)S(1)}, f32[512,128]{1,0:T(8,128)S(1)}, u32[]{:S(2)}, u32[]{:S(2)}) collective-permute-start(f32[512,128]{1,0:T(8,128)S(1)} %get-tuple-element.195), channel_id=1, source_target_pairs={{0,2},{1,3},{2,0},{3,1},{4,6},{5,7},{6,4},{7,5},{8,10},{9,11},{10,... | collective-permute-start | bytes 786440 | tf_op jit(solution)/shard_map/ppermute | solution.py:188
  61.7 0.5 collective-permute-done.14.refs_0_.refs_4_
  62.2 2.5 %mul.12 = (f32[512,128]{1,0:T(8,128)S(1)}, s32[1]{0:T(128)}) custom-call(s32[1]{0:T(128)} %get-tuple-element.177.turn, f32[4,512,128]{2,1,0:T(8,128)S(1)} %pad_maximum_fusion.mine, f32[4,512,128]{2,1,0:T(8,128)S(1)} %collective-permute-done.9.other, f32[256,4096]{1,0:T(8,128)S(1)} %copy-done.1, f32[256,1920]{1,0:T(8,128)S(1)} %collective-permute-done.8.theirs.c1, ...), custom_call_target="tpu_custom_call" | custom-call | flops 402653184 | tf_op jit(solution)/shard_map/mul/pallas_call | solution.py:141
  64.7 1.5 %collective-permute-start.18 = (f32[512,128]{1,0:T(8,128)S(1)}, f32[512,128]{1,0:T(8,128)S(1)}, u32[]{:S(2)}, u32[]{:S(2)}) collective-permute-start(f32[512,128]{1,0:T(8,128)S(1)} %get-tuple-element.193), channel_id=1, source_target_pairs={{0,16},{1,17},{2,18},{3,19},{4,20},{5,21},{6,22},{7,23},{8,24},{9,... | collective-permute-start | bytes 786440 | tf_op jit(solution)/shard_map/ppermute | solution.py:188
  66.1 0.6 collective-permute-start.21
  66.8 1.1 %collective-permute-done.17.refs_0_.refs_5_ = f32[512,128]{1,0:T(8,128)S(1)} collective-permute-done((f32[512,128]{1,0:T(8,128)S(1)}, f32[512,128]{1,0:T(8,128)S(1)}, u32[]{:S(2)}, u32[]{:S(2)}) %collective-permute-start.17) | collective-permute-done | bytes 262176 | tf_op jit(solution)/shard_map/ppermute | solution.py:188
  67.8 2.4 %mul.13 = (f32[512,128]{1,0:T(8,128)S(1)}, s32[1]{0:T(128)}) custom-call(s32[1]{0:T(128)} %get-tuple-element.190.turn, f32[4,512,128]{2,1,0:T(8,128)S(1)} %pad_maximum_fusion.mine, f32[4,512,128]{2,1,0:T(8,128)S(1)} %collective-permute-done.9.other, f32[256,4096]{1,0:T(8,128)S(1)} %copy-done.1, f32[256,1920]{1,0:T(8,128)S(1)} %collective-permute-done.8.theirs.c1, ...), custom_call_target="tpu_custom_call" | custom-call | flops 402653184 | tf_op jit(solution)/shard_map/mul/pallas_call | solution.py:141
  70.3 1.5 %collective-permute-start.20 = (f32[512,128]{1,0:T(8,128)S(1)}, f32[512,128]{1,0:T(8,128)S(1)}, u32[]{:S(2)}, u32[]{:S(2)}) collective-permute-start(f32[512,128]{1,0:T(8,128)S(1)} %get-tuple-element.199), channel_id=1, source_target_pairs={{0,16},{1,17},{2,18},{3,19},{4,20},{5,21},{6,22},{7,23},{8,24},{9,... | collective-permute-start | bytes 786440 | tf_op jit(solution)/shard_map/ppermute | solution.py:188
  71.8 1.0 collective-permute-start.25
  72.8 0.7 collective-permute-done.19.refs_0_.refs_6_
  73.5 2.5 %mul.14 = (f32[512,128]{1,0:T(8,128)S(1)}, s32[1]{0:T(128)}) custom-call(s32[1]{0:T(128)} %get-tuple-element.196.turn, f32[4,512,128]{2,1,0:T(8,128)S(1)} %pad_maximum_fusion.mine, f32[4,512,128]{2,1,0:T(8,128)S(1)} %collective-permute-done.9.other, f32[256,4096]{1,0:T(8,128)S(1)} %copy-done.1, f32[256,1920]{1,0:T(8,128)S(1)} %collective-permute-done.8.theirs.c1, ...), custom_call_target="tpu_custom_call" | custom-call | flops 402653184 | tf_op jit(solution)/shard_map/mul/pallas_call | solution.py:141
  76.3 1.1 %collective-permute-start.23 = (f32[512,128]{1,0:T(8,128)S(1)}, f32[512,128]{1,0:T(8,128)S(1)}, u32[]{:S(2)}, u32[]{:S(2)}) collective-permute-start(f32[512,128]{1,0:T(8,128)S(1)} %get-tuple-element.207), channel_id=1, source_target_pairs={{0,2},{1,3},{2,0},{3,1},{4,6},{5,7},{6,4},{7,5},{8,10},{9,11},{10,... | collective-permute-start | bytes 786440 | tf_op jit(solution)/shard_map/ppermute | solution.py:188
  77.5 2.4 %mul.15 = (f32[512,128]{1,0:T(8,128)S(1)}, s32[1]{0:T(128)}) custom-call(s32[1]{0:T(128)} %get-tuple-element.202.turn, f32[4,512,128]{2,1,0:T(8,128)S(1)} %pad_maximum_fusion.mine, f32[4,512,128]{2,1,0:T(8,128)S(1)} %collective-permute-done.9.other, f32[256,4096]{1,0:T(8,128)S(1)} %copy-done.1, f32[256,1920]{1,0:T(8,128)S(1)} %collective-permute-done.8.theirs.c1, ...), custom_call_target="tpu_custom_call" | custom-call | flops 402653184 | tf_op jit(solution)/shard_map/mul/pallas_call | solution.py:141
  79.9 2.0 %collective-permute-start.24 = (f32[512,128]{1,0:T(8,128)S(1)}, f32[512,128]{1,0:T(8,128)S(1)}, u32[]{:S(2)}, u32[]{:S(2)}) collective-permute-start(f32[512,128]{1,0:T(8,128)S(1)} %get-tuple-element.211), channel_id=1, source_target_pairs={{0,16},{1,17},{2,18},{3,19},{4,20},{5,21},{6,22},{7,23},{8,24},{9,... | collective-permute-start | bytes 786440 | tf_op jit(solution)/shard_map/ppermute | solution.py:188
  81.9 1.6 %collective-permute-done.22.refs_5_ = f32[512,128]{1,0:T(8,128)S(1)} collective-permute-done((f32[512,128]{1,0:T(8,128)S(1)}, f32[512,128]{1,0:T(8,128)S(1)}, u32[]{:S(2)}, u32[]{:S(2)}) %collective-permute-start.22) | collective-permute-done | bytes 262176 | tf_op jit(solution)/shard_map/ppermute | solution.py:188
  83.6 2.5 %mul.16 = (f32[512,128]{1,0:T(8,128)S(1)}, s32[1]{0:T(128)}) custom-call(s32[1]{0:T(128)} %get-tuple-element.208.turn, f32[4,512,128]{2,1,0:T(8,128)S(1)} %pad_maximum_fusion.mine, f32[4,512,128]{2,1,0:T(8,128)S(1)} %collective-permute-done.9.other, f32[256,4096]{1,0:T(8,128)S(1)} %copy-done.1, f32[256,1920]{1,0:T(8,128)S(1)} %collective-permute-done.8.theirs.c1, ...), custom_call_target="tpu_custom_call" | custom-call | flops 402653184 | tf_op jit(solution)/shard_map/mul/pallas_call | solution.py:141
  86.0 2.0 %collective-permute-done.24.refs_6_ = f32[512,128]{1,0:T(8,128)S(1)} collective-permute-done((f32[512,128]{1,0:T(8,128)S(1)}, f32[512,128]{1,0:T(8,128)S(1)}, u32[]{:S(2)}, u32[]{:S(2)}) %collective-permute-start.24) | collective-permute-done | bytes 262176 | tf_op jit(solution)/shard_map/ppermute | solution.py:188
  88.2 1.8 %collective-permute-start.27 = (f32[512,128]{1,0:T(8,128)S(1)}, f32[512,128]{1,0:T(8,128)S(1)}, u32[]{:S(2)}, u32[]{:S(2)}) collective-permute-start(f32[512,128]{1,0:T(8,128)S(1)} %get-tuple-element.232), channel_id=1, source_target_pairs={{0,16},{1,17},{2,18},{3,19},{4,20},{5,21},{6,22},{7,23},{8,24},{9,... | collective-permute-start | bytes 786440 | tf_op jit(solution)/shard_map/ppermute | solution.py:188
  90.0 0.8 collective-permute-done.26.other
  90.9 5.4 %mul.17 = (f32[512,1024]{1,0:T(8,128)S(1)}, s32[1]{0:T(128)}) custom-call(s32[1]{0:T(128)} %get-tuple-element.220.turn, f32[4,512,128]{2,1,0:T(8,128)S(1)} %constant_dynamic-update-slice_fusion.mine, f32[4,512,128]{2,1,0:T(8,128)S(1)} %collective-permute-done.26.other, f32[256,4096]{1,0:T(8,128)S(1)} %copy-done.1, ...), custom_call_target="tpu_custom_call" | custom-call | flops 3221225472 | tf_op jit(solution)/shard_map/mul/pallas_call | solution.py:141
  96.3 0.7 collective-permute-done.27.refs_7_
  97.0 2.0 %add.2 = f32[512,1024]{1,0:T(8,128)} custom-call(s32[1]{0:T(128)} %get-tuple-element.223.turn, f32[512,1024]{1,0:T(8,128)S(1)} %get-tuple-element.224.a, f32[512,128]{1,0:T(8,128)S(1)} %collective-permute-done.11.refs_0_, f32[512,128]{1,0:T(8,128)S(1)} %collective-permute-done.13.refs_1_, f32[512,128]{1,0:T(8,128)S(1)} %collective-permute-done.15.refs_2_, ...), custom_call_target="tpu_custom_call" | custom-call | tf_op jit(solution)/shard_map/add/pallas_call | solution.py:168
  (32 shorter events, 2.0 us)
Async XLA Ops:
  0.0 18.3 %collective-permute-start.1 = (f32[512,128]{1,0:T(8,128)}, f32[512,128]{1,0:T(8,128)S(1)}, u32[]{:S(2)}, u32[]{:S(2)}) collective-permute-start(f32[512,128]{1,0:T(8,128)} %param.2), channel_id=1, source_target_pairs={{8,16},{9,17},{10,18},{11,19},{12,20},{13,21},{14,22},{15,23},{16,... | collective-permute-start | bytes 786440 | tf_op jit(solution)/shard_map/ppermute | solution.py:188
  0.7 17.7 %collective-permute-start = (f32[512,128]{1,0:T(8,128)}, f32[512,128]{1,0:T(8,128)S(1)}, u32[]{:S(2)}, u32[]{:S(2)}) collective-permute-start(f32[512,128]{1,0:T(8,128)} %param.2), channel_id=1, source_target_pairs={{8,24},{9,25},{10,26},{11,27},{12,28},{13,29},{14,30},{15,31},{16,... | collective-permute-start | bytes 786440 | tf_op jit(solution)/shard_map/ppermute | solution.py:188
  2.0 16.4 %collective-permute-start.4 = (f32[512,128]{1,0:T(8,128)}, f32[512,128]{1,0:T(8,128)S(1)}, u32[]{:S(2)}, u32[]{:S(2)}) collective-permute-start(f32[512,128]{1,0:T(8,128)} %param.2), channel_id=1, source_target_pairs={{0,2},{1,3},{2,0},{3,1},{4,6},{5,7},{6,4},{7,5},{24,26},{25,27},{2... | collective-permute-start | bytes 786440 | tf_op jit(solution)/shard_map/ppermute | solution.py:188
  9.9 7.1 %collective-permute-start.2 = (f32[256,128]{1,0:T(8,128)}, f32[256,128]{1,0:T(8,128)S(1)}, u32[]{:S(2)}, u32[]{:S(2)}) collective-permute-start(f32[256,128]{1,0:T(8,128)} %get-tuple-element.119), channel_id=1, source_target_pairs={{0,2},{1,3},{2,0},{3,1},{4,6},{5,7},{6,4},{7,5},{8,10},{9,11},{10,... | collective-permute-start | bytes 393224 | tf_op jit(solution)/shard_map/ppermute | solution.py:188
  10.0 8.3 %collective-permute-start.3 = (f32[256,128]{1,0:T(8,128)}, f32[256,128]{1,0:T(8,128)S(1)}, u32[]{:S(2)}, u32[]{:S(2)}) collective-permute-start(f32[256,128]{1,0:T(8,128)} %get-tuple-element.120), channel_id=1, source_target_pairs={{0,3},{1,2},{2,1},{3,0},{4,7},{5,6},{6,5},{7,4},{8,11},{9,10},{10,... | collective-permute-start | bytes 393224 | tf_op jit(solution)/shard_map/ppermute | solution.py:188
  18.3 4.3 %collective-permute-start.8 = (f32[256,1920]{1,0:T(8,128)}, f32[256,1920]{1,0:T(8,128)S(1)}, u32[]{:S(2)}, u32[]{:S(2)}) collective-permute-start(f32[256,1920]{1,0:T(8,128)} %get-tuple-element.127), channel_id=1, source_target_pairs={{0,1},{1,0},{2,3},{3,2},{4,5},{5,4},{6,7},{7,6},{8,9},{9,8},{10,11... | collective-permute-start | bytes 5898248 | tf_op jit(solution)/shard_map/ppermute | solution.py:188
  18.9 10.2 %collective-permute-start.7 = (f32[512,128]{1,0:T(8,128)S(1)}, f32[512,128]{1,0:T(8,128)S(1)}, u32[]{:S(2)}, u32[]{:S(2)}) collective-permute-start(f32[512,128]{1,0:T(8,128)S(1)} %broadcast_select_fusion.1), channel_id=1, source_target_pairs={{0,6},{1,7},{2,4},{3,5},{4,2},{5,3},{6,0},{7,1},{8,14},{9,15},{10,... | collective-permute-start | bytes 786440 | tf_op jit(solution)/shard_map/ppermute | solution.py:188
  21.7 12.3 %collective-permute-start.6 = (f32[512,128]{1,0:T(8,128)S(1)}, f32[512,128]{1,0:T(8,128)S(1)}, u32[]{:S(2)}, u32[]{:S(2)}) collective-permute-start(f32[512,128]{1,0:T(8,128)S(1)} %broadcast_select_fusion.1), channel_id=1, source_target_pairs={{0,4},{1,5},{2,6},{3,7},{4,0},{5,1},{6,2},{7,3},{8,12},{9,13},{10,... | collective-permute-start | bytes 786440 | tf_op jit(solution)/shard_map/ppermute | solution.py:188
  22.2 11.9 %collective-permute-start.5 = (f32[512,128]{1,0:T(8,128)S(1)}, f32[512,128]{1,0:T(8,128)S(1)}, u32[]{:S(2)}, u32[]{:S(2)}) collective-permute-start(f32[512,128]{1,0:T(8,128)S(1)} %broadcast_select_fusion.1), channel_id=1, source_target_pairs={{0,2},{1,3},{2,0},{3,1},{4,6},{5,7},{6,4},{7,5},{8,10},{9,11},{10,... | collective-permute-start | bytes 786440 | tf_op jit(solution)/shard_map/ppermute | solution.py:188
  22.7 2.2 %copy-start = (f32[256,4096]{1,0:T(8,128)S(1)}, f32[256,4096]{1,0:T(8,128)}, u32[]{:S(2)}) copy-start(f32[256,4096]{1,0:T(8,128)} %source.21) | copy-start | bytes 12582916
  24.9 12.0 %copy-start.1 = (f32[256,4096]{1,0:T(8,128)S(1)}, f32[256,4096]{1,0:T(8,128)}, u32[]{:S(2)}) copy-start(f32[256,4096]{1,0:T(8,128)} %source.21) | copy-start | bytes 12582916
  34.1 6.5 %copy-start.2 = (f32[512,128]{1,0:T(8,128)S(1)}, f32[512,128]{1,0:T(8,128)}, u32[]{:S(2)}) copy-start(f32[512,128]{1,0:T(8,128)} %param.2) | copy-start | bytes 786436
  34.1 2.7 %collective-permute-start.9 = (f32[4,512,128]{2,1,0:T(8,128)S(1)}, f32[4,512,128]{2,1,0:T(8,128)S(1)}, u32[]{:S(2)}, u32[]{:S(2)}) collective-permute-start(f32[4,512,128]{2,1,0:T(8,128)S(1)} %pad_maximum_fusion.mine), channel_id=1, source_target_pairs={{0,1},{1,0},{2,3},{3,2},{4,5},{5,4},{6,7},{7,6},{8,9},{9,8},{10,11... | collective-permute-start | bytes 3145736 | tf_op jit(solution)/shard_map/ppermute | solution.py:188
  34.2 20.2 %collective-permute-start.12 = (f32[512,128]{1,0:T(8,128)S(1)}, f32[512,128]{1,0:T(8,128)S(1)}, u32[]{:S(2)}, u32[]{:S(2)}) collective-permute-start(f32[512,128]{1,0:T(8,128)S(1)} %get-tuple-element.166), channel_id=1, source_target_pairs={{0,2},{1,3},{2,0},{3,1},{4,6},{5,7},{6,4},{7,5},{8,10},{9,11},{10,... | collective-permute-start | bytes 786440 | tf_op jit(solution)/shard_map/ppermute | solution.py:188
  35.7 12.9 %collective-permute-start.10 = (f32[512,128]{1,0:T(8,128)S(1)}, f32[512,128]{1,0:T(8,128)S(1)}, u32[]{:S(2)}, u32[]{:S(2)}) collective-permute-start(f32[512,128]{1,0:T(8,128)S(1)} %get-tuple-element.158), channel_id=1, source_target_pairs={{0,2},{1,3},{2,0},{3,1},{4,6},{5,7},{6,4},{7,5},{8,10},{9,11},{10,... | collective-permute-start | bytes 786440 | tf_op jit(solution)/shard_map/ppermute | solution.py:188
  38.6 15.7 %collective-permute-start.11 = (f32[512,128]{1,0:T(8,128)S(1)}, f32[512,128]{1,0:T(8,128)S(1)}, u32[]{:S(2)}, u32[]{:S(2)}) collective-permute-start(f32[512,128]{1,0:T(8,128)S(1)} %get-tuple-element.164), channel_id=1, source_target_pairs={{0,16},{1,17},{2,18},{3,19},{4,20},{5,21},{6,22},{7,23},{8,24},{9,... | collective-permute-start | bytes 786440 | tf_op jit(solution)/shard_map/ppermute | solution.py:188
  40.6 26.1 %collective-permute-start.16 = (f32[2,512,128]{2,1,0:T(8,128)S(1)}, f32[2,512,128]{2,1,0:T(8,128)S(1)}, u32[]{:S(2)}, u32[]{:S(2)}) collective-permute-start(f32[2,512,128]{2,1,0:T(8,128)S(1)} %pad_maximum_fusion.1), channel_id=1, source_target_pairs={{0,8},{1,9},{2,10},{3,11},{4,12},{5,13},{6,14},{7,15},{24,16},{25,... | collective-permute-start | bytes 1572872 | tf_op jit(solution)/shard_map/ppermute | solution.py:188
  51.0 8.7 %collective-permute-start.13 = (f32[512,128]{1,0:T(8,128)S(1)}, f32[512,128]{1,0:T(8,128)S(1)}, u32[]{:S(2)}, u32[]{:S(2)}) collective-permute-start(f32[512,128]{1,0:T(8,128)S(1)} %get-tuple-element.172), channel_id=1, source_target_pairs={{0,16},{1,17},{2,18},{3,19},{4,20},{5,21},{6,22},{7,23},{8,24},{9,... | collective-permute-start | bytes 786440 | tf_op jit(solution)/shard_map/ppermute | solution.py:188
  53.0 9.2 %collective-permute-start.14 = (f32[512,128]{1,0:T(8,128)S(1)}, f32[512,128]{1,0:T(8,128)S(1)}, u32[]{:S(2)}, u32[]{:S(2)}) collective-permute-start(f32[512,128]{1,0:T(8,128)S(1)} %get-tuple-element.174), channel_id=1, source_target_pairs={{0,2},{1,3},{2,0},{3,1},{4,6},{5,7},{6,4},{7,5},{8,10},{9,11},{10,... | collective-permute-start | bytes 786440 | tf_op jit(solution)/shard_map/ppermute | solution.py:188
  56.8 9.3 %collective-permute-start.15 = (f32[512,128]{1,0:T(8,128)S(1)}, f32[512,128]{1,0:T(8,128)S(1)}, u32[]{:S(2)}, u32[]{:S(2)}) collective-permute-start(f32[512,128]{1,0:T(8,128)S(1)} %get-tuple-element.180), channel_id=1, source_target_pairs={{0,16},{1,17},{2,18},{3,19},{4,20},{5,21},{6,22},{7,23},{8,24},{9,... | collective-permute-start | bytes 786440 | tf_op jit(solution)/shard_map/ppermute | solution.py:188
  57.0 10.8 %collective-permute-start.17 = (f32[512,128]{1,0:T(8,128)S(1)}, f32[512,128]{1,0:T(8,128)S(1)}, u32[]{:S(2)}, u32[]{:S(2)}) collective-permute-start(f32[512,128]{1,0:T(8,128)S(1)} %get-tuple-element.187), channel_id=1, source_target_pairs={{0,2},{1,3},{2,0},{3,1},{4,6},{5,7},{6,4},{7,5},{8,10},{9,11},{10,... | collective-permute-start | bytes 786440 | tf_op jit(solution)/shard_map/ppermute | solution.py:188
  59.7 13.7 %collective-permute-start.19 = (f32[512,128]{1,0:T(8,128)S(1)}, f32[512,128]{1,0:T(8,128)S(1)}, u32[]{:S(2)}, u32[]{:S(2)}) collective-permute-start(f32[512,128]{1,0:T(8,128)S(1)} %get-tuple-element.195), channel_id=1, source_target_pairs={{0,2},{1,3},{2,0},{3,1},{4,6},{5,7},{6,4},{7,5},{8,10},{9,11},{10,... | collective-permute-start | bytes 786440 | tf_op jit(solution)/shard_map/ppermute | solution.py:188
  64.7 8.1 %collective-permute-start.18 = (f32[512,128]{1,0:T(8,128)S(1)}, f32[512,128]{1,0:T(8,128)S(1)}, u32[]{:S(2)}, u32[]{:S(2)}) collective-permute-start(f32[512,128]{1,0:T(8,128)S(1)} %get-tuple-element.193), channel_id=1, source_target_pairs={{0,16},{1,17},{2,18},{3,19},{4,20},{5,21},{6,22},{7,23},{8,24},{9,... | collective-permute-start | bytes 786440 | tf_op jit(solution)/shard_map/ppermute | solution.py:188
  66.1 11.3 %collective-permute-start.21 = (f32[512,128]{1,0:T(8,128)S(1)}, f32[512,128]{1,0:T(8,128)S(1)}, u32[]{:S(2)}, u32[]{:S(2)}) collective-permute-start(f32[512,128]{1,0:T(8,128)S(1)} %get-tuple-element.201), channel_id=1, source_target_pairs={{0,2},{1,3},{2,0},{3,1},{4,6},{5,7},{6,4},{7,5},{8,10},{9,11},{10,... | collective-permute-start | bytes 786440 | tf_op jit(solution)/shard_map/ppermute | solution.py:188
  70.3 7.2 %collective-permute-start.20 = (f32[512,128]{1,0:T(8,128)S(1)}, f32[512,128]{1,0:T(8,128)S(1)}, u32[]{:S(2)}, u32[]{:S(2)}) collective-permute-start(f32[512,128]{1,0:T(8,128)S(1)} %get-tuple-element.199), channel_id=1, source_target_pairs={{0,16},{1,17},{2,18},{3,19},{4,20},{5,21},{6,22},{7,23},{8,24},{9,... | collective-permute-start | bytes 786440 | tf_op jit(solution)/shard_map/ppermute | solution.py:188
  71.8 16.3 %collective-permute-start.25 = (f32[2,512,128]{2,1,0:T(8,128)S(1)}, f32[2,512,128]{2,1,0:T(8,128)S(1)}, u32[]{:S(2)}, u32[]{:S(2)}) collective-permute-start(f32[2,512,128]{2,1,0:T(8,128)S(1)} %broadcast_select_fusion), channel_id=1, source_target_pairs={{0,4},{1,5},{2,6},{3,7},{4,0},{5,1},{6,2},{7,3},{8,12},{9,13},{10,... | collective-permute-start | bytes 1572872 | tf_op jit(solution)/shard_map/ppermute | solution.py:188
  75.9 7.7 %collective-permute-start.22 = (f32[512,128]{1,0:T(8,128)S(1)}, f32[512,128]{1,0:T(8,128)S(1)}, u32[]{:S(2)}, u32[]{:S(2)}) collective-permute-start(f32[512,128]{1,0:T(8,128)S(1)} %get-tuple-element.205), channel_id=1, source_target_pairs={{0,16},{1,17},{2,18},{3,19},{4,20},{5,21},{6,22},{7,23},{8,24},{9,... | collective-permute-start | bytes 786440 | tf_op jit(solution)/shard_map/ppermute | solution.py:188
  76.3 7.3 %collective-permute-start.23 = (f32[512,128]{1,0:T(8,128)S(1)}, f32[512,128]{1,0:T(8,128)S(1)}, u32[]{:S(2)}, u32[]{:S(2)}) collective-permute-start(f32[512,128]{1,0:T(8,128)S(1)} %get-tuple-element.207), channel_id=1, source_target_pairs={{0,2},{1,3},{2,0},{3,1},{4,6},{5,7},{6,4},{7,5},{8,10},{9,11},{10,... | collective-permute-start | bytes 786440 | tf_op jit(solution)/shard_map/ppermute | solution.py:188
  79.9 8.1 %collective-permute-start.24 = (f32[512,128]{1,0:T(8,128)S(1)}, f32[512,128]{1,0:T(8,128)S(1)}, u32[]{:S(2)}, u32[]{:S(2)}) collective-permute-start(f32[512,128]{1,0:T(8,128)S(1)} %get-tuple-element.211), channel_id=1, source_target_pairs={{0,16},{1,17},{2,18},{3,19},{4,20},{5,21},{6,22},{7,23},{8,24},{9,... | collective-permute-start | bytes 786440 | tf_op jit(solution)/shard_map/ppermute | solution.py:188
  88.2 2.7 %collective-permute-start.26 = (f32[4,512,128]{2,1,0:T(8,128)S(1)}, f32[4,512,128]{2,1,0:T(8,128)S(1)}, u32[]{:S(2)}, u32[]{:S(2)}) collective-permute-start(f32[4,512,128]{2,1,0:T(8,128)S(1)} %constant_dynamic-update-slice_fusion.mine), channel_id=1, source_target_pairs={{0,1},{1,0},{2,3},{3,2},{4,5},{5,4},{6,7},{7,6},{8,9},{9,8},{10,11... | collective-permute-start | bytes 3145736 | tf_op jit(solution)/shard_map/ppermute | solution.py:188
  88.2 8.7 %collective-permute-start.27 = (f32[512,128]{1,0:T(8,128)S(1)}, f32[512,128]{1,0:T(8,128)S(1)}, u32[]{:S(2)}, u32[]{:S(2)}) collective-permute-start(f32[512,128]{1,0:T(8,128)S(1)} %get-tuple-element.232), channel_id=1, source_target_pairs={{0,16},{1,17},{2,18},{3,19},{4,20},{5,21},{6,22},{7,23},{8,24},{9,... | collective-permute-start | bytes 786440 | tf_op jit(solution)/shard_map/ppermute | solution.py:188

commit v4 on v3

--- a/solution.py
+++ b/solution.py
@@ -11,12 +11,13 @@
 ANY = pl.BlockSpec(memory_space=pltpu.HBM)
 FREE = pl.CostEstimate(flops=0, bytes_accessed=0, transcendentals=0)
 OWN = 0
-DEPTH = 3
+DEPTH = 4
 LAG = 1
 MOVED = 3
-PAIR = 7
+PAIR = 5
 CUTLIM = 62
 JOINLIM = 32
+SOME = pl.CostEstimate(flops=4 * 10**8, bytes_accessed=0, transcendentals=0)
 
 
 def gather_plan(amplitudes, integrals):
@@ -95,16 +96,18 @@
     )(integrals, twin)
 
 
-def mul(token, blocks, twin, integrals, near, pieces, at, scale):
+def mul(token, blocks, twin, integrals, near, pieces, at, scale, cost=None, sums=()):
     _, rows, kb = blocks.shape
     depth, width = integrals.shape[0], integrals.shape[1] // 4
     k = 8 * kb
     n = sum(piece[0].shape[1] for piece in pieces)
     flat = [part for piece in pieces for part in piece]
-    count = 8 + 2 * (len(pieces) + 1)
+    done = sum(part.shape[1] for part in sums)
+    count = 8 + 2 * (len(pieces) + 1) + len(sums)
 
     def kernel(turn, mine, other, source, c1, *refs):
-        out, turned, a, b, sems = refs[len(flat) :]
+        out, turned, a, b, sems, *more = refs[len(flat) + len(sums) :]
+        others = refs[len(flat) : len(flat) + len(sums)]
         turned[0] = turn[0]
         layer, p = lax.axis_index("layer"), lax.axis_index("col") % 2
         y, core = layer // 2, layer % 2
@@ -126,58 +129,39 @@
             for ref, where in ((mine, core), (other, 1 - core)):
                 lanes = pl.ds(pl.multiple_of((slot * 2 + where) * kb, kb), kb)
                 pairs.append((ref.at[rel], a.at[:, lanes]))
+        to = 0
+        for other_sum, part in zip(others, sums):
+            pairs.append((other_sum, more[0].at[:, pl.ds(to, part.shape[1])]))
+            to += part.shape[1]
         for copy in copies(pairs, sems):
             copy.wait()
         ah, al = split(a[...])
         for first in range(0, n, 256):
             lanes = pl.ds(first, min(256, n - first))
             bh, bl = split(b[:, lanes])
-            out[:, lanes] = scale * (
+            total = (
                 jnp.dot(ah, bh, preferred_element_type=F32)
                 + jnp.dot(ah, bl, preferred_element_type=F32)
                 + jnp.dot(al, bh, preferred_element_type=F32)
             )
+            if first < done:
+                total += more[0][:, lanes]
+            out[:, lanes] = scale * total
 
     return pl.pallas_call(
         kernel,
         out_shape=(jax.ShapeDtypeStruct((rows, n), F32), jax.ShapeDtypeStruct((1,), jnp.int32)),
-        in_specs=[SMEM] + [ANY] * (4 + len(flat)),
+        in_specs=[SMEM] + [ANY] * (4 + len(flat) + len(sums)),
         out_specs=(pl.BlockSpec(memory_space=pltpu.VMEM), SMEM),
-        scratch_shapes=[pltpu.VMEM((rows, k), F32), pltpu.VMEM((k, n), F32), pltpu.SemaphoreType.DMA((count,))],
+        scratch_shapes=[pltpu.VMEM((rows, k), F32), pltpu.VMEM((k, n), F32), pltpu.SemaphoreType.DMA((count,))]
+        + [pltpu.VMEM((rows, done), F32)] * bool(done),
         compiler_params=pltpu.CompilerParams(vmem_limit_bytes=24 << 20),
-        cost_estimate=pl.CostEstimate(flops=6 * rows * n * k, bytes_accessed=0, transcendentals=0),
+        cost_estimate=SOME if cost is None else cost,
         name="mul",
-    )(token, blocks, twin, integrals, near, *flat)
-
-
-def add(token, mine, others):
-    rows, width = mine.shape
-    starts = [sum(o.shape[1] for o in others[:i]) for i in range(len(others))]
-
-    def kernel(turn, a, *refs):
-        sources, out, total, sems = refs[: len(others)], refs[-3], refs[-2], refs[-1]
-        made = []
-        for i, (source, at) in enumerate(zip(sources, starts)):
-            lanes = pl.ds(at, others[i].shape[1])
-            total[:, lanes] = a[:, lanes] + 0.5 * source[...]
-            made.append(pltpu.make_async_copy(total.at[:, lanes], out.at[:, lanes], sems.at[i]))
-            made[-1].start()
-        for copy in made:
-            copy.wait()
-
-    return pl.pallas_call(
-        kernel,
-        out_shape=jax.ShapeDtypeStruct((rows, width), F32),
-        in_specs=[SMEM] + [pl.BlockSpec(memory_space=pltpu.VMEM)] * (1 + len(others)),
-        out_specs=ANY,
-        scratch_shapes=[pltpu.VMEM((rows, width), F32), pltpu.SemaphoreType.DMA((len(others),))],
-        compiler_params=pltpu.CompilerParams(vmem_limit_bytes=24 << 20),
-        cost_estimate=FREE,
-        name="add",
-    )(token, mine, *others)
-
-
-def swap_plan(C, L, cuts):
+    )(token, blocks, twin, integrals, near, *flat, *sums)
+
+
+def swap_plan(C, L, eighths):
     half = C // 2
     every = [(r, c, l) for r in range(2) for c in range(C) for l in range(L)]
 
@@ -197,6 +181,7 @@
         r, c, l = (lax.axis_index(a) for a in AXES)
         here = c // half == r
         width = integrals.shape[1] // L
+        cuts = [width * part // 8 for part in eighths]
         starts = [sum(cuts[:i]) for i in range(len(cuts))]
         last = len(cuts) - 1
         v = {"turn": r.reshape(1).astype(jnp.int32)}
@@ -259,8 +244,8 @@
                 near = jnp.concatenate(now("own", "pair"))
                 v["near"] = [near, twin_of(near)]
         tick("near")
-        part, v["turn"] = mul(v["turn"], *v["near"], integrals, v["near_twin"], [v["b", i] for i in range(last + 1)], 0, 0.5)
-        return add(v["turn"], part, [v["sum", i] for i in range(last + 1)])
+        part, v["turn"] = mul(v["turn"], *v["near"], integrals, v["near_twin"], [v["b", i] for i in range(last + 1)], 0, 0.5, FREE, [v["sum", i] for i in range(last)])
+        return lax.dynamic_update_slice(part, part[:, starts[last] :] + 0.5 * v["sum", last], (0, starts[last]))
 
     return shards
 
@@ -269,5 +254,5 @@
     in_specs = (P("row", ("col", "layer")), P(("row", "layer"), "col"))
     out_specs = P("row", ("col", "layer"))
     R, C, L = (mesh.shape[a] for a in AXES)
-    plan = swap_plan(C, L, (128, 128, 128, 128, 128, 128, 128, 128)) if (R, C, L) == (2, 4, 4) else gather_plan
+    plan = swap_plan(C, L, (1, 1, 1, 2, 1, 2)) if (R, C, L) == (2, 4, 4) else gather_plan
     return jax.shard_map(plan, mesh=mesh, in_specs=in_specs, out_specs=out_specs, check_vma=False)

time: 99.8 us -> 98.3 us (0.985)
  waiting for transfers between devices: 30.2 us -> 37 us
  Pallas kernels: 29.7 us -> 23.1 us
  starting transfers between devices: 36.4 us -> 33.4 us
  other arithmetic: 0.2 us -> 2.09 us
    ppermute x28 -> x24, waiting for transfers between devices: 30.2 us -> 37 us  [send(): lax.ppermute(value, AXES, [(flat(*d), flat(*where(*d))) for d in every if...]
    pallas_call x9 -> x7, Pallas kernels: 24.3 us -> 19.7 us  [mul(): pl.pallas_call(kernel, out_shape=(jax.ShapeDtypeStruct((rows, n), F32), j...]
    ppermute x28 -> x24, starting transfers between devices: 36.4 us -> 33.4 us  [send(): lax.ppermute(value, AXES, [(flat(*d), flat(*where(*d))) for d in every if...]
    pallas_call x1 -> x0, Pallas kernels: 2.02 us -> none  [add(): pl.pallas_call(kernel, out_shape=jax.ShapeDtypeStruct((rows, width), F32)...]
    dynamic_update_slice x0 -> x1, other arithmetic: none -> 1.9 us  [shards(): lax.dynamic_update_slice(part, part[:, starts[last]:] + 0.5 * v['sum', la...]
  transfers between devices with their start and end apart: 28 -> 24, of which waited for: 15 -> 11; matrix products, arithmetic and copies ran while one was open for 0% -> 0% of each run, Pallas kernels for 28% -> 24%
where the time goes in v4:
time: 98.3 us; the launch traced here: 98 us
  waiting for transfers between devices  37 us (38%)
  starting transfers between devices  33.4 us (34%)
  Pallas kernels  23.1 us (23%)
  local copies, waits for them, and re-layouts  2.27 us (2%)
  other arithmetic  2.09 us (2%)
    ppermute x24, waiting for transfers between devices, send(): lax.ppermute(value, AXES, [(flat(*d), flat(*where(*d))) for d in every if...  37 us
    ppermute x24, starting transfers between devices, send(): lax.ppermute(value, AXES, [(flat(*d), flat(*where(*d))) for d in every if...  33.4 us
    pallas_call x7, Pallas kernels, mul(): pl.pallas_call(kernel, out_shape=(jax.ShapeDtypeStruct((rows, n), F32), j...  19.7 us
    pallas_call x1, Pallas kernels, cut(): pl.pallas_call(kernel, out_shape=[jax.ShapeDtypeStruct((rows, n), F32) fo...  3.04 us
    unnamed x7, local copies, waits for them, and re-layouts  2.23 us
  transfers between devices with their start and end apart: 24, of which 11 were waited for; matrix products, arithmetic and copies ran while one was open for 0% of the time, Pallas kernels for 24%

profile of v4, /device:TPU:0, one launch (start us, length us, event | category | flops | bytes accessed | tf_op | source)
XLA Modules:
  0.0 98.0 jit_solution(10808468699446671224)
XLA Ops:
  0.0 0.7 collective-permute-start.1
  0.7 1.3 %collective-permute-start = (f32[512,128]{1,0:T(8,128)}, f32[512,128]{1,0:T(8,128)S(1)}, u32[]{:S(2)}, u32[]{:S(2)}) collective-permute-start(f32[512,128]{1,0:T(8,128)} %param.2), channel_id=1, source_target_pairs={{8,24},{9,25},{10,26},{11,27},{12,28},{13,29},{14,30},{15,31},{16,... | collective-permute-start | bytes 786440 | tf_op jit(solution)/shard_map/ppermute | solution.py:172
  2.0 4.9 %collective-permute-start.4 = (f32[512,128]{1,0:T(8,128)}, f32[512,128]{1,0:T(8,128)S(1)}, u32[]{:S(2)}, u32[]{:S(2)}) collective-permute-start(f32[512,128]{1,0:T(8,128)} %param.2), channel_id=1, source_target_pairs={{0,2},{1,3},{2,0},{3,1},{4,6},{5,7},{6,4},{7,5},{24,26},{25,27},{2... | collective-permute-start | bytes 786440 | tf_op jit(solution)/shard_map/ppermute | solution.py:172
  6.9 3.0 %cut.1 = (f32[256,128]{1,0:T(8,128)}, f32[256,128]{1,0:T(8,128)}, f32[256,1920]{1,0:T(8,128)}) custom-call(f32[256,4096]{1,0:T(8,128)} %source.17), custom_call_target="tpu_custom_call" | custom-call | tf_op jit(solution)/shard_map/cut/pallas_call | solution.py:63
  9.9 0.1 collective-permute-start.2
  10.0 0.9 collective-permute-start.3
  10.9 6.1 %collective-permute-done.2.refs_0_ = f32[256,128]{1,0:T(8,128)S(1)} collective-permute-done((f32[256,128]{1,0:T(8,128)}, f32[256,128]{1,0:T(8,128)S(1)}, u32[]{:S(2)}, u32[]{:S(2)}) %collective-permute-start.2) | collective-permute-done | bytes 131104 | tf_op jit(solution)/shard_map/ppermute | solution.py:172
  17.0 1.3 %collective-permute-done.3.refs_1_ = f32[256,128]{1,0:T(8,128)S(1)} collective-permute-done((f32[256,128]{1,0:T(8,128)}, f32[256,128]{1,0:T(8,128)S(1)}, u32[]{:S(2)}, u32[]{:S(2)}) %collective-permute-start.3) | collective-permute-done | bytes 131104 | tf_op jit(solution)/shard_map/ppermute | solution.py:172
  18.3 0.5 collective-permute-start.8
  18.9 2.8 %collective-permute-start.7 = (f32[512,128]{1,0:T(8,128)S(1)}, f32[512,128]{1,0:T(8,128)S(1)}, u32[]{:S(2)}, u32[]{:S(2)}) collective-permute-start(f32[512,128]{1,0:T(8,128)S(1)} %broadcast_select_fusion.1), channel_id=1, source_target_pairs={{0,6},{1,7},{2,4},{3,5},{4,2},{5,3},{6,0},{7,1},{8,14},{9,15},{10,... | collective-permute-start | bytes 786440 | tf_op jit(solution)/shard_map/ppermute | solution.py:172
  21.7 0.4 collective-permute-start.6
  22.2 0.3 collective-permute-start.5
  22.5 0.2 collective-permute-done.8.theirs.c1
  22.7 2.2 %copy-done = f32[256,4096]{1,0:T(8,128)S(1)} copy-done((f32[256,4096]{1,0:T(8,128)S(1)}, f32[256,4096]{1,0:T(8,128)}, u32[]{:S(2)}) %copy-start) | copy-done | bytes 4194328
  24.9 0.3 join.1
  25.2 3.9 %collective-permute-done.7 = f32[512,128]{1,0:T(8,128)S(1)} collective-permute-done((f32[512,128]{1,0:T(8,128)S(1)}, f32[512,128]{1,0:T(8,128)S(1)}, u32[]{:S(2)}, u32[]{:S(2)}) %collective-permute-start.7) | collective-permute-done | bytes 262176 | tf_op jit(solution)/shard_map/ppermute | solution.py:172
  29.1 5.0 %collective-permute-done.6 = f32[512,128]{1,0:T(8,128)S(1)} collective-permute-done((f32[512,128]{1,0:T(8,128)S(1)}, f32[512,128]{1,0:T(8,128)S(1)}, u32[]{:S(2)}, u32[]{:S(2)}) %collective-permute-start.6) | collective-permute-done | bytes 262176 | tf_op jit(solution)/shard_map/ppermute | solution.py:172
  34.1 0.1 pad_maximum_fusion.mine
  34.1 0.1 collective-permute-start.9
  34.2 1.5 %collective-permute-start.12 = (f32[512,128]{1,0:T(8,128)S(1)}, f32[512,128]{1,0:T(8,128)S(1)}, u32[]{:S(2)}, u32[]{:S(2)}) collective-permute-start(f32[512,128]{1,0:T(8,128)S(1)} %get-tuple-element.145), channel_id=1, source_target_pairs={{0,2},{1,3},{2,0},{3,1},{4,6},{5,7},{6,4},{7,5},{8,10},{9,11},{10,... | collective-permute-start | bytes 786440 | tf_op jit(solution)/shard_map/ppermute | solution.py:172
  35.7 0.6 collective-permute-start.10
  36.3 1.4 %collective-permute-start.14 = (f32[512,256]{1,0:T(8,128)S(1)}, f32[512,256]{1,0:T(8,128)S(1)}, u32[]{:S(2)}, u32[]{:S(2)}) collective-permute-start(f32[512,256]{1,0:T(8,128)S(1)} %get-tuple-element.151), channel_id=1, source_target_pairs={{0,2},{1,3},{2,0},{3,1},{4,6},{5,7},{6,4},{7,5},{8,10},{9,11},{10,... | collective-permute-start | bytes 1572872 | tf_op jit(solution)/shard_map/ppermute | solution.py:172
  37.7 1.8 %mul.17 = (f32[512,128]{1,0:T(8,128)S(1)}, s32[1]{0:T(128)}) custom-call(s32[1]{0:T(128)} %bitcast.turn, f32[4,512,128]{2,1,0:T(8,128)S(1)} %pad_maximum_fusion.mine, f32[4,512,128]{2,1,0:T(8,128)S(1)} %collective-permute-done.9.other, f32[256,4096]{1,0:T(8,128)S(1)} %copy-done.1, f32[256,1920]{1,0:T(8,128)S(1)} %collective-permute-done.8.theirs.c1, ...), custom_call_target="tpu_custom_call" | custom-call | flops 400000000 | tf_op jit(solution)/shard_map/mul/pallas_call | solution.py:151
  39.5 2.0 %collective-permute-start.11 = (f32[512,128]{1,0:T(8,128)S(1)}, f32[512,128]{1,0:T(8,128)S(1)}, u32[]{:S(2)}, u32[]{:S(2)}) collective-permute-start(f32[512,128]{1,0:T(8,128)S(1)} %get-tuple-element.143), channel_id=1, source_target_pairs={{0,16},{1,17},{2,18},{3,19},{4,20},{5,21},{6,22},{7,23},{8,24},{9,... | collective-permute-start | bytes 786440 | tf_op jit(solution)/shard_map/ppermute | solution.py:172
  41.5 4.3 %collective-permute-start.16 = (f32[2,512,128]{2,1,0:T(8,128)S(1)}, f32[2,512,128]{2,1,0:T(8,128)S(1)}, u32[]{:S(2)}, u32[]{:S(2)}) collective-permute-start(f32[2,512,128]{2,1,0:T(8,128)S(1)} %pad_maximum_fusion.1), channel_id=1, source_target_pairs={{0,8},{1,9},{2,10},{3,11},{4,12},{5,13},{6,14},{7,15},{24,16},{25,... | collective-permute-start | bytes 1572872 | tf_op jit(solution)/shard_map/ppermute | solution.py:172
  45.8 3.2 %collective-permute-done.10.refs_0_.refs_2_ = f32[512,128]{1,0:T(8,128)S(1)} collective-permute-done((f32[512,128]{1,0:T(8,128)S(1)}, f32[512,128]{1,0:T(8,128)S(1)}, u32[]{:S(2)}, u32[]{:S(2)}) %collective-permute-start.10) | collective-permute-done | bytes 262176 | tf_op jit(solution)/shard_map/ppermute | solution.py:172
  49.0 2.5 %mul.18 = (f32[512,128]{1,0:T(8,128)S(1)}, s32[1]{0:T(128)}) custom-call(s32[1]{0:T(128)} %get-tuple-element.140.turn, f32[4,512,128]{2,1,0:T(8,128)S(1)} %pad_maximum_fusion.mine, f32[4,512,128]{2,1,0:T(8,128)S(1)} %collective-permute-done.9.other, f32[256,4096]{1,0:T(8,128)S(1)} %copy-done.1, f32[256,1920]{1,0:T(8,128)S(1)} %collective-permute-done.8.theirs.c1, ...), custom_call_target="tpu_custom_call" | custom-call | flops 400000000 | tf_op jit(solution)/shard_map/mul/pallas_call | solution.py:151
  51.5 2.0 %collective-permute-start.13 = (f32[512,128]{1,0:T(8,128)S(1)}, f32[512,128]{1,0:T(8,128)S(1)}, u32[]{:S(2)}, u32[]{:S(2)}) collective-permute-start(f32[512,128]{1,0:T(8,128)S(1)} %get-tuple-element.149), channel_id=1, source_target_pairs={{0,16},{1,17},{2,18},{3,19},{4,20},{5,21},{6,22},{7,23},{8,24},{9,... | collective-permute-start | bytes 786440 | tf_op jit(solution)/shard_map/ppermute | solution.py:172
  53.4 2.4 %mul.19 = (f32[512,128]{1,0:T(8,128)S(1)}, s32[1]{0:T(128)}) custom-call(s32[1]{0:T(128)} %get-tuple-element.146.turn, f32[4,512,128]{2,1,0:T(8,128)S(1)} %pad_maximum_fusion.mine, f32[4,512,128]{2,1,0:T(8,128)S(1)} %collective-permute-done.9.other, f32[256,4096]{1,0:T(8,128)S(1)} %copy-done.1, f32[256,1920]{1,0:T(8,128)S(1)} %collective-permute-done.8.theirs.c1, ...), custom_call_target="tpu_custom_call" | custom-call | flops 400000000 | tf_op jit(solution)/shard_map/mul/pallas_call | solution.py:151
  55.8 0.2 collective-permute-start.15
  56.0 1.4 %collective-permute-start.17 = (f32[512,128]{1,0:T(8,128)S(1)}, f32[512,128]{1,0:T(8,128)S(1)}, u32[]{:S(2)}, u32[]{:S(2)}) collective-permute-start(f32[512,128]{1,0:T(8,128)S(1)} %get-tuple-element.162), channel_id=1, source_target_pairs={{0,2},{1,3},{2,0},{3,1},{4,6},{5,7},{6,4},{7,5},{8,10},{9,11},{10,... | collective-permute-start | bytes 786440 | tf_op jit(solution)/shard_map/ppermute | solution.py:172
  57.4 3.4 %collective-permute-done.13.refs_8_ = f32[512,128]{1,0:T(8,128)S(1)} collective-permute-done((f32[512,128]{1,0:T(8,128)S(1)}, f32[512,128]{1,0:T(8,128)S(1)}, u32[]{:S(2)}, u32[]{:S(2)}) %collective-permute-start.13) | collective-permute-done | bytes 262176 | tf_op jit(solution)/shard_map/ppermute | solution.py:172
  60.8 1.4 %collective-permute-start.19 = (f32[512,256]{1,0:T(8,128)S(1)}, f32[512,256]{1,0:T(8,128)S(1)}, u32[]{:S(2)}, u32[]{:S(2)}) collective-permute-start(f32[512,256]{1,0:T(8,128)S(1)} %get-tuple-element.168), channel_id=1, source_target_pairs={{0,2},{1,3},{2,0},{3,1},{4,6},{5,7},{6,4},{7,5},{8,10},{9,11},{10,... | collective-permute-start | bytes 1572872 | tf_op jit(solution)/shard_map/ppermute | solution.py:172
  62.2 2.2 %mul.20 = (f32[512,256]{1,0:T(8,128)S(1)}, s32[1]{0:T(128)}) custom-call(s32[1]{0:T(128)} %get-tuple-element.152.turn, f32[4,512,128]{2,1,0:T(8,128)S(1)} %pad_maximum_fusion.mine, f32[4,512,128]{2,1,0:T(8,128)S(1)} %collective-permute-done.9.other, f32[256,4096]{1,0:T(8,128)S(1)} %copy-done.1, f32[256,1920]{1,0:T(8,128)S(1)} %collective-permute-done.8.theirs.c1, ...), custom_call_target="tpu_custom_call" | custom-call | flops 400000000 | tf_op jit(solution)/shard_map/mul/pallas_call | solution.py:151
  64.4 2.0 %collective-permute-start.18 = (f32[512,256]{1,0:T(8,128)S(1)}, f32[512,256]{1,0:T(8,128)S(1)}, u32[]{:S(2)}, u32[]{:S(2)}) collective-permute-start(f32[512,256]{1,0:T(8,128)S(1)} %get-tuple-element.166), channel_id=1, source_target_pairs={{0,16},{1,17},{2,18},{3,19},{4,20},{5,21},{6,22},{7,23},{8,24},{9,... | collective-permute-start | bytes 1572872 | tf_op jit(solution)/shard_map/ppermute | solution.py:172
  66.3 0.1 broadcast_select_fusion
  66.4 2.7 %collective-permute-start.21 = (f32[2,512,128]{2,1,0:T(8,128)S(1)}, f32[2,512,128]{2,1,0:T(8,128)S(1)}, u32[]{:S(2)}, u32[]{:S(2)}) collective-permute-start(f32[2,512,128]{2,1,0:T(8,128)S(1)} %broadcast_select_fusion), channel_id=1, source_target_pairs={{0,4},{1,5},{2,6},{3,7},{4,0},{5,1},{6,2},{7,3},{8,12},{9,13},{10,... | collective-permute-start | bytes 1572872 | tf_op jit(solution)/shard_map/ppermute | solution.py:172
  69.1 2.4 %mul.21 = (f32[512,128]{1,0:T(8,128)S(1)}, s32[1]{0:T(128)}) custom-call(s32[1]{0:T(128)} %get-tuple-element.163.turn, f32[4,512,128]{2,1,0:T(8,128)S(1)} %pad_maximum_fusion.mine, f32[4,512,128]{2,1,0:T(8,128)S(1)} %collective-permute-done.9.other, f32[256,4096]{1,0:T(8,128)S(1)} %copy-done.1, f32[256,1920]{1,0:T(8,128)S(1)} %collective-permute-done.8.theirs.c1, ...), custom_call_target="tpu_custom_call" | custom-call | flops 400000000 | tf_op jit(solution)/shard_map/mul/pallas_call | solution.py:151
  71.5 0.1 collective-permute-start.20
  71.6 6.4 %collective-permute-done.18.refs_10_ = f32[512,256]{1,0:T(8,128)S(1)} collective-permute-done((f32[512,256]{1,0:T(8,128)S(1)}, f32[512,256]{1,0:T(8,128)S(1)}, u32[]{:S(2)}, u32[]{:S(2)}) %collective-permute-start.18) | collective-permute-done | bytes 524320 | tf_op jit(solution)/shard_map/ppermute | solution.py:172
  78.0 2.2 %mul.22 = (f32[512,256]{1,0:T(8,128)S(1)}, s32[1]{0:T(128)}) custom-call(s32[1]{0:T(128)} %get-tuple-element.169.turn, f32[4,512,128]{2,1,0:T(8,128)S(1)} %pad_maximum_fusion.mine, f32[4,512,128]{2,1,0:T(8,128)S(1)} %collective-permute-done.9.other, f32[256,4096]{1,0:T(8,128)S(1)} %copy-done.1, f32[256,1920]{1,0:T(8,128)S(1)} %collective-permute-done.8.theirs.c1, ...), custom_call_target="tpu_custom_call" | custom-call | flops 400000000 | tf_op jit(solution)/shard_map/mul/pallas_call | solution.py:151
  80.2 1.4 %collective-permute-done.20.refs_11_ = f32[512,128]{1,0:T(8,128)S(1)} collective-permute-done((f32[512,128]{1,0:T(8,128)S(1)}, f32[512,128]{1,0:T(8,128)S(1)}, u32[]{:S(2)}, u32[]{:S(2)}) %collective-permute-start.20) | collective-permute-done | bytes 262176 | tf_op jit(solution)/shard_map/ppermute | solution.py:172
  81.7 0.1 collective-permute-start.22
  81.7 1.8 %collective-permute-start.23 = (f32[512,256]{1,0:T(8,128)S(1)}, f32[512,256]{1,0:T(8,128)S(1)}, u32[]{:S(2)}, u32[]{:S(2)}) collective-permute-start(f32[512,256]{1,0:T(8,128)S(1)} %get-tuple-element.190), channel_id=1, source_target_pairs={{0,16},{1,17},{2,18},{3,19},{4,20},{5,21},{6,22},{7,23},{8,24},{9,... | collective-permute-start | bytes 1572872 | tf_op jit(solution)/shard_map/ppermute | solution.py:172
  83.5 0.8 collective-permute-done.22.other
  84.4 6.5 %mul.23 = (f32[512,1024]{1,0:T(8,128)}, s32[1]{0:T(128)}) custom-call(s32[1]{0:T(128)} %get-tuple-element.181.turn, f32[4,512,128]{2,1,0:T(8,128)S(1)} %constant_dynamic-update-slice_fusion.mine, f32[4,512,128]{2,1,0:T(8,128)S(1)} %collective-permute-done.22.other, f32[256,4096]{1,0:T(8,128)S(1)} %copy-done.1, ...), custom_call_target="tpu_custom_call" | custom-call | tf_op jit(solution)/shard_map/mul/pallas_call | solution.py:151
  90.9 5.2 %collective-permute-done.23 = f32[512,256]{1,0:T(8,128)S(1)} collective-permute-done((f32[512,256]{1,0:T(8,128)S(1)}, f32[512,256]{1,0:T(8,128)S(1)}, u32[]{:S(2)}, u32[]{:S(2)}) %collective-permute-start.23) | collective-permute-done | bytes 524320 | tf_op jit(solution)/shard_map/ppermute | solution.py:172
  96.1 1.9 %add_dynamic-update-slice_fusion = f32[512,1024]{1,0:T(8,128)} fusion(f32[512,1024]{1,0:T(8,128)} %get-tuple-element.189, f32[512,256]{1,0:T(8,128)S(1)} %collective-permute-done.23), kind=kLoop, calls=%fused_computation.2 | loop fusion | flops 262144 | bytes 1572864 | tf_op jit(solution)/shard_map/dynamic_update_slice | solution.py:248
  (22 shorter events, 0.2 us)
Async XLA Ops:
  0.0 18.3 %collective-permute-start.1 = (f32[512,128]{1,0:T(8,128)}, f32[512,128]{1,0:T(8,128)S(1)}, u32[]{:S(2)}, u32[]{:S(2)}) collective-permute-start(f32[512,128]{1,0:T(8,128)} %param.2), channel_id=1, source_target_pairs={{8,16},{9,17},{10,18},{11,19},{12,20},{13,21},{14,22},{15,23},{16,... | collective-permute-start | bytes 786440 | tf_op jit(solution)/shard_map/ppermute | solution.py:172
  0.7 17.7 %collective-permute-start = (f32[512,128]{1,0:T(8,128)}, f32[512,128]{1,0:T(8,128)S(1)}, u32[]{:S(2)}, u32[]{:S(2)}) collective-permute-start(f32[512,128]{1,0:T(8,128)} %param.2), channel_id=1, source_target_pairs={{8,24},{9,25},{10,26},{11,27},{12,28},{13,29},{14,30},{15,31},{16,... | collective-permute-start | bytes 786440 | tf_op jit(solution)/shard_map/ppermute | solution.py:172
  2.0 16.4 %collective-permute-start.4 = (f32[512,128]{1,0:T(8,128)}, f32[512,128]{1,0:T(8,128)S(1)}, u32[]{:S(2)}, u32[]{:S(2)}) collective-permute-start(f32[512,128]{1,0:T(8,128)} %param.2), channel_id=1, source_target_pairs={{0,2},{1,3},{2,0},{3,1},{4,6},{5,7},{6,4},{7,5},{24,26},{25,27},{2... | collective-permute-start | bytes 786440 | tf_op jit(solution)/shard_map/ppermute | solution.py:172
  9.9 7.1 %collective-permute-start.2 = (f32[256,128]{1,0:T(8,128)}, f32[256,128]{1,0:T(8,128)S(1)}, u32[]{:S(2)}, u32[]{:S(2)}) collective-permute-start(f32[256,128]{1,0:T(8,128)} %get-tuple-element.98), channel_id=1, source_target_pairs={{0,2},{1,3},{2,0},{3,1},{4,6},{5,7},{6,4},{7,5},{8,10},{9,11},{10,... | collective-permute-start | bytes 393224 | tf_op jit(solution)/shard_map/ppermute | solution.py:172
  10.0 8.3 %collective-permute-start.3 = (f32[256,128]{1,0:T(8,128)}, f32[256,128]{1,0:T(8,128)S(1)}, u32[]{:S(2)}, u32[]{:S(2)}) collective-permute-start(f32[256,128]{1,0:T(8,128)} %get-tuple-element.99), channel_id=1, source_target_pairs={{0,3},{1,2},{2,1},{3,0},{4,7},{5,6},{6,5},{7,4},{8,11},{9,10},{10,... | collective-permute-start | bytes 393224 | tf_op jit(solution)/shard_map/ppermute | solution.py:172
  18.3 4.3 %collective-permute-start.8 = (f32[256,1920]{1,0:T(8,128)}, f32[256,1920]{1,0:T(8,128)S(1)}, u32[]{:S(2)}, u32[]{:S(2)}) collective-permute-start(f32[256,1920]{1,0:T(8,128)} %get-tuple-element.106), channel_id=1, source_target_pairs={{0,1},{1,0},{2,3},{3,2},{4,5},{5,4},{6,7},{7,6},{8,9},{9,8},{10,11... | collective-permute-start | bytes 5898248 | tf_op jit(solution)/shard_map/ppermute | solution.py:172
  18.9 10.2 %collective-permute-start.7 = (f32[512,128]{1,0:T(8,128)S(1)}, f32[512,128]{1,0:T(8,128)S(1)}, u32[]{:S(2)}, u32[]{:S(2)}) collective-permute-start(f32[512,128]{1,0:T(8,128)S(1)} %broadcast_select_fusion.1), channel_id=1, source_target_pairs={{0,6},{1,7},{2,4},{3,5},{4,2},{5,3},{6,0},{7,1},{8,14},{9,15},{10,... | collective-permute-start | bytes 786440 | tf_op jit(solution)/shard_map/ppermute | solution.py:172
  21.7 12.3 %collective-permute-start.6 = (f32[512,128]{1,0:T(8,128)S(1)}, f32[512,128]{1,0:T(8,128)S(1)}, u32[]{:S(2)}, u32[]{:S(2)}) collective-permute-start(f32[512,128]{1,0:T(8,128)S(1)} %broadcast_select_fusion.1), channel_id=1, source_target_pairs={{0,4},{1,5},{2,6},{3,7},{4,0},{5,1},{6,2},{7,3},{8,12},{9,13},{10,... | collective-permute-start | bytes 786440 | tf_op jit(solution)/shard_map/ppermute | solution.py:172
  22.2 11.9 %collective-permute-start.5 = (f32[512,128]{1,0:T(8,128)S(1)}, f32[512,128]{1,0:T(8,128)S(1)}, u32[]{:S(2)}, u32[]{:S(2)}) collective-permute-start(f32[512,128]{1,0:T(8,128)S(1)} %broadcast_select_fusion.1), channel_id=1, source_target_pairs={{0,2},{1,3},{2,0},{3,1},{4,6},{5,7},{6,4},{7,5},{8,10},{9,11},{10,... | collective-permute-start | bytes 786440 | tf_op jit(solution)/shard_map/ppermute | solution.py:172
  22.7 2.2 %copy-start = (f32[256,4096]{1,0:T(8,128)S(1)}, f32[256,4096]{1,0:T(8,128)}, u32[]{:S(2)}) copy-start(f32[256,4096]{1,0:T(8,128)} %source.17) | copy-start | bytes 12582916
  24.9 12.9 %copy-start.1 = (f32[256,4096]{1,0:T(8,128)S(1)}, f32[256,4096]{1,0:T(8,128)}, u32[]{:S(2)}) copy-start(f32[256,4096]{1,0:T(8,128)} %source.17) | copy-start | bytes 12582916
  34.1 7.3 %copy-start.2 = (f32[512,128]{1,0:T(8,128)S(1)}, f32[512,128]{1,0:T(8,128)}, u32[]{:S(2)}) copy-start(f32[512,128]{1,0:T(8,128)} %param.2) | copy-start | bytes 786436
  34.1 3.6 %collective-permute-start.9 = (f32[4,512,128]{2,1,0:T(8,128)S(1)}, f32[4,512,128]{2,1,0:T(8,128)S(1)}, u32[]{:S(2)}, u32[]{:S(2)}) collective-permute-start(f32[4,512,128]{2,1,0:T(8,128)S(1)} %pad_maximum_fusion.mine), channel_id=1, source_target_pairs={{0,1},{1,0},{2,3},{3,2},{4,5},{5,4},{6,7},{7,6},{8,9},{9,8},{10,11... | collective-permute-start | bytes 3145736 | tf_op jit(solution)/shard_map/ppermute | solution.py:172
  34.2 19.2 %collective-permute-start.12 = (f32[512,128]{1,0:T(8,128)S(1)}, f32[512,128]{1,0:T(8,128)S(1)}, u32[]{:S(2)}, u32[]{:S(2)}) collective-permute-start(f32[512,128]{1,0:T(8,128)S(1)} %get-tuple-element.145), channel_id=1, source_target_pairs={{0,2},{1,3},{2,0},{3,1},{4,6},{5,7},{6,4},{7,5},{8,10},{9,11},{10,... | collective-permute-start | bytes 786440 | tf_op jit(solution)/shard_map/ppermute | solution.py:172
  35.7 13.3 %collective-permute-start.10 = (f32[512,128]{1,0:T(8,128)S(1)}, f32[512,128]{1,0:T(8,128)S(1)}, u32[]{:S(2)}, u32[]{:S(2)}) collective-permute-start(f32[512,128]{1,0:T(8,128)S(1)} %get-tuple-element.137), channel_id=1, source_target_pairs={{0,2},{1,3},{2,0},{3,1},{4,6},{5,7},{6,4},{7,5},{8,10},{9,11},{10,... | collective-permute-start | bytes 786440 | tf_op jit(solution)/shard_map/ppermute | solution.py:172
  36.3 25.9 %collective-permute-start.14 = (f32[512,256]{1,0:T(8,128)S(1)}, f32[512,256]{1,0:T(8,128)S(1)}, u32[]{:S(2)}, u32[]{:S(2)}) collective-permute-start(f32[512,256]{1,0:T(8,128)S(1)} %get-tuple-element.151), channel_id=1, source_target_pairs={{0,2},{1,3},{2,0},{3,1},{4,6},{5,7},{6,4},{7,5},{8,10},{9,11},{10,... | collective-permute-start | bytes 1572872 | tf_op jit(solution)/shard_map/ppermute | solution.py:172
  39.5 13.9 %collective-permute-start.11 = (f32[512,128]{1,0:T(8,128)S(1)}, f32[512,128]{1,0:T(8,128)S(1)}, u32[]{:S(2)}, u32[]{:S(2)}) collective-permute-start(f32[512,128]{1,0:T(8,128)S(1)} %get-tuple-element.143), channel_id=1, source_target_pairs={{0,16},{1,17},{2,18},{3,19},{4,20},{5,21},{6,22},{7,23},{8,24},{9,... | collective-permute-start | bytes 786440 | tf_op jit(solution)/shard_map/ppermute | solution.py:172
  41.5 24.8 %collective-permute-start.16 = (f32[2,512,128]{2,1,0:T(8,128)S(1)}, f32[2,512,128]{2,1,0:T(8,128)S(1)}, u32[]{:S(2)}, u32[]{:S(2)}) collective-permute-start(f32[2,512,128]{2,1,0:T(8,128)S(1)} %pad_maximum_fusion.1), channel_id=1, source_target_pairs={{0,8},{1,9},{2,10},{3,11},{4,12},{5,13},{6,14},{7,15},{24,16},{25,... | collective-permute-start | bytes 1572872 | tf_op jit(solution)/shard_map/ppermute | solution.py:172
  51.5 9.3 %collective-permute-start.13 = (f32[512,128]{1,0:T(8,128)S(1)}, f32[512,128]{1,0:T(8,128)S(1)}, u32[]{:S(2)}, u32[]{:S(2)}) collective-permute-start(f32[512,128]{1,0:T(8,128)S(1)} %get-tuple-element.149), channel_id=1, source_target_pairs={{0,16},{1,17},{2,18},{3,19},{4,20},{5,21},{6,22},{7,23},{8,24},{9,... | collective-permute-start | bytes 786440 | tf_op jit(solution)/shard_map/ppermute | solution.py:172
  55.8 10.5 %collective-permute-start.15 = (f32[512,128]{1,0:T(8,128)S(1)}, f32[512,128]{1,0:T(8,128)S(1)}, u32[]{:S(2)}, u32[]{:S(2)}) collective-permute-start(f32[512,128]{1,0:T(8,128)S(1)} %get-tuple-element.155), channel_id=1, source_target_pairs={{0,16},{1,17},{2,18},{3,19},{4,20},{5,21},{6,22},{7,23},{8,24},{9,... | collective-permute-start | bytes 786440 | tf_op jit(solution)/shard_map/ppermute | solution.py:172
  56.0 13.1 %collective-permute-start.17 = (f32[512,128]{1,0:T(8,128)S(1)}, f32[512,128]{1,0:T(8,128)S(1)}, u32[]{:S(2)}, u32[]{:S(2)}) collective-permute-start(f32[512,128]{1,0:T(8,128)S(1)} %get-tuple-element.162), channel_id=1, source_target_pairs={{0,2},{1,3},{2,0},{3,1},{4,6},{5,7},{6,4},{7,5},{8,10},{9,11},{10,... | collective-permute-start | bytes 786440 | tf_op jit(solution)/shard_map/ppermute | solution.py:172
  60.8 17.3 %collective-permute-start.19 = (f32[512,256]{1,0:T(8,128)S(1)}, f32[512,256]{1,0:T(8,128)S(1)}, u32[]{:S(2)}, u32[]{:S(2)}) collective-permute-start(f32[512,256]{1,0:T(8,128)S(1)} %get-tuple-element.168), channel_id=1, source_target_pairs={{0,2},{1,3},{2,0},{3,1},{4,6},{5,7},{6,4},{7,5},{8,10},{9,11},{10,... | collective-permute-start | bytes 1572872 | tf_op jit(solution)/shard_map/ppermute | solution.py:172
  64.4 13.7 %collective-permute-start.18 = (f32[512,256]{1,0:T(8,128)S(1)}, f32[512,256]{1,0:T(8,128)S(1)}, u32[]{:S(2)}, u32[]{:S(2)}) collective-permute-start(f32[512,256]{1,0:T(8,128)S(1)} %get-tuple-element.166), channel_id=1, source_target_pairs={{0,16},{1,17},{2,18},{3,19},{4,20},{5,21},{6,22},{7,23},{8,24},{9,... | collective-permute-start | bytes 1572872 | tf_op jit(solution)/shard_map/ppermute | solution.py:172
  66.4 15.2 %collective-permute-start.21 = (f32[2,512,128]{2,1,0:T(8,128)S(1)}, f32[2,512,128]{2,1,0:T(8,128)S(1)}, u32[]{:S(2)}, u32[]{:S(2)}) collective-permute-start(f32[2,512,128]{2,1,0:T(8,128)S(1)} %broadcast_select_fusion), channel_id=1, source_target_pairs={{0,4},{1,5},{2,6},{3,7},{4,0},{5,1},{6,2},{7,3},{8,12},{9,13},{10,... | collective-permute-start | bytes 1572872 | tf_op jit(solution)/shard_map/ppermute | solution.py:172
  71.5 10.1 %collective-permute-start.20 = (f32[512,128]{1,0:T(8,128)S(1)}, f32[512,128]{1,0:T(8,128)S(1)}, u32[]{:S(2)}, u32[]{:S(2)}) collective-permute-start(f32[512,128]{1,0:T(8,128)S(1)} %get-tuple-element.172), channel_id=1, source_target_pairs={{0,16},{1,17},{2,18},{3,19},{4,20},{5,21},{6,22},{7,23},{8,24},{9,... | collective-permute-start | bytes 786440 | tf_op jit(solution)/shard_map/ppermute | solution.py:172
  81.7 2.7 %collective-permute-start.22 = (f32[4,512,128]{2,1,0:T(8,128)S(1)}, f32[4,512,128]{2,1,0:T(8,128)S(1)}, u32[]{:S(2)}, u32[]{:S(2)}) collective-permute-start(f32[4,512,128]{2,1,0:T(8,128)S(1)} %constant_dynamic-update-slice_fusion.mine), channel_id=1, source_target_pairs={{0,1},{1,0},{2,3},{3,2},{4,5},{5,4},{6,7},{7,6},{8,9},{9,8},{10,11... | collective-permute-start | bytes 3145736 | tf_op jit(solution)/shard_map/ppermute | solution.py:172
  81.7 14.3 %collective-permute-start.23 = (f32[512,256]{1,0:T(8,128)S(1)}, f32[512,256]{1,0:T(8,128)S(1)}, u32[]{:S(2)}, u32[]{:S(2)}) collective-permute-start(f32[512,256]{1,0:T(8,128)S(1)} %get-tuple-element.190), channel_id=1, source_target_pairs={{0,16},{1,17},{2,18},{3,19},{4,20},{5,21},{6,22},{7,23},{8,24},{9,... | collective-permute-start | bytes 1572872 | tf_op jit(solution)/shard_map/ppermute | solution.py:172

commit v5 on v4

--- a/solution.py
+++ b/solution.py
@@ -133,12 +133,19 @@
         for other_sum, part in zip(others, sums):
             pairs.append((other_sum, more[0].at[:, pl.ds(to, part.shape[1])]))
             to += part.shape[1]
-        for copy in copies(pairs, sems):
+        made = copies(pairs, sems)
+        early = 2 + 2 * len(pieces)
+        for copy in made[:early]:
+            copy.wait()
+        if len(pieces) == 1:
+            bh, bl = split(b[...])
+        for copy in made[early:]:
             copy.wait()
         ah, al = split(a[...])
         for first in range(0, n, 256):
             lanes = pl.ds(first, min(256, n - first))
-            bh, bl = split(b[:, lanes])
+            if len(pieces) > 1:
+                bh, bl = split(b[:, lanes])
             total = (
                 jnp.dot(ah, bh, preferred_element_type=F32)
                 + jnp.dot(ah, bl, preferred_element_type=F32)

time: 98.3 us -> 98.4 us (level)
  no operation moved by 1% of the time
where the time goes in v5:
time: 98.4 us; the launch traced here: 98.1 us
  waiting for transfers between devices  36.6 us (37%)
  starting transfers between devices  33.3 us (34%)
  Pallas kernels  23.6 us (24%)
  local copies, waits for them, and re-layouts  2.27 us (2%)
  other arithmetic  2.09 us (2%)
    ppermute x24, waiting for transfers between devices, send(): lax.ppermute(value, AXES, [(flat(*d), flat(*where(*d))) for d in every if...  36.6 us
    ppermute x24, starting transfers between devices, send(): lax.ppermute(value, AXES, [(flat(*d), flat(*where(*d))) for d in every if...  33.3 us
    pallas_call x7, Pallas kernels, mul(): pl.pallas_call(kernel, out_shape=(jax.ShapeDtypeStruct((rows, n), F32), j...  20.3 us
    pallas_call x1, Pallas kernels, cut(): pl.pallas_call(kernel, out_shape=[jax.ShapeDtypeStruct((rows, n), F32) fo...  3.04 us
    unnamed x7, local copies, waits for them, and re-layouts  2.23 us
  transfers between devices with their start and end apart: 24, of which 11 were waited for; matrix products, arithmetic and copies ran while one was open for 0% of the time, Pallas kernels for 24%

profile of v5, /device:TPU:0, one launch (start us, length us, event | category | flops | bytes accessed | tf_op | source)
XLA Modules:
  0.0 98.1 jit_solution(4164457463254132893)
XLA Ops:
  0.0 0.7 collective-permute-start.1
  0.7 1.3 %collective-permute-start = (f32[512,128]{1,0:T(8,128)}, f32[512,128]{1,0:T(8,128)S(1)}, u32[]{:S(2)}, u32[]{:S(2)}) collective-permute-start(f32[512,128]{1,0:T(8,128)} %param.2), channel_id=1, source_target_pairs={{8,24},{9,25},{10,26},{11,27},{12,28},{13,29},{14,30},{15,31},{16,... | collective-permute-start | bytes 786440 | tf_op jit(solution)/shard_map/ppermute | solution.py:179
  2.0 4.9 %collective-permute-start.4 = (f32[512,128]{1,0:T(8,128)}, f32[512,128]{1,0:T(8,128)S(1)}, u32[]{:S(2)}, u32[]{:S(2)}) collective-permute-start(f32[512,128]{1,0:T(8,128)} %param.2), channel_id=1, source_target_pairs={{0,2},{1,3},{2,0},{3,1},{4,6},{5,7},{6,4},{7,5},{24,26},{25,27},{2... | collective-permute-start | bytes 786440 | tf_op jit(solution)/shard_map/ppermute | solution.py:179
  6.9 3.0 %cut.1 = (f32[256,128]{1,0:T(8,128)}, f32[256,128]{1,0:T(8,128)}, f32[256,1920]{1,0:T(8,128)}) custom-call(f32[256,4096]{1,0:T(8,128)} %source.17), custom_call_target="tpu_custom_call" | custom-call | tf_op jit(solution)/shard_map/cut/pallas_call | solution.py:63
  9.9 0.1 collective-permute-start.2
  10.0 0.9 collective-permute-start.3
  10.9 6.1 %collective-permute-done.2.refs_0_ = f32[256,128]{1,0:T(8,128)S(1)} collective-permute-done((f32[256,128]{1,0:T(8,128)}, f32[256,128]{1,0:T(8,128)S(1)}, u32[]{:S(2)}, u32[]{:S(2)}) %collective-permute-start.2) | collective-permute-done | bytes 131104 | tf_op jit(solution)/shard_map/ppermute | solution.py:179
  17.0 1.3 %collective-permute-done.3.refs_1_ = f32[256,128]{1,0:T(8,128)S(1)} collective-permute-done((f32[256,128]{1,0:T(8,128)}, f32[256,128]{1,0:T(8,128)S(1)}, u32[]{:S(2)}, u32[]{:S(2)}) %collective-permute-start.3) | collective-permute-done | bytes 131104 | tf_op jit(solution)/shard_map/ppermute | solution.py:179
  18.3 0.5 collective-permute-start.8
  18.9 2.8 %collective-permute-start.7 = (f32[512,128]{1,0:T(8,128)S(1)}, f32[512,128]{1,0:T(8,128)S(1)}, u32[]{:S(2)}, u32[]{:S(2)}) collective-permute-start(f32[512,128]{1,0:T(8,128)S(1)} %broadcast_select_fusion.1), channel_id=1, source_target_pairs={{0,6},{1,7},{2,4},{3,5},{4,2},{5,3},{6,0},{7,1},{8,14},{9,15},{10,... | collective-permute-start | bytes 786440 | tf_op jit(solution)/shard_map/ppermute | solution.py:179
  21.7 0.4 collective-permute-start.6
  22.2 0.3 collective-permute-start.5
  22.5 0.2 collective-permute-done.8.theirs.c1
  22.7 2.2 %copy-done = f32[256,4096]{1,0:T(8,128)S(1)} copy-done((f32[256,4096]{1,0:T(8,128)S(1)}, f32[256,4096]{1,0:T(8,128)}, u32[]{:S(2)}) %copy-start) | copy-done | bytes 4194328
  24.9 0.3 join.1
  25.2 3.9 %collective-permute-done.7 = f32[512,128]{1,0:T(8,128)S(1)} collective-permute-done((f32[512,128]{1,0:T(8,128)S(1)}, f32[512,128]{1,0:T(8,128)S(1)}, u32[]{:S(2)}, u32[]{:S(2)}) %collective-permute-start.7) | collective-permute-done | bytes 262176 | tf_op jit(solution)/shard_map/ppermute | solution.py:179
  29.1 5.0 %collective-permute-done.6 = f32[512,128]{1,0:T(8,128)S(1)} collective-permute-done((f32[512,128]{1,0:T(8,128)S(1)}, f32[512,128]{1,0:T(8,128)S(1)}, u32[]{:S(2)}, u32[]{:S(2)}) %collective-permute-start.6) | collective-permute-done | bytes 262176 | tf_op jit(solution)/shard_map/ppermute | solution.py:179
  34.1 0.1 pad_maximum_fusion.mine
  34.1 0.1 collective-permute-start.9
  34.2 1.5 %collective-permute-start.12 = (f32[512,128]{1,0:T(8,128)S(1)}, f32[512,128]{1,0:T(8,128)S(1)}, u32[]{:S(2)}, u32[]{:S(2)}) collective-permute-start(f32[512,128]{1,0:T(8,128)S(1)} %get-tuple-element.145), channel_id=1, source_target_pairs={{0,2},{1,3},{2,0},{3,1},{4,6},{5,7},{6,4},{7,5},{8,10},{9,11},{10,... | collective-permute-start | bytes 786440 | tf_op jit(solution)/shard_map/ppermute | solution.py:179
  35.7 0.6 collective-permute-start.10
  36.3 1.4 %collective-permute-start.14 = (f32[512,256]{1,0:T(8,128)S(1)}, f32[512,256]{1,0:T(8,128)S(1)}, u32[]{:S(2)}, u32[]{:S(2)}) collective-permute-start(f32[512,256]{1,0:T(8,128)S(1)} %get-tuple-element.151), channel_id=1, source_target_pairs={{0,2},{1,3},{2,0},{3,1},{4,6},{5,7},{6,4},{7,5},{8,10},{9,11},{10,... | collective-permute-start | bytes 1572872 | tf_op jit(solution)/shard_map/ppermute | solution.py:179
  37.7 1.8 %mul.17 = (f32[512,128]{1,0:T(8,128)S(1)}, s32[1]{0:T(128)}) custom-call(s32[1]{0:T(128)} %bitcast.turn, f32[4,512,128]{2,1,0:T(8,128)S(1)} %pad_maximum_fusion.mine, f32[4,512,128]{2,1,0:T(8,128)S(1)} %collective-permute-done.9.other, f32[256,4096]{1,0:T(8,128)S(1)} %copy-done.1, f32[256,1920]{1,0:T(8,128)S(1)} %collective-permute-done.8.theirs.c1, ...), custom_call_target="tpu_custom_call" | custom-call | flops 400000000 | tf_op jit(solution)/shard_map/mul/pallas_call | solution.py:158
  39.6 2.0 %collective-permute-start.11 = (f32[512,128]{1,0:T(8,128)S(1)}, f32[512,128]{1,0:T(8,128)S(1)}, u32[]{:S(2)}, u32[]{:S(2)}) collective-permute-start(f32[512,128]{1,0:T(8,128)S(1)} %get-tuple-element.143), channel_id=1, source_target_pairs={{0,16},{1,17},{2,18},{3,19},{4,20},{5,21},{6,22},{7,23},{8,24},{9,... | collective-permute-start | bytes 786440 | tf_op jit(solution)/shard_map/ppermute | solution.py:179
  41.6 4.3 %collective-permute-start.16 = (f32[2,512,128]{2,1,0:T(8,128)S(1)}, f32[2,512,128]{2,1,0:T(8,128)S(1)}, u32[]{:S(2)}, u32[]{:S(2)}) collective-permute-start(f32[2,512,128]{2,1,0:T(8,128)S(1)} %pad_maximum_fusion.1), channel_id=1, source_target_pairs={{0,8},{1,9},{2,10},{3,11},{4,12},{5,13},{6,14},{7,15},{24,16},{25,... | collective-permute-start | bytes 1572872 | tf_op jit(solution)/shard_map/ppermute | solution.py:179
  45.9 3.1 %collective-permute-done.10.refs_0_.refs_2_ = f32[512,128]{1,0:T(8,128)S(1)} collective-permute-done((f32[512,128]{1,0:T(8,128)S(1)}, f32[512,128]{1,0:T(8,128)S(1)}, u32[]{:S(2)}, u32[]{:S(2)}) %collective-permute-start.10) | collective-permute-done | bytes 262176 | tf_op jit(solution)/shard_map/ppermute | solution.py:179
  49.0 2.5 %mul.18 = (f32[512,128]{1,0:T(8,128)S(1)}, s32[1]{0:T(128)}) custom-call(s32[1]{0:T(128)} %get-tuple-element.140.turn, f32[4,512,128]{2,1,0:T(8,128)S(1)} %pad_maximum_fusion.mine, f32[4,512,128]{2,1,0:T(8,128)S(1)} %collective-permute-done.9.other, f32[256,4096]{1,0:T(8,128)S(1)} %copy-done.1, f32[256,1920]{1,0:T(8,128)S(1)} %collective-permute-done.8.theirs.c1, ...), custom_call_target="tpu_custom_call" | custom-call | flops 400000000 | tf_op jit(solution)/shard_map/mul/pallas_call | solution.py:158
  51.5 2.0 %collective-permute-start.13 = (f32[512,128]{1,0:T(8,128)S(1)}, f32[512,128]{1,0:T(8,128)S(1)}, u32[]{:S(2)}, u32[]{:S(2)}) collective-permute-start(f32[512,128]{1,0:T(8,128)S(1)} %get-tuple-element.149), channel_id=1, source_target_pairs={{0,16},{1,17},{2,18},{3,19},{4,20},{5,21},{6,22},{7,23},{8,24},{9,... | collective-permute-start | bytes 786440 | tf_op jit(solution)/shard_map/ppermute | solution.py:179
  53.5 2.4 %mul.19 = (f32[512,128]{1,0:T(8,128)S(1)}, s32[1]{0:T(128)}) custom-call(s32[1]{0:T(128)} %get-tuple-element.146.turn, f32[4,512,128]{2,1,0:T(8,128)S(1)} %pad_maximum_fusion.mine, f32[4,512,128]{2,1,0:T(8,128)S(1)} %collective-permute-done.9.other, f32[256,4096]{1,0:T(8,128)S(1)} %copy-done.1, f32[256,1920]{1,0:T(8,128)S(1)} %collective-permute-done.8.theirs.c1, ...), custom_call_target="tpu_custom_call" | custom-call | flops 400000000 | tf_op jit(solution)/shard_map/mul/pallas_call | solution.py:158
  55.9 0.2 collective-permute-start.15
  56.1 1.4 %collective-permute-start.17 = (f32[512,128]{1,0:T(8,128)S(1)}, f32[512,128]{1,0:T(8,128)S(1)}, u32[]{:S(2)}, u32[]{:S(2)}) collective-permute-start(f32[512,128]{1,0:T(8,128)S(1)} %get-tuple-element.162), channel_id=1, source_target_pairs={{0,2},{1,3},{2,0},{3,1},{4,6},{5,7},{6,4},{7,5},{8,10},{9,11},{10,... | collective-permute-start | bytes 786440 | tf_op jit(solution)/shard_map/ppermute | solution.py:179
  57.6 3.2 %collective-permute-done.13.refs_8_ = f32[512,128]{1,0:T(8,128)S(1)} collective-permute-done((f32[512,128]{1,0:T(8,128)S(1)}, f32[512,128]{1,0:T(8,128)S(1)}, u32[]{:S(2)}, u32[]{:S(2)}) %collective-permute-start.13) | collective-permute-done | bytes 262176 | tf_op jit(solution)/shard_map/ppermute | solution.py:179
  60.8 1.4 %collective-permute-start.19 = (f32[512,256]{1,0:T(8,128)S(1)}, f32[512,256]{1,0:T(8,128)S(1)}, u32[]{:S(2)}, u32[]{:S(2)}) collective-permute-start(f32[512,256]{1,0:T(8,128)S(1)} %get-tuple-element.168), channel_id=1, source_target_pairs={{0,2},{1,3},{2,0},{3,1},{4,6},{5,7},{6,4},{7,5},{8,10},{9,11},{10,... | collective-permute-start | bytes 1572872 | tf_op jit(solution)/shard_map/ppermute | solution.py:179
  62.2 2.3 %mul.20 = (f32[512,256]{1,0:T(8,128)S(1)}, s32[1]{0:T(128)}) custom-call(s32[1]{0:T(128)} %get-tuple-element.152.turn, f32[4,512,128]{2,1,0:T(8,128)S(1)} %pad_maximum_fusion.mine, f32[4,512,128]{2,1,0:T(8,128)S(1)} %collective-permute-done.9.other, f32[256,4096]{1,0:T(8,128)S(1)} %copy-done.1, f32[256,1920]{1,0:T(8,128)S(1)} %collective-permute-done.8.theirs.c1, ...), custom_call_target="tpu_custom_call" | custom-call | flops 400000000 | tf_op jit(solution)/shard_map/mul/pallas_call | solution.py:158
  64.5 2.1 %collective-permute-start.18 = (f32[512,256]{1,0:T(8,128)S(1)}, f32[512,256]{1,0:T(8,128)S(1)}, u32[]{:S(2)}, u32[]{:S(2)}) collective-permute-start(f32[512,256]{1,0:T(8,128)S(1)} %get-tuple-element.166), channel_id=1, source_target_pairs={{0,16},{1,17},{2,18},{3,19},{4,20},{5,21},{6,22},{7,23},{8,24},{9,... | collective-permute-start | bytes 1572872 | tf_op jit(solution)/shard_map/ppermute | solution.py:179
  66.5 0.1 broadcast_select_fusion
  66.6 2.6 %collective-permute-start.21 = (f32[2,512,128]{2,1,0:T(8,128)S(1)}, f32[2,512,128]{2,1,0:T(8,128)S(1)}, u32[]{:S(2)}, u32[]{:S(2)}) collective-permute-start(f32[2,512,128]{2,1,0:T(8,128)S(1)} %broadcast_select_fusion), channel_id=1, source_target_pairs={{0,4},{1,5},{2,6},{3,7},{4,0},{5,1},{6,2},{7,3},{8,12},{9,13},{10,... | collective-permute-start | bytes 1572872 | tf_op jit(solution)/shard_map/ppermute | solution.py:179
  69.2 2.4 %mul.21 = (f32[512,128]{1,0:T(8,128)S(1)}, s32[1]{0:T(128)}) custom-call(s32[1]{0:T(128)} %get-tuple-element.163.turn, f32[4,512,128]{2,1,0:T(8,128)S(1)} %pad_maximum_fusion.mine, f32[4,512,128]{2,1,0:T(8,128)S(1)} %collective-permute-done.9.other, f32[256,4096]{1,0:T(8,128)S(1)} %copy-done.1, f32[256,1920]{1,0:T(8,128)S(1)} %collective-permute-done.8.theirs.c1, ...), custom_call_target="tpu_custom_call" | custom-call | flops 400000000 | tf_op jit(solution)/shard_map/mul/pallas_call | solution.py:158
  71.6 0.1 collective-permute-start.20
  71.7 6.4 %collective-permute-done.18.refs_10_ = f32[512,256]{1,0:T(8,128)S(1)} collective-permute-done((f32[512,256]{1,0:T(8,128)S(1)}, f32[512,256]{1,0:T(8,128)S(1)}, u32[]{:S(2)}, u32[]{:S(2)}) %collective-permute-start.18) | collective-permute-done | bytes 524320 | tf_op jit(solution)/shard_map/ppermute | solution.py:179
  78.1 2.3 %mul.22 = (f32[512,256]{1,0:T(8,128)S(1)}, s32[1]{0:T(128)}) custom-call(s32[1]{0:T(128)} %get-tuple-element.169.turn, f32[4,512,128]{2,1,0:T(8,128)S(1)} %pad_maximum_fusion.mine, f32[4,512,128]{2,1,0:T(8,128)S(1)} %collective-permute-done.9.other, f32[256,4096]{1,0:T(8,128)S(1)} %copy-done.1, f32[256,1920]{1,0:T(8,128)S(1)} %collective-permute-done.8.theirs.c1, ...), custom_call_target="tpu_custom_call" | custom-call | flops 400000000 | tf_op jit(solution)/shard_map/mul/pallas_call | solution.py:158
  80.4 1.2 %collective-permute-done.20.refs_11_ = f32[512,128]{1,0:T(8,128)S(1)} collective-permute-done((f32[512,128]{1,0:T(8,128)S(1)}, f32[512,128]{1,0:T(8,128)S(1)}, u32[]{:S(2)}, u32[]{:S(2)}) %collective-permute-start.20) | collective-permute-done | bytes 262176 | tf_op jit(solution)/shard_map/ppermute | solution.py:179
  81.7 0.1 collective-permute-start.22
  81.8 1.8 %collective-permute-start.23 = (f32[512,256]{1,0:T(8,128)S(1)}, f32[512,256]{1,0:T(8,128)S(1)}, u32[]{:S(2)}, u32[]{:S(2)}) collective-permute-start(f32[512,256]{1,0:T(8,128)S(1)} %get-tuple-element.190), channel_id=1, source_target_pairs={{0,16},{1,17},{2,18},{3,19},{4,20},{5,21},{6,22},{7,23},{8,24},{9,... | collective-permute-start | bytes 1572872 | tf_op jit(solution)/shard_map/ppermute | solution.py:179
  83.6 0.8 collective-permute-done.22.other
  84.5 6.5 %mul.23 = (f32[512,1024]{1,0:T(8,128)}, s32[1]{0:T(128)}) custom-call(s32[1]{0:T(128)} %get-tuple-element.181.turn, f32[4,512,128]{2,1,0:T(8,128)S(1)} %constant_dynamic-update-slice_fusion.mine, f32[4,512,128]{2,1,0:T(8,128)S(1)} %collective-permute-done.22.other, f32[256,4096]{1,0:T(8,128)S(1)} %copy-done.1, ...), custom_call_target="tpu_custom_call" | custom-call | tf_op jit(solution)/shard_map/mul/pallas_call | solution.py:158
  90.9 5.2 %collective-permute-done.23 = f32[512,256]{1,0:T(8,128)S(1)} collective-permute-done((f32[512,256]{1,0:T(8,128)S(1)}, f32[512,256]{1,0:T(8,128)S(1)}, u32[]{:S(2)}, u32[]{:S(2)}) %collective-permute-start.23) | collective-permute-done | bytes 524320 | tf_op jit(solution)/shard_map/ppermute | solution.py:179
  96.2 1.9 %add_dynamic-update-slice_fusion = f32[512,1024]{1,0:T(8,128)} fusion(f32[512,1024]{1,0:T(8,128)} %get-tuple-element.189, f32[512,256]{1,0:T(8,128)S(1)} %collective-permute-done.23), kind=kLoop, calls=%fused_computation.2 | loop fusion | flops 262144 | bytes 1572864 | tf_op jit(solution)/shard_map/dynamic_update_slice | solution.py:255
  (22 shorter events, 0.2 us)
Async XLA Ops:
  0.0 18.3 %collective-permute-start.1 = (f32[512,128]{1,0:T(8,128)}, f32[512,128]{1,0:T(8,128)S(1)}, u32[]{:S(2)}, u32[]{:S(2)}) collective-permute-start(f32[512,128]{1,0:T(8,128)} %param.2), channel_id=1, source_target_pairs={{8,16},{9,17},{10,18},{11,19},{12,20},{13,21},{14,22},{15,23},{16,... | collective-permute-start | bytes 786440 | tf_op jit(solution)/shard_map/ppermute | solution.py:179
  0.7 17.7 %collective-permute-start = (f32[512,128]{1,0:T(8,128)}, f32[512,128]{1,0:T(8,128)S(1)}, u32[]{:S(2)}, u32[]{:S(2)}) collective-permute-start(f32[512,128]{1,0:T(8,128)} %param.2), channel_id=1, source_target_pairs={{8,24},{9,25},{10,26},{11,27},{12,28},{13,29},{14,30},{15,31},{16,... | collective-permute-start | bytes 786440 | tf_op jit(solution)/shard_map/ppermute | solution.py:179
  2.0 16.4 %collective-permute-start.4 = (f32[512,128]{1,0:T(8,128)}, f32[512,128]{1,0:T(8,128)S(1)}, u32[]{:S(2)}, u32[]{:S(2)}) collective-permute-start(f32[512,128]{1,0:T(8,128)} %param.2), channel_id=1, source_target_pairs={{0,2},{1,3},{2,0},{3,1},{4,6},{5,7},{6,4},{7,5},{24,26},{25,27},{2... | collective-permute-start | bytes 786440 | tf_op jit(solution)/shard_map/ppermute | solution.py:179
  9.9 7.1 %collective-permute-start.2 = (f32[256,128]{1,0:T(8,128)}, f32[256,128]{1,0:T(8,128)S(1)}, u32[]{:S(2)}, u32[]{:S(2)}) collective-permute-start(f32[256,128]{1,0:T(8,128)} %get-tuple-element.98), channel_id=1, source_target_pairs={{0,2},{1,3},{2,0},{3,1},{4,6},{5,7},{6,4},{7,5},{8,10},{9,11},{10,... | collective-permute-start | bytes 393224 | tf_op jit(solution)/shard_map/ppermute | solution.py:179
  10.0 8.3 %collective-permute-start.3 = (f32[256,128]{1,0:T(8,128)}, f32[256,128]{1,0:T(8,128)S(1)}, u32[]{:S(2)}, u32[]{:S(2)}) collective-permute-start(f32[256,128]{1,0:T(8,128)} %get-tuple-element.99), channel_id=1, source_target_pairs={{0,3},{1,2},{2,1},{3,0},{4,7},{5,6},{6,5},{7,4},{8,11},{9,10},{10,... | collective-permute-start | bytes 393224 | tf_op jit(solution)/shard_map/ppermute | solution.py:179
  18.3 4.3 %collective-permute-start.8 = (f32[256,1920]{1,0:T(8,128)}, f32[256,1920]{1,0:T(8,128)S(1)}, u32[]{:S(2)}, u32[]{:S(2)}) collective-permute-start(f32[256,1920]{1,0:T(8,128)} %get-tuple-element.106), channel_id=1, source_target_pairs={{0,1},{1,0},{2,3},{3,2},{4,5},{5,4},{6,7},{7,6},{8,9},{9,8},{10,11... | collective-permute-start | bytes 5898248 | tf_op jit(solution)/shard_map/ppermute | solution.py:179
  18.9 10.2 %collective-permute-start.7 = (f32[512,128]{1,0:T(8,128)S(1)}, f32[512,128]{1,0:T(8,128)S(1)}, u32[]{:S(2)}, u32[]{:S(2)}) collective-permute-start(f32[512,128]{1,0:T(8,128)S(1)} %broadcast_select_fusion.1), channel_id=1, source_target_pairs={{0,6},{1,7},{2,4},{3,5},{4,2},{5,3},{6,0},{7,1},{8,14},{9,15},{10,... | collective-permute-start | bytes 786440 | tf_op jit(solution)/shard_map/ppermute | solution.py:179
  21.7 12.3 %collective-permute-start.6 = (f32[512,128]{1,0:T(8,128)S(1)}, f32[512,128]{1,0:T(8,128)S(1)}, u32[]{:S(2)}, u32[]{:S(2)}) collective-permute-start(f32[512,128]{1,0:T(8,128)S(1)} %broadcast_select_fusion.1), channel_id=1, source_target_pairs={{0,4},{1,5},{2,6},{3,7},{4,0},{5,1},{6,2},{7,3},{8,12},{9,13},{10,... | collective-permute-start | bytes 786440 | tf_op jit(solution)/shard_map/ppermute | solution.py:179
  22.2 11.9 %collective-permute-start.5 = (f32[512,128]{1,0:T(8,128)S(1)}, f32[512,128]{1,0:T(8,128)S(1)}, u32[]{:S(2)}, u32[]{:S(2)}) collective-permute-start(f32[512,128]{1,0:T(8,128)S(1)} %broadcast_select_fusion.1), channel_id=1, source_target_pairs={{0,2},{1,3},{2,0},{3,1},{4,6},{5,7},{6,4},{7,5},{8,10},{9,11},{10,... | collective-permute-start | bytes 786440 | tf_op jit(solution)/shard_map/ppermute | solution.py:179
  22.7 2.2 %copy-start = (f32[256,4096]{1,0:T(8,128)S(1)}, f32[256,4096]{1,0:T(8,128)}, u32[]{:S(2)}) copy-start(f32[256,4096]{1,0:T(8,128)} %source.17) | copy-start | bytes 12582916
  24.9 12.9 %copy-start.1 = (f32[256,4096]{1,0:T(8,128)S(1)}, f32[256,4096]{1,0:T(8,128)}, u32[]{:S(2)}) copy-start(f32[256,4096]{1,0:T(8,128)} %source.17) | copy-start | bytes 12582916
  34.1 7.4 %copy-start.2 = (f32[512,128]{1,0:T(8,128)S(1)}, f32[512,128]{1,0:T(8,128)}, u32[]{:S(2)}) copy-start(f32[512,128]{1,0:T(8,128)} %param.2) | copy-start | bytes 786436
  34.1 3.6 %collective-permute-start.9 = (f32[4,512,128]{2,1,0:T(8,128)S(1)}, f32[4,512,128]{2,1,0:T(8,128)S(1)}, u32[]{:S(2)}, u32[]{:S(2)}) collective-permute-start(f32[4,512,128]{2,1,0:T(8,128)S(1)} %pad_maximum_fusion.mine), channel_id=1, source_target_pairs={{0,1},{1,0},{2,3},{3,2},{4,5},{5,4},{6,7},{7,6},{8,9},{9,8},{10,11... | collective-permute-start | bytes 3145736 | tf_op jit(solution)/shard_map/ppermute | solution.py:179
  34.2 19.3 %collective-permute-start.12 = (f32[512,128]{1,0:T(8,128)S(1)}, f32[512,128]{1,0:T(8,128)S(1)}, u32[]{:S(2)}, u32[]{:S(2)}) collective-permute-start(f32[512,128]{1,0:T(8,128)S(1)} %get-tuple-element.145), channel_id=1, source_target_pairs={{0,2},{1,3},{2,0},{3,1},{4,6},{5,7},{6,4},{7,5},{8,10},{9,11},{10,... | collective-permute-start | bytes 786440 | tf_op jit(solution)/shard_map/ppermute | solution.py:179
  35.7 13.3 %collective-permute-start.10 = (f32[512,128]{1,0:T(8,128)S(1)}, f32[512,128]{1,0:T(8,128)S(1)}, u32[]{:S(2)}, u32[]{:S(2)}) collective-permute-start(f32[512,128]{1,0:T(8,128)S(1)} %get-tuple-element.137), channel_id=1, source_target_pairs={{0,2},{1,3},{2,0},{3,1},{4,6},{5,7},{6,4},{7,5},{8,10},{9,11},{10,... | collective-permute-start | bytes 786440 | tf_op jit(solution)/shard_map/ppermute | solution.py:179
  36.3 25.9 %collective-permute-start.14 = (f32[512,256]{1,0:T(8,128)S(1)}, f32[512,256]{1,0:T(8,128)S(1)}, u32[]{:S(2)}, u32[]{:S(2)}) collective-permute-start(f32[512,256]{1,0:T(8,128)S(1)} %get-tuple-element.151), channel_id=1, source_target_pairs={{0,2},{1,3},{2,0},{3,1},{4,6},{5,7},{6,4},{7,5},{8,10},{9,11},{10,... | collective-permute-start | bytes 1572872 | tf_op jit(solution)/shard_map/ppermute | solution.py:179
  39.6 13.9 %collective-permute-start.11 = (f32[512,128]{1,0:T(8,128)S(1)}, f32[512,128]{1,0:T(8,128)S(1)}, u32[]{:S(2)}, u32[]{:S(2)}) collective-permute-start(f32[512,128]{1,0:T(8,128)S(1)} %get-tuple-element.143), channel_id=1, source_target_pairs={{0,16},{1,17},{2,18},{3,19},{4,20},{5,21},{6,22},{7,23},{8,24},{9,... | collective-permute-start | bytes 786440 | tf_op jit(solution)/shard_map/ppermute | solution.py:179
  41.6 25.0 %collective-permute-start.16 = (f32[2,512,128]{2,1,0:T(8,128)S(1)}, f32[2,512,128]{2,1,0:T(8,128)S(1)}, u32[]{:S(2)}, u32[]{:S(2)}) collective-permute-start(f32[2,512,128]{2,1,0:T(8,128)S(1)} %pad_maximum_fusion.1), channel_id=1, source_target_pairs={{0,8},{1,9},{2,10},{3,11},{4,12},{5,13},{6,14},{7,15},{24,16},{25,... | collective-permute-start | bytes 1572872 | tf_op jit(solution)/shard_map/ppermute | solution.py:179
  51.5 9.2 %collective-permute-start.13 = (f32[512,128]{1,0:T(8,128)S(1)}, f32[512,128]{1,0:T(8,128)S(1)}, u32[]{:S(2)}, u32[]{:S(2)}) collective-permute-start(f32[512,128]{1,0:T(8,128)S(1)} %get-tuple-element.149), channel_id=1, source_target_pairs={{0,16},{1,17},{2,18},{3,19},{4,20},{5,21},{6,22},{7,23},{8,24},{9,... | collective-permute-start | bytes 786440 | tf_op jit(solution)/shard_map/ppermute | solution.py:179
  55.9 10.6 %collective-permute-start.15 = (f32[512,128]{1,0:T(8,128)S(1)}, f32[512,128]{1,0:T(8,128)S(1)}, u32[]{:S(2)}, u32[]{:S(2)}) collective-permute-start(f32[512,128]{1,0:T(8,128)S(1)} %get-tuple-element.155), channel_id=1, source_target_pairs={{0,16},{1,17},{2,18},{3,19},{4,20},{5,21},{6,22},{7,23},{8,24},{9,... | collective-permute-start | bytes 786440 | tf_op jit(solution)/shard_map/ppermute | solution.py:179
  56.1 13.0 %collective-permute-start.17 = (f32[512,128]{1,0:T(8,128)S(1)}, f32[512,128]{1,0:T(8,128)S(1)}, u32[]{:S(2)}, u32[]{:S(2)}) collective-permute-start(f32[512,128]{1,0:T(8,128)S(1)} %get-tuple-element.162), channel_id=1, source_target_pairs={{0,2},{1,3},{2,0},{3,1},{4,6},{5,7},{6,4},{7,5},{8,10},{9,11},{10,... | collective-permute-start | bytes 786440 | tf_op jit(solution)/shard_map/ppermute | solution.py:179
  60.8 17.3 %collective-permute-start.19 = (f32[512,256]{1,0:T(8,128)S(1)}, f32[512,256]{1,0:T(8,128)S(1)}, u32[]{:S(2)}, u32[]{:S(2)}) collective-permute-start(f32[512,256]{1,0:T(8,128)S(1)} %get-tuple-element.168), channel_id=1, source_target_pairs={{0,2},{1,3},{2,0},{3,1},{4,6},{5,7},{6,4},{7,5},{8,10},{9,11},{10,... | collective-permute-start | bytes 1572872 | tf_op jit(solution)/shard_map/ppermute | solution.py:179
  64.5 13.6 %collective-permute-start.18 = (f32[512,256]{1,0:T(8,128)S(1)}, f32[512,256]{1,0:T(8,128)S(1)}, u32[]{:S(2)}, u32[]{:S(2)}) collective-permute-start(f32[512,256]{1,0:T(8,128)S(1)} %get-tuple-element.166), channel_id=1, source_target_pairs={{0,16},{1,17},{2,18},{3,19},{4,20},{5,21},{6,22},{7,23},{8,24},{9,... | collective-permute-start | bytes 1572872 | tf_op jit(solution)/shard_map/ppermute | solution.py:179
  66.6 15.0 %collective-permute-start.21 = (f32[2,512,128]{2,1,0:T(8,128)S(1)}, f32[2,512,128]{2,1,0:T(8,128)S(1)}, u32[]{:S(2)}, u32[]{:S(2)}) collective-permute-start(f32[2,512,128]{2,1,0:T(8,128)S(1)} %broadcast_select_fusion), channel_id=1, source_target_pairs={{0,4},{1,5},{2,6},{3,7},{4,0},{5,1},{6,2},{7,3},{8,12},{9,13},{10,... | collective-permute-start | bytes 1572872 | tf_op jit(solution)/shard_map/ppermute | solution.py:179
  71.6 10.0 %collective-permute-start.20 = (f32[512,128]{1,0:T(8,128)S(1)}, f32[512,128]{1,0:T(8,128)S(1)}, u32[]{:S(2)}, u32[]{:S(2)}) collective-permute-start(f32[512,128]{1,0:T(8,128)S(1)} %get-tuple-element.172), channel_id=1, source_target_pairs={{0,16},{1,17},{2,18},{3,19},{4,20},{5,21},{6,22},{7,23},{8,24},{9,... | collective-permute-start | bytes 786440 | tf_op jit(solution)/shard_map/ppermute | solution.py:179
  81.7 2.7 %collective-permute-start.22 = (f32[4,512,128]{2,1,0:T(8,128)S(1)}, f32[4,512,128]{2,1,0:T(8,128)S(1)}, u32[]{:S(2)}, u32[]{:S(2)}) collective-permute-start(f32[4,512,128]{2,1,0:T(8,128)S(1)} %constant_dynamic-update-slice_fusion.mine), channel_id=1, source_target_pairs={{0,1},{1,0},{2,3},{3,2},{4,5},{5,4},{6,7},{7,6},{8,9},{9,8},{10,11... | collective-permute-start | bytes 3145736 | tf_op jit(solution)/shard_map/ppermute | solution.py:179
  81.8 14.3 %collective-permute-start.23 = (f32[512,256]{1,0:T(8,128)S(1)}, f32[512,256]{1,0:T(8,128)S(1)}, u32[]{:S(2)}, u32[]{:S(2)}) collective-permute-start(f32[512,256]{1,0:T(8,128)S(1)} %get-tuple-element.190), channel_id=1, source_target_pairs={{0,16},{1,17},{2,18},{3,19},{4,20},{5,21},{6,22},{7,23},{8,24},{9,... | collective-permute-start | bytes 1572872 | tf_op jit(solution)/shard_map/ppermute | solution.py:179
